TPU v7x, 32 devices: a whole 2x2x4 slice. The times are simulated.
32 devices in a mesh: dp: 4 (over x, core), adapter: 8 (over z, y).
Axes of the slice: x: 2, y: 2, z: 4, core: 2. Of those that a mesh axis runs over, the one named last changes fastest.
Arguments:
- residual_input: bfloat16 [16384, 2560], P(('dp', 'adapter')), may hold values from -6 to 6
- input_norm_gain: float32 [2560], replicated, may hold values from 0.5 to 1.5
- base_projection_weight: bfloat16 [2560, 4096], P('adapter', 'dp'), may hold values from -0.125 to 0.125
- query_key_gains: float32 [2, 256], replicated, may hold values from 0.5 to 1.5
- adapter_down_weight: bfloat16 [32, 2560, 48], P('adapter'), may hold values from -0.125 to 0.125
- adapter_up_weight: bfloat16 [32, 16, 4096], P('adapter'), may hold values from -1.5 to 1.5
- row_adapter_index: int32 [16384, 1], P(('dp', 'adapter')), may hold values from 0 to 31; in each aligned block of 512 rows (0 to 511, 512 to 1023, ...) at most 32 rows name the same one
- row_sequence_index: int32 [16384], P(('dp', 'adapter')), may hold values from 0 to 1, never falling along the last dimension, each value on 1 to 12288 neighbouring positions
Outputs:
- attended: bfloat16 [16384, 2048], P(('dp', 'adapter'))
Inputs may be any that keep to these rules, and one draw needn't show every extreme that they name: `row_adapter_index`: among the rows of one device, no adapter serves more than 32 rows; some adapter serves exactly 32 rows of some device. `row_sequence_index`: sequence numbers never fall along the rows; every sequence has 1 to 12288 rows, one exactly 12288.
All inputs are finite; a program needn't handle non-finite values.
Results may differ from a plain program's by a relative error of at most 0.02.
Values may be sent and summed in bfloat16 or wider, within the bound.
No kernel may reach another device: no remote copies, remote signals or barrier semaphores. Data moves between devices by JAX's collectives and lax.ppermute only.
A program may use at most 128 MiB of HBM per device.

v0:
```python
import jax
import jax.numpy as jnp
from jax import lax
from jax.sharding import PartitionSpec as P

HEADS = 8
KV_HEADS = 4
HEAD_DIM = 256
WINDOW = 1024


def shifted(value, axis, by):
    size = lax.axis_size(axis)
    pairs = [(i, i + by) for i in range(size) if 0 <= i + by < size]
    return lax.ppermute(value, axis, pairs)


def head_norm(block, heads, gain):
    shaped = block.reshape(block.shape[0], heads, HEAD_DIM)
    scaled = shaped * lax.rsqrt(jnp.mean(shaped * shaped, axis=-1, keepdims=True) + 1e-06) * gain
    return scaled.astype(jnp.bfloat16)


def adapter_delta(rank_values, up_matrices):
    width_q = HEADS * HEAD_DIM
    width_k = KV_HEADS * HEAD_DIM
    inner = up_matrices.shape[1]
    part_q = jnp.einsum(
        "nacr,arq->nacq",
        rank_values[..., 0:inner],
        up_matrices[:, :, 0:width_q],
        preferred_element_type=jnp.float32,
    )
    part_k = jnp.einsum(
        "nacr,arq->nacq",
        rank_values[..., inner : 2 * inner],
        up_matrices[:, :, width_q : width_q + width_k],
        preferred_element_type=jnp.float32,
    )
    part_v = jnp.einsum(
        "nacr,arq->nacq",
        rank_values[..., 2 * inner : 3 * inner],
        up_matrices[:, :, width_q + width_k :],
        preferred_element_type=jnp.float32,
    )
    return jnp.concatenate([part_q, part_k, part_v], axis=-1).astype(jnp.bfloat16)


def adapter_ranks(adapter_slots, down_matrices):
    return jnp.einsum(
        "nacd,adr->nacr", adapter_slots, down_matrices, preferred_element_type=jnp.float32
    ).astype(jnp.bfloat16)


def body(
    residual_input,
    input_norm_gain,
    base_projection_weight,
    query_key_gains,
    adapter_down_weight,
    adapter_up_weight,
    row_adapter_index,
    row_sequence_index,
):
    rows = residual_input.shape[0]
    width = residual_input.shape[1]
    width_q = HEADS * HEAD_DIM
    width_k = KV_HEADS * HEAD_DIM
    group = HEADS // KV_HEADS
    values_in = residual_input.astype(jnp.float32)
    normed = (
        values_in
        * lax.rsqrt(jnp.mean(values_in * values_in, axis=-1, keepdims=True) + 1e-06)
        * input_norm_gain
    ).astype(jnp.bfloat16)
    slab = lax.all_gather(base_projection_weight, "dp", axis=1, tiled=True)
    base = jnp.dot(
        normed,
        lax.all_gather(slab, "adapter", axis=0, tiled=True),
        preferred_element_type=jnp.float32,
    ).astype(jnp.bfloat16)
    total_width = base.shape[1]
    owners = lax.axis_size("adapter")
    local_adapter_count = adapter_down_weight.shape[0]
    adapters_all = owners * local_adapter_count
    capacity = 2 * rows // adapters_all
    adapter_ids = row_adapter_index[:, 0]
    onehot = (adapter_ids[:, None] == jnp.arange(adapters_all, dtype=jnp.int32)[None, :]).astype(
        jnp.int32
    )
    earlier = jnp.cumsum(onehot, axis=0) - onehot
    place = jnp.sum(earlier * onehot, axis=1)
    slot = adapter_ids * capacity + place
    scratch_buffer = jnp.zeros((adapters_all * capacity, width), jnp.bfloat16).at[slot].set(normed)
    scratch_buffer = scratch_buffer.reshape(owners, local_adapter_count, capacity, width)
    adapter_corrections = adapter_delta(
        adapter_ranks(
            lax.all_to_all(scratch_buffer, "adapter", split_axis=0, concat_axis=0, tiled=True),
            adapter_down_weight,
        ),
        adapter_up_weight,
    )
    returned = lax.all_to_all(
        adapter_corrections, "adapter", split_axis=0, concat_axis=0, tiled=True
    )
    delta_slots = returned.reshape(adapters_all * capacity, total_width)
    delta_update = delta_slots[slot]
    projected = base.astype(jnp.float32) + delta_update.astype(jnp.float32)
    queries = head_norm(projected[:, 0:width_q], HEADS, query_key_gains[0]).reshape(
        rows, KV_HEADS, group, HEAD_DIM
    )
    keys = head_norm(
        projected[:, width_q : width_q + width_k], KV_HEADS, query_key_gains[1]
    ).reshape(rows, width_k)
    values = projected[:, width_q + width_k :].astype(jnp.bfloat16)
    before = (WINDOW + rows - 2) // rows
    key_parts = []
    value_parts = []
    seg_parts = []
    for offset in range(before, 0, -1):
        moved_keys, moved_values, moved_seg = shifted(
            (keys, values, row_sequence_index), ("dp", "adapter"), offset
        )
        key_parts.append(moved_keys)
        value_parts.append(moved_values)
        seg_parts.append(moved_seg)
    key_parts.append(keys)
    value_parts.append(values)
    seg_parts.append(row_sequence_index)
    span = (before + 1) * rows
    key_all = jnp.concatenate(key_parts, axis=0).reshape(span, KV_HEADS, HEAD_DIM)
    value_all = jnp.concatenate(value_parts, axis=0).reshape(span, KV_HEADS, HEAD_DIM)
    seg_all = jnp.concatenate(seg_parts, axis=0)
    position = lax.axis_index(("dp", "adapter"))
    query_pos = position * rows + jnp.arange(rows, dtype=jnp.int32)
    key_pos = (position - before) * rows + jnp.arange(span, dtype=jnp.int32)
    gap = query_pos[:, None] - key_pos[None, :]
    allowed = (
        (row_sequence_index[:, None] == seg_all[None, :])
        & (gap >= 0)
        & (gap < WINDOW)
        & (key_pos[None, :] >= 0)
    )
    scores = jnp.einsum(
        "tkgd,skd->kgts", queries, key_all, preferred_element_type=jnp.float32
    ) * HEAD_DIM ** (-0.5)
    weights = jnp.where(allowed[None, None], jnp.exp(scores), jnp.float32(0.0))
    total = jnp.sum(weights, axis=-1)
    probs = weights.astype(jnp.bfloat16)
    summed = jnp.einsum("kgts,skd->tkgd", probs, value_all, preferred_element_type=jnp.float32)
    result = summed / jnp.transpose(total, (2, 0, 1))[..., None]
    return result.reshape(rows, width_q).astype(jnp.bfloat16)


def solution(mesh):
    placed = (
        P(("dp", "adapter"), None),
        P(),
        P("adapter", "dp"),
        P(),
        P("adapter", None, None),
        P("adapter", None, None),
        P(("dp", "adapter"), None),
        P(("dp", "adapter")),
    )
    return jax.shard_map(
        body, mesh=mesh, in_specs=placed, out_specs=P(("dp", "adapter"), None), check_vma=False
    )
```

profile of v0, /device:TPU:6, one launch (start us, length us, event | category | flops | bytes accessed | tf_op | source)
XLA Modules:
  0.0 745.4 jit_solution(10566264076661114102)
XLA Ops:
  7.3 27.5 %all-gather.3.cloned.1.call-done = bf16[320,4096]{1,0:T(8,128)(2,1)} async-done(((bf16[320,1024]{1,0:T(8,128)(2,1)}), bf16[320,4096]{1,0:T(8,128)(2,1)}) %all-gather.3.cloned.1.call-update) | async-done | bytes 2621456 | tf_op jit(solution)/shard_map/all_gather | solution.py:76
  37.7 2.3 fusion.7
  40.1 8.8 %scatter_custom_fusion = bf16[1024,2560]{1,0:T(8,128)(2,1)} fusion(s32[512]{0:T(512)S(1)} %bitcast.119, bf16[]{:T(256)} %constant.17.clone.1, bf16[512,2560]{1,0:T(8,128)(2,1)} %param.8, f32[2560]{0:T(1024)S(1)} %copy-done.8, f32[512]{0:T(512)S(1)} %add_rsqrt_fusion.2), kind=kCustom, calls=%fused_computation.37 | custom fusion | flops 5242880 | bytes 7878658 | tf_op jit(solution)/shard_map/scatter | solution.py:94
  48.9 187.8 %all_to_all.10 = bf16[8,4,32,2560]{3,2,1,0:T(8,128)(2,1)S(1)} all-to-all(bf16[8,4,32,2560]{3,2,1,0:T(8,128)(2,1)} %bitcast.105), channel_id=1, replica_groups=mesh['dp'=4,'adapter'=8] {'adapter'}, dimensions={0} | all-to-all | bytes 10485760 | tf_op jit(solution)/shard_map/all_to_all | solution.py:98
  241.0 3.7 pad_maximum_fusion
  244.7 7.8 %copy.80 = bf16[8,4,32,4096]{3,2,1,0:T(8,128)(2,1)} copy(bf16[8,4,32,4096]{3,2,0,1:T(8,128)(2,1)} %pad_maximum_fusion) | data formatting | bytes 16777216 | tf_op jit(solution)/shard_map/concatenate | solution.py:46
  252.5 9.7 %all-to-all-start.1 = ((bf16[8,4,32,4096]{3,2,1,0:T(8,128)(2,1)}), bf16[8,4,32,4096]{3,2,1,0:T(8,128)(2,1)}, u32[]{:S(2)}, u32[]{:S(2)}) async-start(bf16[8,4,32,4096]{3,2,1,0:T(8,128)(2,1)} %copy.80), calls=%async_computation.1 | async-start | bytes 16777216 | tf_op jit(solution)/shard_map/all_to_all | solution.py:103
  262.2 3.4 collective-permute-start.3
  265.6 3.4 collective-permute-start.2
  269.1 192.2 %collective-permute-done.3 = s32[512]{0:T(512)S(1)} collective-permute-done((s32[512]{0:T(512)S(1)}, s32[512]{0:T(512)S(1)}, u32[]{:S(2)}, u32[]{:S(2)}) %collective-permute-start.3) | collective-permute-done | bytes 2080 | tf_op jit(solution)/shard_map/ppermute | solution.py:15
  461.3 2.5 fusion.22
  463.8 51.7 %all-to-all-done.1 = bf16[8,4,32,4096]{3,2,1,0:T(8,128)(2,1)} async-done(((bf16[8,4,32,4096]{3,2,1,0:T(8,128)(2,1)}), bf16[8,4,32,4096]{3,2,1,0:T(8,128)(2,1)}, u32[]{:S(2)}, u32[]{:S(2)}) %all-to-all-start.1) | async-done | bytes 8388640 | tf_op jit(solution)/shard_map/all_to_all | solution.py:103
  515.5 13.2 %gather_fusion = bf16[512,4096]{1,0:T(8,128)(2,1)} fusion(bf16[1024,4096]{1,0:T(8,128)(2,1)} %bitcast.18, s32[1024]{0:T(1024)S(1)} %pad_clamp_fusion), kind=kCustom, calls=%fused_computation | custom fusion | bytes 8390656 | tf_op jit(solution)/shard_map/gather | solution.py:107
  528.7 55.6 %all-gather.5.cloned.1.call-done = bf16[2560,4096]{1,0:T(8,128)(2,1)} async-done(((bf16[320,4096]{1,0:T(8,128)(2,1)}), bf16[2560,4096]{1,0:T(8,128)(2,1)}) %all-gather.5.cloned.1.call-update) | async-done | bytes 20971536 | tf_op jit(solution)/shard_map/all_gather | solution.py:79
  584.3 16.6 %convert_add_fusion = f32[512,4096]{1,0:T(8,128)S(1)} fusion(bf16[512,4096]{1,0:T(8,128)(2,1)} %gather_fusion, bf16[2560,4096]{1,0:T(8,128)(2,1)} %all-gather.5.cloned.1.call-done, bf16[512,2560]{1,0:T(8,128)(2,1)} %param.8, f32[2560]{0:T(1024)S(1)} %copy-done.8, f32[512]{0:T(512)S(1)} %add_rsqrt_fusion.2), kind=kOutput, calls=%fused_computation.10 | convolution fusion | flops 10751049728 | bytes 36188160 | tf_op jit(solution)/shard_map/dot_general | solution.py:77
  602.2 15.7 %collective-permute-start.1 = (bf16[512,1024]{1,0:T(8,128)(2,1)}, bf16[512,1024]{1,0:T(8,128)(2,1)}, u32[]{:S(2)}, u32[]{:S(2)}) collective-permute-start(bf16[512,1024]{1,0:T(8,128)(2,1)} %slice.85), channel_id=1, source_target_pairs={{0,1},{1,2},{2,3},{3,4},{4,5},{5,6},{6,7},{7,8},{8,9},{9,10},{10,1... | collective-permute-start | bytes 3145736 | tf_op jit(solution)/shard_map/ppermute | solution.py:15
  621.4 2.2 mul.115
  625.3 2.3 multiply_convert_fusion
  629.7 5.4 collective-permute-start.4
  635.2 4.3 slice_multiply_fusion.1
  639.5 6.6 reshape.168
  646.0 6.1 copy.108
  652.1 2.8 reduce_sum.51
  656.1 9.2 %collective-permute-done = bf16[512,1024]{1,0:T(8,128)(2,1)} collective-permute-done((bf16[512,1024]{1,0:T(8,128)(2,1)}, bf16[512,1024]{1,0:T(8,128)(2,1)}, u32[]{:S(2)}, u32[]{:S(2)}) %collective-permute-start) | collective-permute-done | bytes 1048608 | tf_op jit(solution)/shard_map/ppermute | solution.py:15
  665.3 3.2 pad_maximum_fusion.1
  668.6 4.8 copy.101
  673.3 13.3 %collective-permute-done.5 = bf16[512,1024]{1,0:T(8,128)(2,1)} collective-permute-done((bf16[512,1024]{1,0:T(8,128)(2,1)S(1)}, bf16[512,1024]{1,0:T(8,128)(2,1)}, u32[]{:S(2)}, u32[]{:S(2)}) %collective-permute-start.5) | collective-permute-done | bytes 1048608 | tf_op jit(solution)/shard_map/ppermute | solution.py:15
  686.6 2.3 copy.129
  688.9 21.4 %collective-permute-done.4 = bf16[512,1024]{1,0:T(8,128)(2,1)} collective-permute-done((bf16[512,1024]{1,0:T(8,128)(2,1)S(1)}, bf16[512,1024]{1,0:T(8,128)(2,1)}, u32[]{:S(2)}, u32[]{:S(2)}) %collective-permute-start.4) | collective-permute-done | bytes 1048608 | tf_op jit(solution)/shard_map/ppermute | solution.py:15
  711.6 13.2 %fusion = (f32[4,2,512]{2,1,0:T(2,128)S(1)}, f32[4,1536,512,2]{2,1,3,0:T(8,128)}) fusion(pred[512,1536]{0,1:T(8,128)(4,1)S(1)} %copy-done.5, f32[512,4,2,256]{3,2,1,0:T(2,128)S(1)} %copy-done.4, f32[256]{0:T(256)S(1)} %bitcast.123, f32[512,4,2]{0,2,1:T(2,128)S(1)} %rsqrt.30, bf16[512,4,256]{2,0,1:T(8,128)(2,1)} %bitcast.113, ...), kind=kOutput, calls=%fused_computation.3 | convolution fusion | flops 3252678656 | bytes 33326080 | tf_op jit(solution)/shard_map/tkgd,skd->kgts/dot_general | solution.py:144
  724.8 11.4 %fusion.12 = bf16[512,4,2,256]{0,3,2,1:T(8,128)(2,1)S(1)} fusion(bf16[1536,4,256,1]{0,2,3,1:T(8,128)(2,1)} %bitcast.111, f32[4,1536,512,2]{2,1,3,0:T(8,128)} %get-tuple-element.10, pred[512,1536]{0,1:T(8,128)(4,1)} %fusion.22, f32[512,4,2]{0,2,1:T(2,128)S(1)} %bitcast.124), kind=kOutput, calls=%fused_computation.22 | convolution fusion | flops 3242196992 | bytes 31211520 | tf_op jit(solution)/shard_map/kgts,skd->tkgd/dot_general | solution.py:150
  736.2 2.4 copy.90
  (61 shorter events, 18.9 us)
Async XLA Ops:
  6.5 230.2 %copy-start = (bf16[4,2560,48]{1,2,0:T(8,128)(2,1)S(1)}, bf16[4,2560,48]{1,2,0:T(8,128)(2,1)}, u32[]{:S(2)}) copy-start(bf16[4,2560,48]{1,2,0:T(8,128)(2,1)} %param.12) | copy-start | bytes 2949124
  6.5 33.5 %copy-start.7 = (s32[512,1]{0,1:T(1,128)S(1)}, s32[512,1]{0,1:T(1,128)}, u32[]{:S(2)}) copy-start(s32[512,1]{0,1:T(1,128)} %param.14) | copy-start | bytes 6148
  6.5 33.5 %copy-start.8 = (f32[2560]{0:T(1024)S(1)}, f32[2560]{0:T(1024)}, u32[]{:S(2)}) copy-start(f32[2560]{0:T(1024)} %param.9) | copy-start | bytes 30724
  6.5 28.2 %all-gather.3.cloned.1.call-start = ((), (), s32[]{:S(2)}) async-start(), calls=%async_computation.2 | async-start | bytes 3276800 | tf_op jit(solution)/shard_map/all_gather | solution.py:76
  7.3 577.0 %all-gather.5.cloned.1.call-start = ((), (), s32[]{:S(2)}) async-start(), calls=%async_computation.3 | async-start | bytes 23592960 | tf_op jit(solution)/shard_map/all_gather | solution.py:79
  236.8 1.5 copy-start.6
  252.5 9.7 %copy-start.9 = (s32[512]{0:T(512)S(1)}, s32[512]{0:T(512)}, u32[]{:S(2)}) copy-start(s32[512]{0:T(512)} %param.15) | copy-start | bytes 6148
  252.5 16.5 %copy-start.10 = (f32[2,256]{1,0:T(2,128)S(1)}, f32[2,256]{1,0:T(2,128)}, u32[]{:S(2)}) copy-start(f32[2,256]{1,0:T(2,128)} %param.11) | copy-start | bytes 6148
  252.5 263.0 %all-to-all-start.1 = ((bf16[8,4,32,4096]{3,2,1,0:T(8,128)(2,1)}), bf16[8,4,32,4096]{3,2,1,0:T(8,128)(2,1)}, u32[]{:S(2)}, u32[]{:S(2)}) async-start(bf16[8,4,32,4096]{3,2,1,0:T(8,128)(2,1)} %copy.80), calls=%async_computation.1 | async-start | bytes 16777216 | tf_op jit(solution)/shard_map/all_to_all | solution.py:103
  262.2 199.0 %collective-permute-start.3 = (s32[512]{0:T(512)S(1)}, s32[512]{0:T(512)S(1)}, u32[]{:S(2)}, u32[]{:S(2)}) collective-permute-start(s32[512]{0:T(512)S(1)} %copy-done.9), channel_id=1, source_target_pairs={{0,1},{1,2},{2,3},{3,4},{4,5},{5,6},{6,7},{7,8},{8,9},{9,10},{10,1... | collective-permute-start | bytes 6152 | tf_op jit(solution)/shard_map/ppermute | solution.py:15
  265.6 195.7 %collective-permute-start.2 = (s32[512]{0:T(512)S(1)}, s32[512]{0:T(512)S(1)}, u32[]{:S(2)}, u32[]{:S(2)}) collective-permute-start(s32[512]{0:T(512)S(1)} %copy-done.9), channel_id=1, source_target_pairs={{0,2},{1,3},{2,4},{3,5},{4,6},{5,7},{6,8},{7,9},{8,10},{9,11},{10,... | collective-permute-start | bytes 6152 | tf_op jit(solution)/shard_map/ppermute | solution.py:15
  600.9 19.0 %copy-start.2 = (f32[512,4096]{1,0:T(8,128)}, f32[512,4096]{1,0:T(8,128)S(1)}, u32[]{:S(2)}) copy-start(f32[512,4096]{1,0:T(8,128)S(1)} %convert_add_fusion) | copy-start | bytes 25165828
  602.2 53.9 %collective-permute-start.1 = (bf16[512,1024]{1,0:T(8,128)(2,1)}, bf16[512,1024]{1,0:T(8,128)(2,1)}, u32[]{:S(2)}, u32[]{:S(2)}) collective-permute-start(bf16[512,1024]{1,0:T(8,128)(2,1)} %slice.85), channel_id=1, source_target_pairs={{0,1},{1,2},{2,3},{3,4},{4,5},{5,6},{6,7},{7,8},{8,9},{9,10},{10,1... | collective-permute-start | bytes 3145736 | tf_op jit(solution)/shard_map/ppermute | solution.py:15
  617.9 47.4 %collective-permute-start = (bf16[512,1024]{1,0:T(8,128)(2,1)}, bf16[512,1024]{1,0:T(8,128)(2,1)}, u32[]{:S(2)}, u32[]{:S(2)}) collective-permute-start(bf16[512,1024]{1,0:T(8,128)(2,1)} %slice.85), channel_id=1, source_target_pairs={{0,2},{1,3},{2,4},{3,5},{4,6},{5,7},{6,8},{7,9},{8,10},{9,11},{10,... | collective-permute-start | bytes 3145736 | tf_op jit(solution)/shard_map/ppermute | solution.py:15
  624.9 10.3 %copy-start.3 = (f32[512,4096]{1,0:T(8,128)S(1)}, f32[512,4096]{1,0:T(8,128)}, u32[]{:S(2)}) copy-start(f32[512,4096]{1,0:T(8,128)} %copy-done.2) | copy-start | bytes 25165828
  627.6 59.0 %collective-permute-start.5 = (bf16[512,1024]{1,0:T(8,128)(2,1)S(1)}, bf16[512,1024]{1,0:T(8,128)(2,1)}, u32[]{:S(2)}, u32[]{:S(2)}) collective-permute-start(bf16[512,1024]{1,0:T(8,128)(2,1)S(1)} %multiply_convert_fusion), channel_id=1, source_target_pairs={{0,1},{1,2},{2,3},{3,4},{4,5},{5,6},{6,7},{7,8},{8,9},{9,10},{10,1... | collective-permute-start | bytes 3145736 | tf_op jit(solution)/shard_map/ppermute | solution.py:15
  629.7 80.6 %collective-permute-start.4 = (bf16[512,1024]{1,0:T(8,128)(2,1)S(1)}, bf16[512,1024]{1,0:T(8,128)(2,1)}, u32[]{:S(2)}, u32[]{:S(2)}) collective-permute-start(bf16[512,1024]{1,0:T(8,128)(2,1)S(1)} %multiply_convert_fusion), channel_id=1, source_target_pairs={{0,2},{1,3},{2,4},{3,5},{4,6},{5,7},{6,8},{7,9},{8,10},{9,11},{10,... | collective-permute-start | bytes 3145736 | tf_op jit(solution)/shard_map/ppermute | solution.py:15
  668.6 43.0 %copy-start.5 = (pred[512,1536]{0,1:T(8,128)(4,1)S(1)}, pred[512,1536]{0,1:T(8,128)(4,1)}, u32[]{:S(2)}) copy-start(pred[512,1536]{0,1:T(8,128)(4,1)} %fusion.22) | copy-start | bytes 2359300
  673.3 38.3 %copy-start.4 = (f32[512,4,2,256]{3,2,1,0:T(2,128)S(1)}, f32[512,4,2,256]{3,2,1,0:T(2,128)}, u32[]{:S(2)}) copy-start(f32[512,4,2,256]{3,2,1,0:T(2,128)} %reshape.168) | copy-start | bytes 12582916
  724.8 13.8 %copy-start.1 = (bf16[4,2560,48]{1,2,0:T(8,128)(2,1)S(1)}, bf16[4,2560,48]{1,2,0:T(8,128)(2,1)}, u32[]{:S(2)}) copy-start(bf16[4,2560,48]{1,2,0:T(8,128)(2,1)} %param.12) | copy-start | bytes 2949124
Sparse Core Ops, SparseCore 0:
  8.9 25.8 all-gather.2
  36.3 547.9 all-gather.4
where the time goes:
time: 747 us; the launch traced here: 745 us
  waiting for transfers between devices  372 us (50%)
  blocking collectives  188 us (25%)
  local copies, waits for them, and re-layouts  50.4 us (7%)
  matrix products  45.4 us (6%)
  starting transfers between devices  41.6 us (6%)
  other arithmetic  34.9 us (5%)
  between operations  13.7 us (2%)
    ppermute x6, waiting for transfers between devices, shifted(): return lax.ppermute(value, axis, pairs)  236 us
    all_to_all x1, blocking collectives, body(): lax.all_to_all(scratch_buffer, 'adapter', split_axis=0, concat_axis=0, ti...  188 us
    all_gather x1, waiting for transfers between devices, body(): lax.all_gather(slab, 'adapter', axis=0, tiled=True)  55.6 us
    all_to_all x1, waiting for transfers between devices, body(): lax.all_to_all(adapter_corrections, 'adapter', split_axis=0, concat_axis=...  51.7 us
    ppermute x6, starting transfers between devices, shifted(): return lax.ppermute(value, axis, pairs)  31.9 us
    all_gather x1, waiting for transfers between devices, body(): slab = lax.all_gather(base_projection_weight, 'dp', axis=1, tiled=True)  27.5 us
    dot_general x1, matrix products, body(): jnp.dot(normed, lax.all_gather(slab, 'adapter', axis=0, tiled=True), pref...  16.6 us
  transfers between devices with their start and end apart: 9, of which 7 were waited for; matrix products, arithmetic and copies ran while one was open for 11% of the time, Pallas kernels for 0%

commit v1 on v0

--- a/solution.py
+++ b/solution.py
@@ -1,6 +1,11 @@
+import functools
+import math
+
 import jax
 import jax.numpy as jnp
 from jax import lax
+from jax.experimental import pallas as pl
+from jax.experimental.pallas import tpu as pltpu
 from jax.sharding import PartitionSpec as P
 
 HEADS = 8
@@ -52,7 +57,7 @@
     ).astype(jnp.bfloat16)
 
 
-def body(
+def general_body(
     residual_input,
     input_norm_gain,
     base_projection_weight,
@@ -152,6 +157,483 @@
     return result.reshape(rows, width_q).astype(jnp.bfloat16)
 
 
+BF16 = jnp.bfloat16
+F32 = jnp.float32
+ANY = pl.BlockSpec(memory_space=pl.ANY)
+SMEM = pl.BlockSpec(memory_space=pltpu.SMEM)
+VMEM = pl.BlockSpec(memory_space=pltpu.VMEM)
+Q_ROW, KV_KIND, KV_ROW, UP_EVEN, UP_ODD, DOWN_ID = range(6)
+
+
+def params(mib):
+    return pltpu.CompilerParams(vmem_limit_bytes=mib << 20)
+
+
+def route(value, depth, rule):
+    pairs = []
+    for x in range(2):
+        for core in range(2):
+            for z in range(depth):
+                for y in range(2):
+                    to = rule(x, core, z, y)
+                    if to is not None:
+                        source = (2 * x + core) * 2 * depth + 2 * z + y
+                        pairs.append((source, (2 * to[0] + to[1]) * 2 * depth + 2 * to[2] + to[3]))
+    return lax.ppermute(value, ("dp", "adapter"), pairs)
+
+
+def row_norm(values, gain):
+    values = values.astype(F32)
+    scale = lax.rsqrt(jnp.mean(values * values, axis=-1, keepdims=True) + 1e-06)
+    return (values * scale * gain).astype(BF16)
+
+
+def copies_done(copies):
+    for copy in copies:
+        copy.start()
+    for copy in copies:
+        copy.wait()
+
+
+def rank_kernel(count, *refs):
+    scalars, ids, normed = refs[:3]
+    pieces = refs[3 : 3 + count]
+    out, down, sems = refs[3 + count :]
+    deep = pieces[0].shape[0]
+    copies_done(
+        [
+            pltpu.make_async_copy(pieces[i], down.at[pl.ds(i * deep, deep)], sems.at[i])
+            for i in range(count)
+        ]
+    )
+    every = lax.dot_general(
+        down[...], normed[...], (((1,), (1,)), ((), ())), preferred_element_type=F32
+    )
+    total = jnp.zeros(out.shape, F32)
+    for i in range(count):
+        mine = ids[...] == scalars[DOWN_ID, i]
+        total = total + jnp.where(mine, every[i * deep : (i + 1) * deep], 0.0)
+    out[...] = total.astype(BF16)
+
+
+def adapter_ranks_of(scalars, ids, normed, pieces):
+    rows, width = normed.shape
+    count, deep = len(pieces), pieces[0].shape[0]
+    return pl.pallas_call(
+        functools.partial(rank_kernel, count),
+        out_shape=jax.ShapeDtypeStruct((deep, rows), BF16),
+        in_specs=[SMEM, VMEM, VMEM] + [ANY] * count,
+        out_specs=VMEM,
+        scratch_shapes=[
+            pltpu.VMEM((count * deep, width), BF16),
+            pltpu.SemaphoreType.DMA((count,)),
+        ],
+        compiler_params=params(24),
+        cost_estimate=pl.CostEstimate(
+            flops=2 * rows * width * count * deep,
+            bytes_accessed=2 * (rows + count * deep) * width,
+            transcendentals=0,
+        ),
+    )(scalars, ids, normed, *pieces)
+
+
+def spread(ranks, ids, scalars, count, into):
+    inner = ranks.shape[0]
+    for i in range(count):
+        for odd in range(2):
+            mine = ids[...] == scalars[UP_EVEN + odd, i]
+            at = (2 * i + odd) * inner
+            into[at : at + inner, :] = jnp.where(mine, ranks, jnp.zeros_like(ranks))
+
+
+def project(normed, weight, into, up):
+    base = jnp.dot(normed, weight, preferred_element_type=F32).astype(BF16)
+    delta = lax.dot_general(
+        into, up, (((0,), (0,)), ((), ())), preferred_element_type=F32
+    ).astype(BF16)
+    return base.astype(F32) + delta.astype(F32)
+
+
+def unit(block, gain):
+    scale = lax.rsqrt(jnp.mean(block * block, axis=-1, keepdims=True) + 1e-06)
+    return (block * scale * gain).astype(BF16)
+
+
+def kv_kernel(count, inner, *refs):
+    scalars, ids, gains, normed, ranks_a, ranks_b = refs[:6]
+    pieces = refs[6 : 6 + count]
+    out, weight, up, into_k, into_v, sems = refs[6 + count :]
+    deep = pieces[0].shape[0] - 4 * inner
+    copies = []
+    for i in range(count):
+        kind = scalars[KV_KIND, i]
+        row = pl.multiple_of(scalars[KV_ROW, i], deep)
+        copies.append(
+            pltpu.make_async_copy(
+                pieces[i].at[pl.ds(0, deep)], weight.at[kind, pl.ds(row, deep)], sems.at[3 * i]
+            )
+        )
+        for both in range(2):
+            copies.append(
+                pltpu.make_async_copy(
+                    pieces[i].at[pl.ds(deep + 2 * inner * both, 2 * inner)],
+                    up.at[both, pl.ds(2 * inner * i, 2 * inner)],
+                    sems.at[3 * i + 1 + both],
+                )
+            )
+    for copy in copies:
+        copy.start()
+    ranks = ranks_a[...] + ranks_b[...]
+    spread(ranks[inner : 2 * inner], ids, scalars, count, into_k)
+    spread(ranks[2 * inner : 3 * inner], ids, scalars, count, into_v)
+    for copy in copies:
+        copy.wait()
+    for head in range(weight.shape[2] // HEAD_DIM):
+        cut = slice(head * HEAD_DIM, (head + 1) * HEAD_DIM)
+        keys = project(normed[...], weight[0, :, cut], into_k[...], up[0, :, cut])
+        out[head, :, 0:HEAD_DIM] = unit(keys, gains[1:2, :])
+        values = project(normed[...], weight[1, :, cut], into_v[...], up[1, :, cut])
+        out[head, :, HEAD_DIM:] = values.astype(BF16)
+
+
+def keys_values(scalars, ids, gains, normed, ranks_a, ranks_b, pieces):
+    rows, width = normed.shape
+    count, inner = len(pieces), ranks_a.shape[0] // 3
+    columns = pieces[0].shape[1]
+    heads = columns // HEAD_DIM
+    return pl.pallas_call(
+        functools.partial(kv_kernel, count, inner),
+        out_shape=jax.ShapeDtypeStruct((heads, rows, 2 * HEAD_DIM), BF16),
+        in_specs=[SMEM, VMEM, VMEM, VMEM, VMEM, VMEM] + [ANY] * count,
+        out_specs=VMEM,
+        scratch_shapes=[
+            pltpu.VMEM((2, width, columns), BF16),
+            pltpu.VMEM((2, 2 * inner * count, columns), BF16),
+            pltpu.VMEM((2 * inner * count, rows), BF16),
+            pltpu.VMEM((2 * inner * count, rows), BF16),
+            pltpu.SemaphoreType.DMA((3 * count,)),
+        ],
+        compiler_params=params(32),
+        cost_estimate=pl.CostEstimate(
+            flops=4 * rows * width * columns,
+            bytes_accessed=2 * (rows + 2 * columns) * width,
+            transcendentals=0,
+        ),
+    )(scalars, ids, gains, normed, ranks_a, ranks_b, *pieces)
+
+
+def query_kernel(count, inner, *refs):
+    scalars, ids_own, ids_nb, gains, normed_own, normed_nb = refs[:6]
+    ranks = refs[6:10]
+    pieces = refs[10 : 10 + count]
+    out_own, out_nb, weight, up, into_own, into_nb, sems = refs[10 + count :]
+    deep = pieces[0].shape[0] - 2 * inner
+    copies = []
+    for i in range(count):
+        row = pl.multiple_of(scalars[Q_ROW, i], deep)
+        copies.append(
+            pltpu.make_async_copy(
+                pieces[i].at[pl.ds(0, deep)], weight.at[pl.ds(row, deep)], sems.at[2 * i]
+            )
+        )
+        copies.append(
+            pltpu.make_async_copy(
+                pieces[i].at[pl.ds(deep, 2 * inner)],
+                up.at[pl.ds(2 * inner * i, 2 * inner)],
+                sems.at[2 * i + 1],
+            )
+        )
+    for copy in copies:
+        copy.start()
+    spread(ranks[0][0:inner] + ranks[1][0:inner], ids_own, scalars, count, into_own)
+    spread(ranks[2][0:inner] + ranks[3][0:inner], ids_nb, scalars, count, into_nb)
+    for copy in copies:
+        copy.wait()
+    for head in range(weight.shape[1] // HEAD_DIM):
+        cut = slice(head * HEAD_DIM, (head + 1) * HEAD_DIM)
+        for normed, into, out in ((normed_nb, into_nb, out_nb), (normed_own, into_own, out_own)):
+            block = project(normed[...], weight[:, cut], into[...], up[:, cut])
+            out[:, cut] = unit(block, gains[0:1, :])
+
+
+def queries_of(scalars, ids_own, ids_nb, gains, normed_own, normed_nb, ranks, pieces):
+    rows, width = normed_own.shape
+    count, inner = len(pieces), ranks[0].shape[0] // 3
+    columns = pieces[0].shape[1]
+    return pl.pallas_call(
+        functools.partial(query_kernel, count, inner),
+        out_shape=[jax.ShapeDtypeStruct((rows, columns), BF16)] * 2,
+        in_specs=[SMEM] + [VMEM] * 9 + [ANY] * count,
+        out_specs=[VMEM, VMEM],
+        scratch_shapes=[
+            pltpu.VMEM((width, columns), BF16),
+            pltpu.VMEM((2 * inner * count, columns), BF16),
+            pltpu.VMEM((2 * inner * count, rows), BF16),
+            pltpu.VMEM((2 * inner * count, rows), BF16),
+            pltpu.SemaphoreType.DMA((2 * count,)),
+        ],
+        compiler_params=params(40),
+        cost_estimate=pl.CostEstimate(
+            flops=4 * rows * width * columns,
+            bytes_accessed=2 * (2 * rows + columns) * width,
+            transcendentals=0,
+        ),
+    )(scalars, ids_own, ids_nb, gains, normed_own, normed_nb, *ranks, *pieces)
+
+
+def attend_kernel(places, queries, seg_rows, seg_keys, *refs):
+    blocks, out, held, sems = refs[:4], refs[4], refs[5], refs[6]
+    rows = queries.shape[0]
+    slots = held.shape[0]
+    for wait in (False, True):
+        for i in range(4):
+            slot = places[i]
+
+            @pl.when((slot >= 0) & (slot < slots))
+            def _():
+                copy = pltpu.make_async_copy(blocks[i], held.at[slot], sems.at[i])
+                if wait:
+                    copy.wait()
+                else:
+                    copy.start()
+
+    tile = HEAD_DIM
+    heads = queries.shape[1] // HEAD_DIM
+    tiles = WINDOW // tile + 1
+    per_block = rows // tile
+    row = lax.broadcasted_iota(jnp.int32, (tile, tile), 0)
+    column = lax.broadcasted_iota(jnp.int32, (tile, tile), 1)
+    for part in range(rows // tile):
+        here = slice(part * tile, (part + 1) * tile)
+        query = jnp.concatenate(
+            [queries[here, h * HEAD_DIM : (h + 1) * HEAD_DIM] for h in range(heads)], axis=0
+        )
+        total = jnp.zeros((heads * tile, 128), F32)
+        summed = jnp.zeros((heads * tile, HEAD_DIM), F32)
+        for step in range(tiles):
+            at = part + step
+            block, inside = at // per_block, at % per_block
+            span = slice(inside * tile, (inside + 1) * tile)
+            keys = held[block, span, 0:HEAD_DIM]
+            values = held[block, span, HEAD_DIM:]
+            allowed = seg_rows[here, :] == seg_keys[:, at * tile : (at + 1) * tile]
+            if step == 0:
+                allowed = allowed & (column > row)
+            if step == tiles - 1:
+                allowed = allowed & (column <= row)
+            scores = lax.dot_general(
+                query, keys, (((1,), (1,)), ((), ())), preferred_element_type=F32
+            )
+            weights = jnp.exp2(scores * (HEAD_DIM ** (-0.5) * math.log2(math.e)))
+            weights = jnp.where(jnp.concatenate([allowed] * heads, axis=0), weights, 0.0)
+            for cut in range(tile // 128):
+                total = total + weights[:, cut * 128 : (cut + 1) * 128]
+            summed = summed + jnp.dot(
+                weights.astype(BF16), values, preferred_element_type=F32
+            )
+        result = summed / jnp.sum(total, axis=-1, keepdims=True)
+        for h in range(heads):
+            out[here, h * HEAD_DIM : (h + 1) * HEAD_DIM] = result[
+                h * tile : (h + 1) * tile
+            ].astype(BF16)
+
+
+def attend(head, places, queries, seg_rows, seg_keys, blocks):
+    rows = queries.shape[0]
+    width = queries.shape[1] // 2
+    slots = seg_keys.shape[1] // rows
+    return pl.pallas_call(
+        attend_kernel,
+        grid=(1,),
+        out_shape=jax.ShapeDtypeStruct((rows, width), BF16),
+        in_specs=[
+            SMEM,
+            pl.BlockSpec((rows, width), lambda i: (0, head)),
+            pl.BlockSpec((rows, 1), lambda i: (0, 0)),
+            pl.BlockSpec((1, slots * rows), lambda i: (0, 0)),
+        ]
+        + [ANY] * 4,
+        out_specs=pl.BlockSpec((rows, width), lambda i: (0, 0)),
+        scratch_shapes=[
+            pltpu.VMEM((slots, rows, 2 * HEAD_DIM), BF16),
+            pltpu.SemaphoreType.DMA((4,)),
+        ],
+        compiler_params=params(24),
+        cost_estimate=pl.CostEstimate(
+            flops=4 * rows * width * (WINDOW + HEAD_DIM),
+            bytes_accessed=2 * rows * HEAD_DIM * 12,
+            transcendentals=2 * rows * (WINDOW + HEAD_DIM),
+        ),
+    )(places, queries, seg_rows, seg_keys, *blocks)
+
+
+def paired_body(
+    residual_input,
+    input_norm_gain,
+    base_projection_weight,
+    query_key_gains,
+    adapter_down_weight,
+    adapter_up_weight,
+    row_adapter_index,
+    row_sequence_index,
+):
+    rows = residual_input.shape[0]
+    width_q, width_k = HEADS * HEAD_DIM, KV_HEADS * HEAD_DIM
+    half_q, half_k = width_q // 2, width_k // 2
+    depth = lax.axis_size("adapter") // 2
+    local = adapter_down_weight.shape[0]
+    deep = base_projection_weight.shape[0]
+    place = lax.axis_index("dp")
+    x, core = place // 2, place % 2
+    owner = lax.axis_index("adapter")
+    z, y = owner // 2, owner % 2
+    swap_y = lambda v: route(v, depth, lambda x, c, z, y: (x, c, z, 1 - y))
+    swap_x = lambda v: route(v, depth, lambda x, c, z, y: (1 - x, c, z, y))
+    swap_core = lambda v: route(v, depth, lambda x, c, z, y: (x, 1 - c, z, y))
+    ring = lambda v: route(v, depth, lambda x, c, z, y: (x, c, (z + 1) % depth, y))
+
+    def onward(x, c, z, y):
+        if z + 1 < depth:
+            return (x, c, z + 1, y)
+        after = 2 * x + c + 1
+        return (after // 2, after % 2, 0, y) if after < 4 else None
+
+    halo = lambda v: route(v, depth, onward)
+
+    block = base_projection_weight
+    top, bottom = block[: deep // 2], block[deep // 2 :]
+    mine = lax.dynamic_slice_in_dim(block, y * half_k, half_k, 1)
+    theirs = lax.dynamic_slice_in_dim(block, (1 - y) * half_k, half_k, 1)
+    got_top = route(top, depth, lambda x, c, z, y: (0, y, z, c) if x == 0 and c != y else None)
+    got_bottom = route(bottom, depth, lambda x, c, z, y: (1, y, z, c) if x == 0 else None)
+    got_theirs = route(
+        theirs,
+        depth,
+        lambda x, c, z, y: None if x == 0 else (1, c, z, 1) if y == 0 else (0, c, z, 0),
+    )
+    got_mine = route(mine, depth, lambda x, c, z, y: (0, c, z, 1) if x == 1 and y == 1 else None)
+    share_q = jnp.where(x == 1, got_bottom, jnp.where(core == y, top, got_top))
+    share_kv = jnp.where(
+        x == 0, jnp.where(y == 0, got_theirs, got_mine), jnp.where(y == 0, mine, got_theirs)
+    )
+    up_one = lax.dynamic_index_in_dim(adapter_up_weight, place, 0, keepdims=False)
+
+    def up_half(which):
+        return (
+            lax.dynamic_slice_in_dim(up_one, which * half_q, half_q, 1),
+            lax.dynamic_slice_in_dim(up_one, width_q + which * half_k, half_k, 1),
+            lax.dynamic_slice_in_dim(up_one, width_q + width_k + which * half_k, half_k, 1),
+        )
+
+    up_own = jnp.concatenate(up_half(y), axis=1)
+    up_other = swap_y(jnp.concatenate(up_half(1 - y), axis=1))
+    up_pair = jnp.concatenate(
+        [jnp.where(y == 0, up_own, up_other), jnp.where(y == 0, up_other, up_own)], axis=0
+    )
+    share_q = jnp.concatenate([share_q, up_pair[:, :half_q]], axis=0)
+    share_kv = jnp.concatenate(
+        [share_kv, up_pair[:, half_q : half_q + half_k], up_pair[:, half_q + half_k :]], axis=0
+    )
+    share_down = lax.dynamic_index_in_dim(adapter_down_weight, place, 0, keepdims=False).T
+
+    other_input = swap_y(residual_input)
+    numbers = jnp.stack([row_adapter_index[:, 0], row_sequence_index])
+    other_numbers = swap_y(numbers)
+    ids_own, ids_nb = numbers[0:1], other_numbers[0:1]
+    seg_pair = jnp.where(
+        y == 0,
+        jnp.concatenate([numbers[1], other_numbers[1]]),
+        jnp.concatenate([other_numbers[1], numbers[1]]),
+    )
+    seg_before = jnp.where((place == 0) & (z == 0), -1, halo(seg_pair))
+    seg_span = jnp.concatenate([seg_before, seg_pair])
+    normed_own = row_norm(residual_input, input_norm_gain)
+    normed_nb = row_norm(other_input, input_norm_gain)
+
+    def gathered(share):
+        pieces = []
+        for step in range(depth):
+            if step:
+                share = ring(share)
+            across = swap_x(share)
+            pieces += [share, across, swap_core(share), swap_core(across)]
+        return pieces
+
+    down_pieces = gathered(share_down)
+    kv_pieces = gathered(share_kv)
+    q_pieces = gathered(share_q)
+    table = []
+    for step in range(depth):
+        chunk = (z + depth - step) % depth
+        for flip_x, flip_core in ((0, 0), (1, 0), (0, 1), (1, 1)):
+            at_x = x + flip_x * (1 - 2 * x)
+            at_core = core + flip_core * (1 - 2 * core)
+            adapter = 2 * chunk * local + 2 * at_x + at_core
+            table.append(
+                jnp.stack(
+                    [
+                        (2 * chunk + at_core) * deep + at_x * (deep // 2),
+                        at_core,
+                        (2 * chunk + 1 - at_x) * deep,
+                        adapter,
+                        adapter + local,
+                        adapter + y * local,
+                    ]
+                )
+            )
+    scalars = jnp.stack(table, axis=1).astype(jnp.int32)
+
+    part_own = adapter_ranks_of(scalars, ids_own, normed_own, down_pieces)
+    part_nb = adapter_ranks_of(scalars, ids_nb, normed_nb, down_pieces)
+    back_nb = swap_y(part_own)
+    back_own = swap_y(part_nb)
+    gains = query_key_gains
+    kv_own = keys_values(scalars, ids_own, gains, normed_own, part_own, back_own, kv_pieces)
+    kv_nb = keys_values(scalars, ids_nb, gains, normed_nb, part_nb, back_nb, kv_pieces)
+    queries_own, queries_nb = queries_of(
+        scalars,
+        ids_own,
+        ids_nb,
+        gains,
+        normed_own,
+        normed_nb,
+        (part_own, back_own, part_nb, back_nb),
+        q_pieces,
+    )
+
+    spans = {}
+    for name, parity in (("own", y), ("nb", 1 - y)):
+        seg_keys = lax.dynamic_slice_in_dim(seg_span, parity * rows, 3 * rows, 0)[None, :]
+        seg_rows = lax.dynamic_slice_in_dim(seg_pair, parity * rows, rows, 0)[:, None]
+        places = jnp.stack([y, 1 - y, 2 + y, 3 - y]) - parity
+        spans[name] = (places.astype(jnp.int32), seg_rows, seg_keys)
+    left, right = [], []
+    for head in range(kv_own.shape[0]):
+        blocks = (halo(kv_own[head]), halo(kv_nb[head]), kv_own[head], kv_nb[head])
+        places, seg_rows, seg_keys = spans["nb"]
+        sent = attend(head, places, queries_nb, seg_rows, seg_keys, blocks)
+        places, seg_rows, seg_keys = spans["own"]
+        kept = attend(head, places, queries_own, seg_rows, seg_keys, blocks)
+        got = swap_y(sent)
+        left.append(jnp.where(y == 0, kept, got))
+        right.append(jnp.where(y == 0, got, kept))
+    return jnp.concatenate(left + right, axis=1)
+
+
+def paired(mesh, shapes):
+    residual, _, weight, _, down = shapes[:5]
+    rows = residual[0] // mesh.size
+    return (
+        mesh.shape["dp"] == 4
+        and mesh.shape["adapter"] % 2 == 0
+        and down[0] // mesh.shape["adapter"] == 4
+        and rows % HEAD_DIM == 0
+        and 2 * rows == WINDOW
+        and weight[1] == (HEADS + 2 * KV_HEADS) * HEAD_DIM
+        and weight[0] // mesh.shape["adapter"] % 32 == 0
+    )
+
+
 def solution(mesh):
     placed = (
         P(("dp", "adapter"), None),
@@ -163,6 +645,11 @@
         P(("dp", "adapter"), None),
         P(("dp", "adapter")),
     )
-    return jax.shard_map(
-        body, mesh=mesh, in_specs=placed, out_specs=P(("dp", "adapter"), None), check_vma=False
-    )
+
+    def whole(*arrays):
+        body = paired_body if paired(mesh, [a.shape for a in arrays]) else general_body
+        return jax.shard_map(
+            body, mesh=mesh, in_specs=placed, out_specs=P(("dp", "adapter"), None), check_vma=False
+        )(*arrays)
+
+    return whole

time: 747 us -> 295 us (0.39)
  waiting for transfers between devices: 372 us -> 156 us
  blocking collectives: 188 us -> 0 us
  Pallas kernels: 0 us -> 55 us
  matrix products: 45.4 us -> 0 us
  local copies, waits for them, and re-layouts: 50.4 us -> 15 us
  other arithmetic: 34.9 us -> 11.6 us
  between operations: 13.7 us -> 1.13 us
  starting transfers between devices: 41.6 us -> 52.3 us
    all_to_all x1 -> x0, blocking collectives: 188 us -> none  [body(): lax.all_to_all(scratch_buffer, 'adapter', split_axis=0, concat_axis=0, ti...]
    all_gather x2 -> x0, waiting for transfers between devices: 83.1 us -> none  [the longest x1 55.6 us: body(): lax.all_gather(slab, 'adapter', axis=0, tiled=True)]
    ppermute x6 -> x61, waiting for transfers between devices: 236 us -> 156 us  [route(): return lax.ppermute(value, ('dp', 'adapter'), pairs)]
    pallas_call x0 -> x9, Pallas kernels: none -> 55 us  [the longest x2 15.9 us: keys_values(): pl.pallas_call(functools.partial(kv_kernel, count, inner), out_shape=jax....]
    all_to_all x1 -> x0, waiting for transfers between devices: 51.7 us -> none  [body(): lax.all_to_all(adapter_corrections, 'adapter', split_axis=0, concat_axis=...]
    dot_general x7 -> x0, matrix products: 45.4 us -> none  [the longest x1 16.6 us: body(): jnp.dot(normed, lax.all_gather(slab, 'adapter', axis=0, tiled=True), pref...]
    ppermute x6 -> x61, starting transfers between devices: 31.9 us -> 52.3 us  [route(): return lax.ppermute(value, ('dp', 'adapter'), pairs)]
    gather x1 -> x0, local copies, waits for them, and re-layouts: 13.2 us -> none  [body(): delta_update = delta_slots[slot]]
  transfers between devices with their start and end apart: 9 -> 61, of which waited for: 7 -> 21; matrix products, arithmetic and copies ran while one was open for 11% -> 7% of each run, Pallas kernels for 0% -> 19%
where the time goes in v1:
time: 295 us; the launch traced here: 291 us
  waiting for transfers between devices  156 us (53%)
  Pallas kernels  55 us (19%)
  starting transfers between devices  52.3 us (18%)
  local copies, waits for them, and re-layouts  15 us (5%)
  other arithmetic  11.6 us (4%)
    ppermute x61, waiting for transfers between devices, route(): return lax.ppermute(value, ('dp', 'adapter'), pairs)  156 us
    ppermute x61, starting transfers between devices, route(): return lax.ppermute(value, ('dp', 'adapter'), pairs)  52.3 us
    pallas_call x2, Pallas kernels, keys_values(): pl.pallas_call(functools.partial(kv_kernel, count, inner), out_shape=jax....  15.9 us
    pallas_call x2, Pallas kernels, adapter_ranks_of(): pl.pallas_call(functools.partial(rank_kernel, count), out_shape=jax.Shape...  14.2 us
    pallas_call x4, Pallas kernels, attend(): pl.pallas_call(attend_kernel, grid=(1,), out_shape=jax.ShapeDtypeStruct((...  13.8 us
    pallas_call x1, Pallas kernels, queries_of(): pl.pallas_call(functools.partial(query_kernel, count, inner), out_shape=[...  11.1 us
  transfers between devices with their start and end apart: 61, of which 21 were waited for; matrix products, arithmetic and copies ran while one was open for 7% of the time, Pallas kernels for 19%

profile of v1, /device:TPU:6, one launch (start us, length us, event | category | flops | bytes accessed | tf_op | source)
XLA Modules:
  0.0 291.1 jit_solution(4840754439665374052)
XLA Ops:
  10.7 3.5 %collective-permute-start.37 = (s32[1024]{0:T(1024)S(1)}, s32[1024]{0:T(1024)S(1)}, u32[]{:S(2)}, u32[]{:S(2)}) collective-permute-start(s32[1024]{0:T(1024)S(1)} %add_select_fusion), channel_id=1, source_target_pairs={{0,2},{1,3},{2,4},{3,5},{4,6},{5,7},{6,8},{7,9},{8,10},{9,11},{10,... | collective-permute-start | bytes 12296 | tf_op jit(solution)/shard_map/ppermute | solution.py:182
  15.1 3.2 %collective-permute-done.37 = s32[1024]{0:T(1024)S(1)} collective-permute-done((s32[1024]{0:T(1024)S(1)}, s32[1024]{0:T(1024)S(1)}, u32[]{:S(2)}, u32[]{:S(2)}) %collective-permute-start.37) | collective-permute-done | bytes 4128 | tf_op jit(solution)/shard_map/ppermute | solution.py:182
  20.8 5.5 %collective-permute-start.38 = (bf16[320,512]{1,0:T(8,128)(2,1)}, bf16[320,512]{1,0:T(8,128)(2,1)S(1)}, u32[]{:S(2)}, u32[]{:S(2)}) collective-permute-start(bf16[320,512]{1,0:T(8,128)(2,1)} %get-tuple-element.19), channel_id=1, source_target_pairs={{16,17},{17,0},{18,19},{19,2},{20,21},{21,4},{22,23},{23,6},{24,25... | collective-permute-start | bytes 983048 | tf_op jit(solution)/shard_map/ppermute | solution.py:182
  28.6 2.6 collective-permute-done.19
  31.3 55.3 %collective-permute-done.38 = bf16[320,512]{1,0:T(8,128)(2,1)S(1)} collective-permute-done((bf16[320,512]{1,0:T(8,128)(2,1)}, bf16[320,512]{1,0:T(8,128)(2,1)S(1)}, u32[]{:S(2)}, u32[]{:S(2)}) %collective-permute-start.38) | collective-permute-done | bytes 327712 | tf_op jit(solution)/shard_map/ppermute | solution.py:182
  89.4 9.8 %collective-permute-done.9.refs_11_ = bf16[48,2560]{1,0:T(8,128)(2,1)} collective-permute-done((bf16[48,2560]{1,0:T(8,128)(2,1)S(1)}, bf16[48,2560]{1,0:T(8,128)(2,1)}, u32[]{:S(2)}, u32[]{:S(2)}) %collective-permute-start.9) | collective-permute-done | bytes 245792 | tf_op jit(solution)/shard_map/ppermute | solution.py:182
  101.5 5.6 %collective-permute-done.25.refs_14_ = bf16[192,1024]{1,0:T(8,128)(2,1)} collective-permute-done((bf16[192,1024]{1,0:T(8,128)(2,1)S(1)}, bf16[192,1024]{1,0:T(8,128)(2,1)}, u32[]{:S(2)}, u32[]{:S(2)}) %collective-permute-start.25) | collective-permute-done | bytes 393248 | tf_op jit(solution)/shard_map/ppermute | solution.py:182
  110.6 4.6 %collective-permute-done.43.refs_10_ = bf16[384,512]{1,0:T(8,128)(2,1)S(1)} collective-permute-done((bf16[384,512]{1,0:T(8,128)(2,1)S(1)}, bf16[384,512]{1,0:T(8,128)(2,1)S(1)}, u32[]{:S(2)}, u32[]{:S(2)}) %collective-permute-start.43) | collective-permute-done | bytes 393248 | tf_op jit(solution)/shard_map/ppermute | solution.py:182
  116.5 9.6 %collective-permute-done.13.refs_15_ = bf16[48,2560]{1,0:T(8,128)(2,1)} collective-permute-done((bf16[48,2560]{1,0:T(8,128)(2,1)}, bf16[48,2560]{1,0:T(8,128)(2,1)}, u32[]{:S(2)}, u32[]{:S(2)}) %collective-permute-start.13) | collective-permute-done | bytes 245792 | tf_op jit(solution)/shard_map/ppermute | solution.py:182
  137.6 9.3 %collective-permute-done.29.refs_18_ = bf16[192,1024]{1,0:T(8,128)(2,1)} collective-permute-done((bf16[192,1024]{1,0:T(8,128)(2,1)}, bf16[192,1024]{1,0:T(8,128)(2,1)}, u32[]{:S(2)}, u32[]{:S(2)}) %collective-permute-start.29) | collective-permute-done | bytes 393248 | tf_op jit(solution)/shard_map/ppermute | solution.py:182
  147.3 2.2 collective-permute-start.48
  149.6 2.8 collective-permute-done.51.refs_18_
  154.1 2.3 fusion.3
  157.2 5.5 %collective-permute-done.33.refs_22_ = bf16[192,1024]{1,0:T(8,128)(2,1)S(1)} collective-permute-done((bf16[192,1024]{1,0:T(8,128)(2,1)}, bf16[192,1024]{1,0:T(8,128)(2,1)S(1)}, u32[]{:S(2)}, u32[]{:S(2)}) %collective-permute-start.33) | collective-permute-done | bytes 393248 | tf_op jit(solution)/shard_map/ppermute | solution.py:182
  163.2 4.2 %collective-permute-done.52.refs_19_ = bf16[384,512]{1,0:T(8,128)(2,1)S(1)} collective-permute-done((bf16[384,512]{1,0:T(8,128)(2,1)}, bf16[384,512]{1,0:T(8,128)(2,1)S(1)}, u32[]{:S(2)}, u32[]{:S(2)}) %collective-permute-start.52) | collective-permute-done | bytes 393248 | tf_op jit(solution)/shard_map/ppermute | solution.py:182
  167.4 3.0 %fusion.5 = (bf16[512,2560]{1,0:T(8,128)(2,1)S(1)}, bf16[512,2560]{1,0:T(8,128)(2,1)S(1)}) fusion(bf16[512,2560]{1,0:T(8,128)(2,1)} %collective-permute-done.1, f32[512]{0:T(512)S(1)} %add_rsqrt_fusion, f32[2560]{0:T(1024)S(1)} %copy-done.41, f32[512]{0:T(512)S(1)} %add_rsqrt_fusion.1, bf16[512,2560]{1,0:T(8,128)(2,1)S(1)} %copy-done.39), kind=kLoop, calls=%fused_computation.9 | loop fusion | flops 10485760 | bytes 10500096 | tf_op jit(solution)/shard_map/convert_element_type | solution.py:188
  170.5 7.2 %shard_map.83.refs_8_.refs_4_ = bf16[48,512]{1,0:T(8,128)(2,1)S(1)} custom-call(s32[6,16]{1,0:T(8,128)S(1)} %stack.480.refs_0_, s32[1,512]{1,0:T(1,128)S(1)} %get-tuple-element.38.refs_1_.refs_2_, bf16[512,2560]{1,0:T(8,128)(2,1)S(1)} %get-tuple-element.31.refs_2_.refs_5_.refs_3_, bf16[48,2560]{1,0:T(8,128)(2,1)S(1)} %copy-done.7, ...), custom_call_target="tpu_custom_call" | custom-call | flops 2013265920 | bytes 6553600 | tf_op jit(solution)/shard_map/pallas_call | solution.py:222
  179.1 7.0 %shard_map.82.refs_6_.refs_4_ = bf16[48,512]{1,0:T(8,128)(2,1)S(1)} custom-call(s32[6,16]{1,0:T(8,128)S(1)} %stack.480.refs_0_, s32[1,512]{1,0:T(1,128)S(1)} %bitcast.124, bf16[512,2560]{1,0:T(8,128)(2,1)S(1)} %get-tuple-element.32.refs_2_.refs_4_.refs_3_, bf16[48,2560]{1,0:T(8,128)(2,1)S(1)} %copy-done.7, bf16[48,2560]{1,0:T(8,128)(2,1)S(1)} %copy-done.17, ...), custom_call_target="tpu_custom_call" | custom-call | flops 2013265920 | bytes 6553600 | tf_op jit(solution)/shard_map/pallas_call | solution.py:222
  189.3 8.0 %shard_map.85 = bf16[2,512,512]{2,1,0:T(8,128)(2,1)S(1)} custom-call(s32[6,16]{1,0:T(8,128)S(1)} %stack.480.refs_0_, s32[1,512]{1,0:T(1,128)S(1)} %bitcast.125, f32[2,256]{1,0:T(2,128)S(1)} %copy-done.9, bf16[512,2560]{1,0:T(8,128)(2,1)S(1)} %get-tuple-element.32.refs_2_.refs_4_.refs_3_, bf16[48,512]{1,0:T(8,128)(2,1)S(1)} %shard_map.82.refs_6_.refs_4_, ...), custom_call_target="tpu_custom_call" | custom-call | flops 2684354560 | bytes 7864320 | tf_op jit(solution)/shard_map/pallas_call | solution.py:304
  200.8 6.0 %collective-permute-done.30.refs_19_ = bf16[192,1024]{1,0:T(8,128)(2,1)S(1)} collective-permute-done((bf16[192,1024]{1,0:T(8,128)(2,1)}, bf16[192,1024]{1,0:T(8,128)(2,1)S(1)}, u32[]{:S(2)}, u32[]{:S(2)}) %collective-permute-start.30) | collective-permute-done | bytes 393248 | tf_op jit(solution)/shard_map/ppermute | solution.py:182
  206.8 7.2 %collective-permute-done.34.refs_23_ = bf16[192,1024]{1,0:T(8,128)(2,1)S(1)} collective-permute-done((bf16[192,1024]{1,0:T(8,128)(2,1)S(1)}, bf16[192,1024]{1,0:T(8,128)(2,1)S(1)}, u32[]{:S(2)}, u32[]{:S(2)}) %collective-permute-start.34) | collective-permute-done | bytes 393248 | tf_op jit(solution)/shard_map/ppermute | solution.py:182
  214.6 7.9 %shard_map.86 = bf16[2,512,512]{2,1,0:T(8,128)(2,1)S(1)} custom-call(s32[6,16]{1,0:T(8,128)S(1)} %stack.480.refs_0_, s32[1,512]{1,0:T(1,128)S(1)} %get-tuple-element.38.refs_1_.refs_2_, f32[2,256]{1,0:T(2,128)S(1)} %copy-done.9, bf16[512,2560]{1,0:T(8,128)(2,1)S(1)} %get-tuple-element.31.refs_2_.refs_5_.refs_3_, ...), custom_call_target="tpu_custom_call" | custom-call | flops 2684354560 | bytes 7864320 | tf_op jit(solution)/shard_map/pallas_call | solution.py:304
  226.5 2.6 collective-permute-start.55
  229.1 5.9 %collective-permute-start.56 = (bf16[512,512]{1,0:T(8,128)(2,1)S(1)}, bf16[512,512]{1,0:T(8,128)(2,1)}, u32[]{:S(2)}, u32[]{:S(2)}) collective-permute-start(bf16[512,512]{1,0:T(8,128)(2,1)S(1)} %get-tuple-element.15.refs_3_), channel_id=1, source_target_pairs={{0,2},{1,3},{2,4},{3,5},{4,6},{5,7},{6,8},{7,9},{8,10},{9,11},{10,... | collective-permute-start | bytes 1572872 | tf_op jit(solution)/shard_map/ppermute | solution.py:182
  235.1 11.1 %shard_map.84 = (bf16[512,1024]{1,0:T(8,128)(2,1)S(1)}, bf16[512,1024]{1,0:T(8,128)(2,1)S(1)}) custom-call(s32[6,16]{1,0:T(8,128)S(1)} %stack.480.refs_0_, s32[1,512]{1,0:T(1,128)S(1)} %bitcast.126, s32[1,512]{1,0:T(1,128)S(1)} %get-tuple-element.38.refs_1_.refs_2_, f32[2,256]{1,0:T(2,128)S(1)} %copy-done.9, ...), custom_call_target="tpu_custom_call" | custom-call | flops 5368709120 | bytes 10485760 | tf_op jit(solution)/shard_map/pallas_call | solution.py:363
  246.2 6.4 %collective-permute-done.59.refs_1_ = bf16[512,512]{1,0:T(8,128)(2,1)S(1)} collective-permute-done((bf16[512,512]{1,0:T(8,128)(2,1)S(1)}, bf16[512,512]{1,0:T(8,128)(2,1)S(1)}, u32[]{:S(2)}, u32[]{:S(2)}) %collective-permute-start.59) | collective-permute-done | bytes 524320 | tf_op jit(solution)/shard_map/ppermute | solution.py:182
  252.6 3.5 %shard_map.90 = bf16[512,512]{1,0:T(8,128)(2,1)} custom-call(s32[4]{0:T(128)S(1)} %broadcast_subtract_fusion.places, bf16[512,1024]{1,0:T(8,128)(2,1)S(1)} %get-tuple-element.8.queries, s32[512,1]{1,0:T(8,128)S(1)} %copy-done.5, s32[1,1536]{1,0:T(1,128)S(1)} %broadcast_in_dim.24.seg_keys, bf16[512,512]{1,0:T(8,128)(2,1)S(1)} %collective-permute-done.58.refs_0_, ...), custom_call_target="tpu_custom_call" | custom-call | flops 1342177280 | bytes 3145728 | tf_op jit(solution)/shard_map/pallas_call | solution.py:445
  257.2 6.7 %collective-permute-done.55.refs_0_ = bf16[512,512]{1,0:T(8,128)(2,1)} collective-permute-done((bf16[512,512]{1,0:T(8,128)(2,1)}, bf16[512,512]{1,0:T(8,128)(2,1)}, u32[]{:S(2)}, u32[]{:S(2)}) %collective-permute-start.55) | collective-permute-done | bytes 524320 | tf_op jit(solution)/shard_map/ppermute | solution.py:182
  264.0 11.2 %collective-permute-done.56.refs_1_ = bf16[512,512]{1,0:T(8,128)(2,1)} collective-permute-done((bf16[512,512]{1,0:T(8,128)(2,1)S(1)}, bf16[512,512]{1,0:T(8,128)(2,1)}, u32[]{:S(2)}, u32[]{:S(2)}) %collective-permute-start.56) | collective-permute-done | bytes 524320 | tf_op jit(solution)/shard_map/ppermute | solution.py:182
  276.4 3.7 %shard_map.88 = bf16[512,512]{1,0:T(8,128)(2,1)S(1)} custom-call(s32[4]{0:T(128)S(1)} %broadcast_subtract_fusion.places, bf16[512,1024]{1,0:T(8,128)(2,1)S(1)} %copy-done.37, s32[512,1]{1,0:T(8,128)S(1)} %copy-done.5, s32[1,1536]{1,0:T(1,128)S(1)} %broadcast_in_dim.24.seg_keys, bf16[512,512]{1,0:T(8,128)(2,1)} %collective-permute-done.55.refs_0_, ...), custom_call_target="tpu_custom_call" | custom-call | flops 1342177280 | bytes 3145728 | tf_op jit(solution)/shard_map/pallas_call | solution.py:445
  281.1 2.9 %shard_map.89 = bf16[512,512]{1,0:T(8,128)(2,1)S(1)} custom-call(s32[4]{0:T(128)S(1)} %get-tuple-element.9.places, bf16[512,1024]{1,0:T(8,128)(2,1)S(1)} %copy-done.35, s32[512,1]{1,0:T(8,128)S(1)} %copy.41.seg_rows, s32[1,1536]{1,0:T(1,128)S(1)} %broadcast_in_dim.22.seg_keys, bf16[512,512]{1,0:T(8,128)(2,1)S(1)} %copy-done.11, ...), custom_call_target="tpu_custom_call" | custom-call | flops 1342177280 | bytes 3145728 | tf_op jit(solution)/shard_map/pallas_call | solution.py:445
  284.0 3.7 %shard_map.87 = bf16[512,512]{1,0:T(8,128)(2,1)S(1)} custom-call(s32[4]{0:T(128)S(1)} %get-tuple-element.9.places, bf16[512,1024]{1,0:T(8,128)(2,1)S(1)} %copy-done.35, s32[512,1]{1,0:T(8,128)S(1)} %copy.41.seg_rows, s32[1,1536]{1,0:T(1,128)S(1)} %broadcast_in_dim.22.seg_keys, bf16[512,512]{1,0:T(8,128)(2,1)} %collective-permute-done.55.refs_0_, ...), custom_call_target="tpu_custom_call" | custom-call | flops 1342177280 | bytes 3145728 | tf_op jit(solution)/shard_map/pallas_call | solution.py:445
  (251 shorter events, 59.8 us)
Async XLA Ops:
  1.2 18.9 %collective-permute-start.2 = (bf16[48,2560]{1,0:T(8,128)(2,1)S(1)}, bf16[48,2560]{1,0:T(8,128)(2,1)S(1)}, u32[]{:S(2)}, u32[]{:S(2)}) collective-permute-start(bf16[48,2560]{1,0:T(8,128)(2,1)S(1)} %dynamic-slice_bitcast_fusion.refs_3_), channel_id=1, source_target_pairs={{0,16},{1,17},{2,18},{3,19},{4,20},{5,21},{6,22},{7,23},{8,24},{9,... | collective-permute-start | bytes 737288 | tf_op jit(solution)/shard_map/ppermute | solution.py:182
  1.8 19.0 %collective-permute-start.3 = (bf16[48,2560]{1,0:T(8,128)(2,1)S(1)}, bf16[48,2560]{1,0:T(8,128)(2,1)S(1)}, u32[]{:S(2)}, u32[]{:S(2)}) collective-permute-start(bf16[48,2560]{1,0:T(8,128)(2,1)S(1)} %dynamic-slice_bitcast_fusion.refs_3_), channel_id=1, source_target_pairs={{0,8},{1,9},{2,10},{3,11},{4,12},{5,13},{6,14},{7,15},{8,0},{9,1},... | collective-permute-start | bytes 737288 | tf_op jit(solution)/shard_map/ppermute | solution.py:182
  1.8 24.6 %collective-permute-start.5 = (bf16[48,2560]{1,0:T(8,128)(2,1)S(1)}, bf16[48,2560]{1,0:T(8,128)(2,1)S(1)}, u32[]{:S(2)}, u32[]{:S(2)}) collective-permute-start(bf16[48,2560]{1,0:T(8,128)(2,1)S(1)} %dynamic-slice_bitcast_fusion.refs_3_), channel_id=1, source_target_pairs={{0,2},{1,3},{2,4},{3,5},{4,6},{5,7},{6,0},{7,1},{8,10},{9,11},{10,... | collective-permute-start | bytes 737288 | tf_op jit(solution)/shard_map/ppermute | solution.py:182
  18.3 134.1 %collective-permute-start.1 = (bf16[512,2560]{1,0:T(8,128)(2,1)}, bf16[512,2560]{1,0:T(8,128)(2,1)}, u32[]{:S(2)}, u32[]{:S(2)}) collective-permute-start(bf16[512,2560]{1,0:T(8,128)(2,1)} %param.8), channel_id=1, source_target_pairs={{0,1},{1,0},{2,3},{3,2},{4,5},{5,4},{6,7},{7,6},{8,9},{9,8},{10,11... | collective-permute-start | bytes 7864328 | tf_op jit(solution)/shard_map/ppermute | solution.py:182
  20.8 65.8 %collective-permute-start.38 = (bf16[320,512]{1,0:T(8,128)(2,1)}, bf16[320,512]{1,0:T(8,128)(2,1)S(1)}, u32[]{:S(2)}, u32[]{:S(2)}) collective-permute-start(bf16[320,512]{1,0:T(8,128)(2,1)} %get-tuple-element.19), channel_id=1, source_target_pairs={{16,17},{17,0},{18,19},{19,2},{20,21},{21,4},{22,23},{23,6},{24,25... | collective-permute-start | bytes 983048 | tf_op jit(solution)/shard_map/ppermute | solution.py:182
  26.4 61.2 %collective-permute-start.39 = (bf16[320,512]{1,0:T(8,128)(2,1)}, bf16[320,512]{1,0:T(8,128)(2,1)S(1)}, u32[]{:S(2)}, u32[]{:S(2)}) collective-permute-start(bf16[320,512]{1,0:T(8,128)(2,1)} %get-tuple-element.20), channel_id=1, source_target_pairs={{17,1},{19,3},{21,5},{23,7},{25,9},{27,11},{29,13},{31,15}} | collective-permute-start | bytes 983048 | tf_op jit(solution)/shard_map/ppermute | solution.py:182
  31.2 57.1 %collective-permute-start.6 = (bf16[48,2560]{1,0:T(8,128)(2,1)S(1)}, bf16[48,2560]{1,0:T(8,128)(2,1)S(1)}, u32[]{:S(2)}, u32[]{:S(2)}) collective-permute-start(bf16[48,2560]{1,0:T(8,128)(2,1)S(1)} %collective-permute-done.5.refs_7_), channel_id=1, source_target_pairs={{0,16},{1,17},{2,18},{3,19},{4,20},{5,21},{6,22},{7,23},{8,24},{9,... | collective-permute-start | bytes 737288 | tf_op jit(solution)/shard_map/ppermute | solution.py:182
  31.2 57.2 %collective-permute-start.7 = (bf16[48,2560]{1,0:T(8,128)(2,1)S(1)}, bf16[48,2560]{1,0:T(8,128)(2,1)S(1)}, u32[]{:S(2)}, u32[]{:S(2)}) collective-permute-start(bf16[48,2560]{1,0:T(8,128)(2,1)S(1)} %collective-permute-done.5.refs_7_), channel_id=1, source_target_pairs={{0,8},{1,9},{2,10},{3,11},{4,12},{5,13},{6,14},{7,15},{8,0},{9,1},... | collective-permute-start | bytes 737288 | tf_op jit(solution)/shard_map/ppermute | solution.py:182
  88.5 18.7 %collective-permute-start.25 = (bf16[192,1024]{1,0:T(8,128)(2,1)S(1)}, bf16[192,1024]{1,0:T(8,128)(2,1)}, u32[]{:S(2)}, u32[]{:S(2)}) collective-permute-start(bf16[192,1024]{1,0:T(8,128)(2,1)S(1)} %pad_maximum_fusion.2.refs_10_), channel_id=1, source_target_pairs={{0,2},{1,3},{2,4},{3,5},{4,6},{5,7},{6,0},{7,1},{8,10},{9,11},{10,... | collective-permute-start | bytes 1179656 | tf_op jit(solution)/shard_map/ppermute | solution.py:182
  108.9 19.0 %collective-permute-start.10 = (bf16[48,2560]{1,0:T(8,128)(2,1)}, bf16[48,2560]{1,0:T(8,128)(2,1)}, u32[]{:S(2)}, u32[]{:S(2)}) collective-permute-start(bf16[48,2560]{1,0:T(8,128)(2,1)} %collective-permute-done.9.refs_11_), channel_id=1, source_target_pairs={{0,16},{1,17},{2,18},{3,19},{4,20},{5,21},{6,22},{7,23},{8,24},{9,... | collective-permute-start | bytes 737288 | tf_op jit(solution)/shard_map/ppermute | solution.py:182
  110.6 17.3 %collective-permute-start.11 = (bf16[48,2560]{1,0:T(8,128)(2,1)}, bf16[48,2560]{1,0:T(8,128)(2,1)}, u32[]{:S(2)}, u32[]{:S(2)}) collective-permute-start(bf16[48,2560]{1,0:T(8,128)(2,1)} %collective-permute-done.9.refs_11_), channel_id=1, source_target_pairs={{0,8},{1,9},{2,10},{3,11},{4,12},{5,13},{6,14},{7,15},{8,0},{9,1},... | collective-permute-start | bytes 737288 | tf_op jit(solution)/shard_map/ppermute | solution.py:182
  115.9 17.5 %collective-permute-start.47 = (bf16[384,512]{1,0:T(8,128)(2,1)S(1)}, bf16[384,512]{1,0:T(8,128)(2,1)S(1)}, u32[]{:S(2)}, u32[]{:S(2)}) collective-permute-start(bf16[384,512]{1,0:T(8,128)(2,1)S(1)} %collective-permute-done.43.refs_10_), channel_id=1, source_target_pairs={{0,2},{1,3},{2,4},{3,5},{4,6},{5,7},{6,0},{7,1},{8,10},{9,11},{10,... | collective-permute-start | bytes 1179656 | tf_op jit(solution)/shard_map/ppermute | solution.py:182
  130.6 16.7 %collective-permute-start.44 = (bf16[384,512]{1,0:T(8,128)(2,1)S(1)}, bf16[384,512]{1,0:T(8,128)(2,1)S(1)}, u32[]{:S(2)}, u32[]{:S(2)}) collective-permute-start(bf16[384,512]{1,0:T(8,128)(2,1)S(1)} %collective-permute-done.43.refs_10_), channel_id=1, source_target_pairs={{0,16},{1,17},{2,18},{3,19},{4,20},{5,21},{6,22},{7,23},{8,24},{9,... | collective-permute-start | bytes 1179656 | tf_op jit(solution)/shard_map/ppermute | solution.py:182
  133.4 19.0 %collective-permute-start.51 = (bf16[384,512]{1,0:T(8,128)(2,1)S(1)}, bf16[384,512]{1,0:T(8,128)(2,1)}, u32[]{:S(2)}, u32[]{:S(2)}) collective-permute-start(bf16[384,512]{1,0:T(8,128)(2,1)S(1)} %collective-permute-done.47.refs_14_), channel_id=1, source_target_pairs={{0,2},{1,3},{2,4},{3,5},{4,6},{5,7},{6,0},{7,1},{8,10},{9,11},{10,... | collective-permute-start | bytes 1179656 | tf_op jit(solution)/shard_map/ppermute | solution.py:182
  156.6 21.7 %collective-permute-start.49 = (bf16[384,512]{1,0:T(8,128)(2,1)S(1)}, bf16[384,512]{1,0:T(8,128)(2,1)S(1)}, u32[]{:S(2)}, u32[]{:S(2)}) collective-permute-start(bf16[384,512]{1,0:T(8,128)(2,1)S(1)} %collective-permute-done.47.refs_14_), channel_id=1, source_target_pairs={{0,8},{1,9},{2,10},{3,11},{4,12},{5,13},{6,14},{7,15},{8,0},{9,1},... | collective-permute-start | bytes 1179656 | tf_op jit(solution)/shard_map/ppermute | solution.py:182
  156.7 21.0 %collective-permute-start.46 = (bf16[384,512]{1,0:T(8,128)(2,1)S(1)}, bf16[384,512]{1,0:T(8,128)(2,1)S(1)}, u32[]{:S(2)}, u32[]{:S(2)}) collective-permute-start(bf16[384,512]{1,0:T(8,128)(2,1)S(1)} %collective-permute-done.44.refs_11_), channel_id=1, source_target_pairs={{0,8},{1,9},{2,10},{3,11},{4,12},{5,13},{6,14},{7,15},{8,0},{9,1},... | collective-permute-start | bytes 1179656 | tf_op jit(solution)/shard_map/ppermute | solution.py:182
  162.7 24.5 %collective-permute-start.53 = (bf16[384,512]{1,0:T(8,128)(2,1)}, bf16[384,512]{1,0:T(8,128)(2,1)S(1)}, u32[]{:S(2)}, u32[]{:S(2)}) collective-permute-start(bf16[384,512]{1,0:T(8,128)(2,1)} %collective-permute-done.51.refs_18_), channel_id=1, source_target_pairs={{0,8},{1,9},{2,10},{3,11},{4,12},{5,13},{6,14},{7,15},{8,0},{9,1},... | collective-permute-start | bytes 1179656 | tf_op jit(solution)/shard_map/ppermute | solution.py:182
  162.7 23.4 %collective-permute-start.50 = (bf16[384,512]{1,0:T(8,128)(2,1)S(1)}, bf16[384,512]{1,0:T(8,128)(2,1)S(1)}, u32[]{:S(2)}, u32[]{:S(2)}) collective-permute-start(bf16[384,512]{1,0:T(8,128)(2,1)S(1)} %collective-permute-done.48.refs_15_), channel_id=1, source_target_pairs={{0,8},{1,9},{2,10},{3,11},{4,12},{5,13},{6,14},{7,15},{8,0},{9,1},... | collective-permute-start | bytes 1179656 | tf_op jit(solution)/shard_map/ppermute | solution.py:182
  167.4 19.8 %collective-permute-start.54 = (bf16[384,512]{1,0:T(8,128)(2,1)S(1)}, bf16[384,512]{1,0:T(8,128)(2,1)S(1)}, u32[]{:S(2)}, u32[]{:S(2)}) collective-permute-start(bf16[384,512]{1,0:T(8,128)(2,1)S(1)} %collective-permute-done.52.refs_19_), channel_id=1, source_target_pairs={{0,8},{1,9},{2,10},{3,11},{4,12},{5,13},{6,14},{7,15},{8,0},{9,1},... | collective-permute-start | bytes 1179656 | tf_op jit(solution)/shard_map/ppermute | solution.py:182
  177.7 19.6 %collective-permute-start.24 = (bf16[192,1024]{1,0:T(8,128)(2,1)}, bf16[192,1024]{1,0:T(8,128)(2,1)S(1)}, u32[]{:S(2)}, u32[]{:S(2)}) collective-permute-start(bf16[192,1024]{1,0:T(8,128)(2,1)} %collective-permute-done.22.refs_11_), channel_id=1, source_target_pairs={{0,8},{1,9},{2,10},{3,11},{4,12},{5,13},{6,14},{7,15},{8,0},{9,1},... | collective-permute-start | bytes 1179656 | tf_op jit(solution)/shard_map/ppermute | solution.py:182
  187.2 19.6 %collective-permute-start.30 = (bf16[192,1024]{1,0:T(8,128)(2,1)}, bf16[192,1024]{1,0:T(8,128)(2,1)S(1)}, u32[]{:S(2)}, u32[]{:S(2)}) collective-permute-start(bf16[192,1024]{1,0:T(8,128)(2,1)} %collective-permute-done.29.refs_18_), channel_id=1, source_target_pairs={{0,16},{1,17},{2,18},{3,19},{4,20},{5,21},{6,22},{7,23},{8,24},{9,... | collective-permute-start | bytes 1179656 | tf_op jit(solution)/shard_map/ppermute | solution.py:182
  188.3 25.8 %collective-permute-start.34 = (bf16[192,1024]{1,0:T(8,128)(2,1)S(1)}, bf16[192,1024]{1,0:T(8,128)(2,1)S(1)}, u32[]{:S(2)}, u32[]{:S(2)}) collective-permute-start(bf16[192,1024]{1,0:T(8,128)(2,1)S(1)} %collective-permute-done.33.refs_22_), channel_id=1, source_target_pairs={{0,16},{1,17},{2,18},{3,19},{4,20},{5,21},{6,22},{7,23},{8,24},{9,... | collective-permute-start | bytes 1179656 | tf_op jit(solution)/shard_map/ppermute | solution.py:182
  197.3 16.8 %collective-permute-start.18 = (bf16[48,512]{1,0:T(8,128)(2,1)S(1)}, bf16[48,512]{1,0:T(8,128)(2,1)S(1)}, u32[]{:S(2)}, u32[]{:S(2)}) collective-permute-start(bf16[48,512]{1,0:T(8,128)(2,1)S(1)} %shard_map.82.refs_6_.refs_4_), channel_id=1, source_target_pairs={{0,1},{1,0},{2,3},{3,2},{4,5},{5,4},{6,7},{7,6},{8,9},{9,8},{10,11... | collective-permute-start | bytes 147464 | tf_op jit(solution)/shard_map/ppermute | solution.py:182
  200.2 24.3 %collective-permute-start.31 = (bf16[192,1024]{1,0:T(8,128)(2,1)}, bf16[192,1024]{1,0:T(8,128)(2,1)S(1)}, u32[]{:S(2)}, u32[]{:S(2)}) collective-permute-start(bf16[192,1024]{1,0:T(8,128)(2,1)} %collective-permute-done.29.refs_18_), channel_id=1, source_target_pairs={{0,8},{1,9},{2,10},{3,11},{4,12},{5,13},{6,14},{7,15},{8,0},{9,1},... | collective-permute-start | bytes 1179656 | tf_op jit(solution)/shard_map/ppermute | solution.py:182
  200.3 22.2 %collective-permute-start.28 = (bf16[192,1024]{1,0:T(8,128)(2,1)S(1)}, bf16[192,1024]{1,0:T(8,128)(2,1)S(1)}, u32[]{:S(2)}, u32[]{:S(2)}) collective-permute-start(bf16[192,1024]{1,0:T(8,128)(2,1)S(1)} %collective-permute-done.26.refs_15_), channel_id=1, source_target_pairs={{0,8},{1,9},{2,10},{3,11},{4,12},{5,13},{6,14},{7,15},{8,0},{9,1},... | collective-permute-start | bytes 1179656 | tf_op jit(solution)/shard_map/ppermute | solution.py:182
  206.8 22.3 %collective-permute-start.35 = (bf16[192,1024]{1,0:T(8,128)(2,1)S(1)}, bf16[192,1024]{1,0:T(8,128)(2,1)S(1)}, u32[]{:S(2)}, u32[]{:S(2)}) collective-permute-start(bf16[192,1024]{1,0:T(8,128)(2,1)S(1)} %collective-permute-done.33.refs_22_), channel_id=1, source_target_pairs={{0,8},{1,9},{2,10},{3,11},{4,12},{5,13},{6,14},{7,15},{8,0},{9,1},... | collective-permute-start | bytes 1179656 | tf_op jit(solution)/shard_map/ppermute | solution.py:182
  214.1 21.0 %collective-permute-start.36 = (bf16[192,1024]{1,0:T(8,128)(2,1)S(1)}, bf16[192,1024]{1,0:T(8,128)(2,1)S(1)}, u32[]{:S(2)}, u32[]{:S(2)}) collective-permute-start(bf16[192,1024]{1,0:T(8,128)(2,1)S(1)} %collective-permute-done.34.refs_23_), channel_id=1, source_target_pairs={{0,8},{1,9},{2,10},{3,11},{4,12},{5,13},{6,14},{7,15},{8,0},{9,1},... | collective-permute-start | bytes 1179656 | tf_op jit(solution)/shard_map/ppermute | solution.py:182
  222.6 23.6 %collective-permute-start.58 = (bf16[512,512]{1,0:T(8,128)(2,1)S(1)}, bf16[512,512]{1,0:T(8,128)(2,1)S(1)}, u32[]{:S(2)}, u32[]{:S(2)}) collective-permute-start(bf16[512,512]{1,0:T(8,128)(2,1)S(1)} %get-tuple-element.18.refs_2_), channel_id=1, source_target_pairs={{0,2},{1,3},{2,4},{3,5},{4,6},{5,7},{6,8},{7,9},{8,10},{9,11},{10,... | collective-permute-start | bytes 1572872 | tf_op jit(solution)/shard_map/ppermute | solution.py:182
  224.5 28.1 %collective-permute-start.59 = (bf16[512,512]{1,0:T(8,128)(2,1)S(1)}, bf16[512,512]{1,0:T(8,128)(2,1)S(1)}, u32[]{:S(2)}, u32[]{:S(2)}) collective-permute-start(bf16[512,512]{1,0:T(8,128)(2,1)S(1)} %get-tuple-element.16.refs_3_), channel_id=1, source_target_pairs={{0,2},{1,3},{2,4},{3,5},{4,6},{5,7},{6,8},{7,9},{8,10},{9,11},{10,... | collective-permute-start | bytes 1572872 | tf_op jit(solution)/shard_map/ppermute | solution.py:182
  226.5 37.4 %collective-permute-start.55 = (bf16[512,512]{1,0:T(8,128)(2,1)}, bf16[512,512]{1,0:T(8,128)(2,1)}, u32[]{:S(2)}, u32[]{:S(2)}) collective-permute-start(bf16[512,512]{1,0:T(8,128)(2,1)} %get-tuple-element.17.refs_2_), channel_id=1, source_target_pairs={{0,2},{1,3},{2,4},{3,5},{4,6},{5,7},{6,8},{7,9},{8,10},{9,11},{10,... | collective-permute-start | bytes 1572872 | tf_op jit(solution)/shard_map/ppermute | solution.py:182
  229.1 46.1 %collective-permute-start.56 = (bf16[512,512]{1,0:T(8,128)(2,1)S(1)}, bf16[512,512]{1,0:T(8,128)(2,1)}, u32[]{:S(2)}, u32[]{:S(2)}) collective-permute-start(bf16[512,512]{1,0:T(8,128)(2,1)S(1)} %get-tuple-element.15.refs_3_), channel_id=1, source_target_pairs={{0,2},{1,3},{2,4},{3,5},{4,6},{5,7},{6,8},{7,9},{8,10},{9,11},{10,... | collective-permute-start | bytes 1572872 | tf_op jit(solution)/shard_map/ppermute | solution.py:182
  256.1 31.7 %collective-permute-start.60 = (bf16[512,512]{1,0:T(8,128)(2,1)}, bf16[512,512]{1,0:T(8,128)(2,1)}, u32[]{:S(2)}, u32[]{:S(2)}) collective-permute-start(bf16[512,512]{1,0:T(8,128)(2,1)} %shard_map.90), channel_id=1, source_target_pairs={{0,1},{1,0},{2,3},{3,2},{4,5},{5,4},{6,7},{7,6},{8,9},{9,8},{10,11... | collective-permute-start | bytes 1572872 | tf_op jit(solution)/shard_map/ppermute | solution.py:182
  (71 other events, 1372.4 us)

commit v2 on v1

--- a/solution.py
+++ b/solution.py
@@ -3,6 +3,7 @@
 
 import jax
 import jax.numpy as jnp
+import numpy as np
 from jax import lax
 from jax.experimental import pallas as pl
 from jax.experimental.pallas import tpu as pltpu
@@ -162,6 +163,7 @@
 ANY = pl.BlockSpec(memory_space=pl.ANY)
 SMEM = pl.BlockSpec(memory_space=pltpu.SMEM)
 VMEM = pl.BlockSpec(memory_space=pltpu.VMEM)
+SMALL = pl.CostEstimate(flops=1, bytes_accessed=1, transcendentals=0)
 Q_ROW, KV_KIND, KV_ROW, UP_EVEN, UP_ODD, DOWN_ID = range(6)
 
 
@@ -182,6 +184,10 @@
     return lax.ppermute(value, ("dp", "adapter"), pairs)
 
 
+def after(value, *others):
+    return lax.optimization_barrier((value, others))[0]
+
+
 def row_norm(values, gain):
     values = values.astype(F32)
     scale = lax.rsqrt(jnp.mean(values * values, axis=-1, keepdims=True) + 1e-06)
@@ -195,17 +201,8 @@
         copy.wait()
 
 
-def rank_kernel(count, *refs):
-    scalars, ids, normed = refs[:3]
-    pieces = refs[3 : 3 + count]
-    out, down, sems = refs[3 + count :]
-    deep = pieces[0].shape[0]
-    copies_done(
-        [
-            pltpu.make_async_copy(pieces[i], down.at[pl.ds(i * deep, deep)], sems.at[i])
-            for i in range(count)
-        ]
-    )
+def masked_ranks(scalars, ids, down, normed, out, count):
+    deep = out.shape[0]
     every = lax.dot_general(
         down[...], normed[...], (((1,), (1,)), ((), ())), preferred_element_type=F32
     )
@@ -216,25 +213,54 @@
     out[...] = total.astype(BF16)
 
 
-def adapter_ranks_of(scalars, ids, normed, pieces):
+def rank_kernel(count, scalars, ids, normed, down, out):
+    masked_ranks(scalars, ids, down, normed, out, count)
+
+
+def first_rank_kernel(pieces, scalars, ids, normed, *refs):
+    held = refs[: len(pieces.arrays)]
+    out, down, sems = refs[len(pieces.arrays) :]
+    deep, count = pieces.deep, len(pieces.names)
+    copies = [
+        pltpu.make_async_copy(
+            pieces.cut(held, i, 0, deep), down.at[pl.ds(i * deep, deep)], sems.at[i]
+        )
+        for i in range(count)
+    ]
+    for copy in copies:
+        copy.start()
+    for copy in copies:
+        copy.wait()
+    masked_ranks(scalars, ids, down, normed, out, count)
+
+
+def first_ranks(scalars, ids, normed, pieces):
     rows, width = normed.shape
-    count, deep = len(pieces), pieces[0].shape[0]
+    count, deep = len(pieces.names), pieces.deep
+    return pl.pallas_call(
+        functools.partial(first_rank_kernel, pieces),
+        out_shape=[
+            jax.ShapeDtypeStruct((deep, rows), BF16),
+            jax.ShapeDtypeStruct((count * deep, width), BF16),
+        ],
+        in_specs=[SMEM, VMEM, VMEM] + [ANY] * len(pieces.arrays),
+        out_specs=[VMEM, VMEM],
+        scratch_shapes=[pltpu.SemaphoreType.DMA((count,))],
+        compiler_params=params(24),
+        cost_estimate=SMALL,
+    )(scalars, ids, normed, *pieces.arrays)
+
+
+def more_ranks(scalars, ids, normed, down, count):
+    rows, width = normed.shape
     return pl.pallas_call(
         functools.partial(rank_kernel, count),
-        out_shape=jax.ShapeDtypeStruct((deep, rows), BF16),
-        in_specs=[SMEM, VMEM, VMEM] + [ANY] * count,
+        out_shape=jax.ShapeDtypeStruct((down.shape[0] // count, rows), BF16),
+        in_specs=[SMEM, VMEM, VMEM, VMEM],
         out_specs=VMEM,
-        scratch_shapes=[
-            pltpu.VMEM((count * deep, width), BF16),
-            pltpu.SemaphoreType.DMA((count,)),
-        ],
         compiler_params=params(24),
-        cost_estimate=pl.CostEstimate(
-            flops=2 * rows * width * count * deep,
-            bytes_accessed=2 * (rows + count * deep) * width,
-            transcendentals=0,
-        ),
-    )(scalars, ids, normed, *pieces)
+        cost_estimate=SMALL,
+    )(scalars, ids, normed, down)
 
 
 def spread(ranks, ids, scalars, count, into):
@@ -259,67 +285,76 @@
     return (block * scale * gain).astype(BF16)
 
 
-def kv_kernel(count, inner, *refs):
-    scalars, ids, gains, normed, ranks_a, ranks_b = refs[:6]
-    pieces = refs[6 : 6 + count]
-    out, weight, up, into_k, into_v, sems = refs[6 + count :]
-    deep = pieces[0].shape[0] - 4 * inner
+class Pieces:
+    def __init__(self, arrays, names, deep):
+        self.arrays, self.names, self.deep = arrays, names, deep
+
+    def cut(self, refs, i, start, size, columns=None):
+        array, at = self.names[i]
+        rows = pl.ds(at * self.deep + start, size)
+        return refs[array].at[rows] if columns is None else refs[array].at[rows, columns]
+
+
+def kv_kernel(pieces, inner, head, *refs):
+    scalars, ids_own, ids_nb, gains = refs[:4]
+    ranks = refs[4:8]
+    normed = refs[8:10]
+    held = refs[10 : 10 + len(pieces.arrays)]
+    out, weight, up, into, sems = refs[10 + len(pieces.arrays) :]
+    deep, count = pieces.deep - 4 * inner, len(pieces.names)
+    columns = pl.ds(head * HEAD_DIM, HEAD_DIM)
     copies = []
     for i in range(count):
         kind = scalars[KV_KIND, i]
         row = pl.multiple_of(scalars[KV_ROW, i], deep)
         copies.append(
             pltpu.make_async_copy(
-                pieces[i].at[pl.ds(0, deep)], weight.at[kind, pl.ds(row, deep)], sems.at[3 * i]
+                pieces.cut(held, i, 0, deep, columns),
+                weight.at[kind, pl.ds(row, deep)],
+                sems.at[3 * i],
             )
         )
         for both in range(2):
             copies.append(
                 pltpu.make_async_copy(
-                    pieces[i].at[pl.ds(deep + 2 * inner * both, 2 * inner)],
+                    pieces.cut(held, i, deep + 2 * inner * both, 2 * inner, columns),
                     up.at[both, pl.ds(2 * inner * i, 2 * inner)],
                     sems.at[3 * i + 1 + both],
                 )
             )
     for copy in copies:
         copy.start()
-    ranks = ranks_a[...] + ranks_b[...]
-    spread(ranks[inner : 2 * inner], ids, scalars, count, into_k)
-    spread(ranks[2 * inner : 3 * inner], ids, scalars, count, into_v)
+    for side, ids in ((0, ids_own), (1, ids_nb)):
+        both = ranks[2 * side][...] + ranks[2 * side + 1][...]
+        for kind in range(2):
+            part = both[(1 + kind) * inner : (2 + kind) * inner]
+            spread(part, ids, scalars, count, into.at[2 * side + kind])
     for copy in copies:
         copy.wait()
-    for head in range(weight.shape[2] // HEAD_DIM):
-        cut = slice(head * HEAD_DIM, (head + 1) * HEAD_DIM)
-        keys = project(normed[...], weight[0, :, cut], into_k[...], up[0, :, cut])
-        out[head, :, 0:HEAD_DIM] = unit(keys, gains[1:2, :])
-        values = project(normed[...], weight[1, :, cut], into_v[...], up[1, :, cut])
-        out[head, :, HEAD_DIM:] = values.astype(BF16)
-
-
-def keys_values(scalars, ids, gains, normed, ranks_a, ranks_b, pieces):
-    rows, width = normed.shape
-    count, inner = len(pieces), ranks_a.shape[0] // 3
-    columns = pieces[0].shape[1]
-    heads = columns // HEAD_DIM
+    for side in range(2):
+        keys = project(normed[side][...], weight[0], into[2 * side], up[0])
+        out[side, :, 0:HEAD_DIM] = unit(keys, gains[1:2, :])
+        values = project(normed[side][...], weight[1], into[2 * side + 1], up[1])
+        out[side, :, HEAD_DIM:] = values.astype(BF16)
+
+
+def keys_values(head, scalars, ids_own, ids_nb, gains, ranks, normed_own, normed_nb, pieces):
+    rows, width = normed_own.shape
+    count, inner = len(pieces.names), ranks[0].shape[0] // 3
     return pl.pallas_call(
-        functools.partial(kv_kernel, count, inner),
-        out_shape=jax.ShapeDtypeStruct((heads, rows, 2 * HEAD_DIM), BF16),
-        in_specs=[SMEM, VMEM, VMEM, VMEM, VMEM, VMEM] + [ANY] * count,
+        functools.partial(kv_kernel, pieces, inner, head),
+        out_shape=jax.ShapeDtypeStruct((2, rows, 2 * HEAD_DIM), BF16),
+        in_specs=[SMEM] + [VMEM] * 9 + [ANY] * len(pieces.arrays),
         out_specs=VMEM,
         scratch_shapes=[
-            pltpu.VMEM((2, width, columns), BF16),
-            pltpu.VMEM((2, 2 * inner * count, columns), BF16),
-            pltpu.VMEM((2 * inner * count, rows), BF16),
-            pltpu.VMEM((2 * inner * count, rows), BF16),
+            pltpu.VMEM((2, width, HEAD_DIM), BF16),
+            pltpu.VMEM((2, 2 * inner * count, HEAD_DIM), BF16),
+            pltpu.VMEM((4, 2 * inner * count, rows), BF16),
             pltpu.SemaphoreType.DMA((3 * count,)),
         ],
         compiler_params=params(32),
-        cost_estimate=pl.CostEstimate(
-            flops=4 * rows * width * columns,
-            bytes_accessed=2 * (rows + 2 * columns) * width,
-            transcendentals=0,
-        ),
-    )(scalars, ids, gains, normed, ranks_a, ranks_b, *pieces)
+        cost_estimate=SMALL,
+    )(scalars, ids_own, ids_nb, gains, *ranks, normed_own, normed_nb, *pieces.arrays)
 
 
 def query_kernel(count, inner, *refs):
@@ -372,17 +407,14 @@
             pltpu.VMEM((2 * inner * count, rows), BF16),
             pltpu.SemaphoreType.DMA((2 * count,)),
         ],
-        compiler_params=params(40),
-        cost_estimate=pl.CostEstimate(
-            flops=4 * rows * width * columns,
-            bytes_accessed=2 * (2 * rows + columns) * width,
-            transcendentals=0,
-        ),
+        compiler_params=params(56),
+        cost_estimate=SMALL,
     )(scalars, ids_own, ids_nb, gains, normed_own, normed_nb, *ranks, *pieces)
 
 
 def attend_kernel(places, queries, seg_rows, seg_keys, *refs):
-    blocks, out, held, sems = refs[:4], refs[4], refs[5], refs[6]
+    before, here_too, out, held, sems = refs
+    blocks = [before.at[0], before.at[1], here_too.at[0], here_too.at[1]]
     rows = queries.shape[0]
     slots = held.shape[0]
     for wait in (False, True):
@@ -452,19 +484,37 @@
             pl.BlockSpec((rows, 1), lambda i: (0, 0)),
             pl.BlockSpec((1, slots * rows), lambda i: (0, 0)),
         ]
-        + [ANY] * 4,
+        + [ANY] * 2,
         out_specs=pl.BlockSpec((rows, width), lambda i: (0, 0)),
         scratch_shapes=[
             pltpu.VMEM((slots, rows, 2 * HEAD_DIM), BF16),
             pltpu.SemaphoreType.DMA((4,)),
         ],
         compiler_params=params(24),
-        cost_estimate=pl.CostEstimate(
-            flops=4 * rows * width * (WINDOW + HEAD_DIM),
-            bytes_accessed=2 * rows * HEAD_DIM * 12,
-            transcendentals=2 * rows * (WINDOW + HEAD_DIM),
-        ),
+        cost_estimate=SMALL,
     )(places, queries, seg_rows, seg_keys, *blocks)
+
+
+def side_kernel(count, where, *refs):
+    y = where[0]
+    out = refs[2 * count]
+    width = refs[0].shape[1]
+    for side, at in ((0, y), (1, 1 - y)):
+        for i in range(count):
+            start = pl.multiple_of((at * count + i) * width, width)
+            out[:, pl.ds(start, width)] = refs[side * count + i][...]
+
+
+def side_by_side(where, kept, got):
+    rows, width = kept[0].shape
+    return pl.pallas_call(
+        functools.partial(side_kernel, len(kept)),
+        out_shape=jax.ShapeDtypeStruct((rows, 2 * width * len(kept)), BF16),
+        in_specs=[SMEM] + [VMEM] * (2 * len(kept)),
+        out_specs=VMEM,
+        compiler_params=params(16),
+        cost_estimate=SMALL,
+    )(where, *kept, *got)
 
 
 def paired_body(
@@ -507,14 +557,7 @@
     got_top = route(top, depth, lambda x, c, z, y: (0, y, z, c) if x == 0 and c != y else None)
     got_bottom = route(bottom, depth, lambda x, c, z, y: (1, y, z, c) if x == 0 else None)
     got_theirs = route(
-        theirs,
-        depth,
-        lambda x, c, z, y: None if x == 0 else (1, c, z, 1) if y == 0 else (0, c, z, 0),
-    )
-    got_mine = route(mine, depth, lambda x, c, z, y: (0, c, z, 1) if x == 1 and y == 1 else None)
-    share_q = jnp.where(x == 1, got_bottom, jnp.where(core == y, top, got_top))
-    share_kv = jnp.where(
-        x == 0, jnp.where(y == 0, got_theirs, got_mine), jnp.where(y == 0, mine, got_theirs)
+        theirs, depth, lambda x, c, z, y: (0, c, z, 1 - y) if x == 1 else None
     )
     up_one = lax.dynamic_index_in_dim(adapter_up_weight, place, 0, keepdims=False)
 
@@ -525,8 +568,17 @@
             lax.dynamic_slice_in_dim(up_one, width_q + width_k + which * half_k, half_k, 1),
         )
 
+    up_other = swap_y(jnp.concatenate(up_half(1 - y), axis=1))
+    share_down = lax.dynamic_index_in_dim(adapter_down_weight, place, 0, keepdims=False).T
+    numbers = jnp.stack([row_adapter_index[:, 0], row_sequence_index])
+    other_numbers = swap_y(numbers)
+    down = [share_down, ring(share_down)]
+    got_top, got_bottom, got_theirs, up_other, other_numbers, down = lax.optimization_barrier(
+        (got_top, got_bottom, got_theirs, up_other, other_numbers, down)
+    )
+    share_q = jnp.where(x == 1, got_bottom, jnp.where(core == y, top, got_top))
+    share_kv = jnp.where(x == 0, got_theirs, mine)
     up_own = jnp.concatenate(up_half(y), axis=1)
-    up_other = swap_y(jnp.concatenate(up_half(1 - y), axis=1))
     up_pair = jnp.concatenate(
         [jnp.where(y == 0, up_own, up_other), jnp.where(y == 0, up_other, up_own)], axis=0
     )
@@ -534,72 +586,113 @@
     share_kv = jnp.concatenate(
         [share_kv, up_pair[:, half_q : half_q + half_k], up_pair[:, half_q + half_k :]], axis=0
     )
-    share_down = lax.dynamic_index_in_dim(adapter_down_weight, place, 0, keepdims=False).T
-
-    other_input = swap_y(residual_input)
-    numbers = jnp.stack([row_adapter_index[:, 0], row_sequence_index])
-    other_numbers = swap_y(numbers)
+
     ids_own, ids_nb = numbers[0:1], other_numbers[0:1]
     seg_pair = jnp.where(
         y == 0,
         jnp.concatenate([numbers[1], other_numbers[1]]),
         jnp.concatenate([other_numbers[1], numbers[1]]),
     )
-    seg_before = jnp.where((place == 0) & (z == 0), -1, halo(seg_pair))
-    seg_span = jnp.concatenate([seg_before, seg_pair])
     normed_own = row_norm(residual_input, input_norm_gain)
-    normed_nb = row_norm(other_input, input_norm_gain)
-
-    def gathered(share):
-        pieces = []
-        for step in range(depth):
-            if step:
-                share = ring(share)
-            across = swap_x(share)
-            pieces += [share, across, swap_core(share), swap_core(across)]
-        return pieces
-
-    down_pieces = gathered(share_down)
-    kv_pieces = gathered(share_kv)
-    q_pieces = gathered(share_q)
-    table = []
-    for step in range(depth):
-        chunk = (z + depth - step) % depth
-        for flip_x, flip_core in ((0, 0), (1, 0), (0, 1), (1, 1)):
-            at_x = x + flip_x * (1 - 2 * x)
-            at_core = core + flip_core * (1 - 2 * core)
-            adapter = 2 * chunk * local + 2 * at_x + at_core
-            table.append(
-                jnp.stack(
-                    [
-                        (2 * chunk + at_core) * deep + at_x * (deep // 2),
-                        at_core,
-                        (2 * chunk + 1 - at_x) * deep,
-                        adapter,
-                        adapter + local,
-                        adapter + y * local,
-                    ]
-                )
-            )
-    scalars = jnp.stack(table, axis=1).astype(jnp.int32)
-
-    part_own = adapter_ranks_of(scalars, ids_own, normed_own, down_pieces)
-    part_nb = adapter_ranks_of(scalars, ids_nb, normed_nb, down_pieces)
+
+    step, flip = np.arange(4).repeat(4), np.tile(np.arange(4), 4)
+    chunk = (z + depth - step) % depth
+    at_x = x + flip % 2 * (1 - 2 * x)
+    at_core = core + flip // 2 * (1 - 2 * core)
+    adapter = 2 * chunk * local + 2 * at_x + at_core
+    scalars = jnp.stack(
+        [
+            (2 * chunk + at_core) * deep + at_x * (deep // 2),
+            at_core,
+            (2 * chunk + jnp.where(at_x == 1, y, 1 - y)) * deep,
+            adapter,
+            adapter + local,
+            adapter + y * local,
+        ]
+    ).astype(jnp.int32)
+
+    residual = jnp.split(residual_input, 4, axis=0)
+
+    def group(ready, *values):
+        return lax.optimization_barrier((values, ready))
+
+    kv, q = [share_kv], [share_q]
+    kv_x, kv_c, kv_xc, q_x, q_c, q_xc = [], [], [], [], [], []
+    down_x, down_c, down_xc, other = [], [], [], []
+    kv.append(ring(kv[0]))
+    other.append(swap_y(residual[0]))
+    kv_x.append(swap_x(kv[0]))
+    kv_c.append(swap_core(kv[0]))
+    down.append(ring(down[1]))
+    down_x.append(swap_x(down[0]))
+    down_c.append(swap_core(down[0]))
+    for step in range(1, 4):
+        (kv[step], kv_x[-1], part), _ = group((kv_c[-1],), kv[step], kv_x[-1], residual[step])
+        if step < 3:
+            kv.append(ring(kv[step]))
+        other.append(swap_y(part))
+        kv_x.append(swap_x(kv[step]))
+        kv_c.append(swap_core(kv[step]))
+        kv_xc.append(swap_core(kv_x[-2]))
+        (onward_z, down[step], down_x[-1]), (_, other[-2]) = group(
+            (down_c[-1], other[-2]),
+            down[2] if step == 1 else q[-1],
+            down[step],
+            down_x[-1],
+        )
+        if step == 1:
+            down[2] = onward_z
+            down.append(ring(down[2]))
+        else:
+            q[-1] = onward_z
+            q.append(ring(q[-1]))
+        down_x.append(swap_x(down[step]))
+        down_c.append(swap_core(down[step]))
+        down_xc.append(swap_core(down_x[-2]))
+    (q[0], kv_x[-1]), _ = group((kv_c[-1],), q[0], kv_x[-1])
+    kv_xc.append(swap_core(kv_x[-1]))
+    (down_x[-1],), (_, other[-1]) = group((down_c[-1], other[-1]), down_x[-1])
+    down_xc.append(swap_core(down_x[-1]))
+    def flat(*lists):
+        return [piece for step in zip(*lists, strict=True) for piece in step]
+
+    down_pieces = flat(down, down_x, down_c, down_xc)
+    kv_pieces = flat(kv, kv_x, kv_c, kv_xc)
+    normed_nb = row_norm(jnp.concatenate(other, axis=0), input_norm_gain)
+
+    def tied(values, *ready):
+        return lax.optimization_barrier((values, ready))[0]
+
+    down_parts = Pieces(down_pieces, [(i, 0) for i in range(16)], down_pieces[0].shape[0])
+    part_own, down_all = first_ranks(scalars, ids_own, normed_own, down_parts)
+    q[2], part_own = tied((q[2], part_own))
+    q.append(ring(q[2]))
+    part_nb = more_ranks(scalars, ids_nb, normed_nb, down_all, 16)
     back_nb = swap_y(part_own)
     back_own = swap_y(part_nb)
+    back_own, back_nb = tied((back_own, back_nb))
     gains = query_key_gains
-    kv_own = keys_values(scalars, ids_own, gains, normed_own, part_own, back_own, kv_pieces)
-    kv_nb = keys_values(scalars, ids_nb, gains, normed_nb, part_nb, back_nb, kv_pieces)
+    ranks = (part_own, back_own, part_nb, back_nb)
+    kv_all = Pieces(kv_pieces, [(i, 0) for i in range(16)], kv_pieces[0].shape[0])
+    kv_heads = [
+        keys_values(head, scalars, ids_own, ids_nb, gains, ranks, normed_own, normed_nb, kv_all)
+        for head in range(half_k // HEAD_DIM)
+    ]
+    seg_before = halo(seg_pair)
+    q_x = [swap_x(part) for part in q[:3]]
+    kv_heads[0], seg_before, q, q_x = tied((kv_heads[0], seg_before, q, q_x))
+    arriving = [halo(kv_heads[0]), halo(kv_heads[1])]
+    q_x.append(swap_x(q[3]))
+    q, q_x[:3] = tied((q, q_x[:3]), kv_heads[1])
+    q_c = [swap_core(part) for part in q]
+    q_x[3], arriving[0] = tied((q_x[3], arriving[0]))
+    q_xc = [swap_core(part) for part in q_x]
+    q_pieces = flat(q, q_x, q_c, q_xc)
     queries_own, queries_nb = queries_of(
-        scalars,
-        ids_own,
-        ids_nb,
-        gains,
-        normed_own,
-        normed_nb,
-        (part_own, back_own, part_nb, back_nb),
-        q_pieces,
-    )
+        scalars, ids_own, ids_nb, gains, normed_own, normed_nb, ranks, q_pieces
+    )
+    seg_before = jnp.where((place == 0) & (z == 0), -1, seg_before)
+    seg_span = jnp.concatenate([seg_before, seg_pair])
 
     spans = {}
     for name, parity in (("own", y), ("nb", 1 - y)):
@@ -607,17 +700,15 @@
         seg_rows = lax.dynamic_slice_in_dim(seg_pair, parity * rows, rows, 0)[:, None]
         places = jnp.stack([y, 1 - y, 2 + y, 3 - y]) - parity
         spans[name] = (places.astype(jnp.int32), seg_rows, seg_keys)
-    left, right = [], []
-    for head in range(kv_own.shape[0]):
-        blocks = (halo(kv_own[head]), halo(kv_nb[head]), kv_own[head], kv_nb[head])
+    where = jnp.stack([y, place, x, core]).astype(jnp.int32)
+    kept, got = [], []
+    for head, both in enumerate(kv_heads):
+        blocks = (tied(arriving[head], kept[-1]) if kept else arriving[head], both)
         places, seg_rows, seg_keys = spans["nb"]
-        sent = attend(head, places, queries_nb, seg_rows, seg_keys, blocks)
+        got.append(swap_y(attend(head, places, queries_nb, seg_rows, seg_keys, blocks)))
         places, seg_rows, seg_keys = spans["own"]
-        kept = attend(head, places, queries_own, seg_rows, seg_keys, blocks)
-        got = swap_y(sent)
-        left.append(jnp.where(y == 0, kept, got))
-        right.append(jnp.where(y == 0, got, kept))
-    return jnp.concatenate(left + right, axis=1)
+        kept.append(attend(head, places, queries_own, seg_rows, seg_keys, blocks))
+    return side_by_side(where, kept, got)
 
 
 def paired(mesh, shapes):
@@ -625,7 +716,7 @@
     rows = residual[0] // mesh.size
     return (
         mesh.shape["dp"] == 4
-        and mesh.shape["adapter"] % 2 == 0
+        and mesh.shape["adapter"] == 8
         and down[0] // mesh.shape["adapter"] == 4
         and rows % HEAD_DIM == 0
         and 2 * rows == WINDOW

time: 295 us -> 219 us (0.74); the launches traced: 291 us -> 218 us
  waiting for transfers between devices: 156 us -> 87.5 us
  Pallas kernels: 55 us -> 50.6 us
    ppermute x61, waiting for transfers between devices: 156 us -> 87.5 us  [route(): return lax.ppermute(value, ('dp', 'adapter'), pairs)]
    pallas_call x4 -> x5, Pallas kernels: 30.1 us -> 24.5 us  [the longest x2 12.2 us: keys_values(): pl.pallas_call(functools.partial(kv_kernel, pieces, inner, head), out_sha...]
    split x0 -> x1, local copies, waits for them, and re-layouts: none -> 3.19 us  [paired_body(): residual = jnp.split(residual_input, 4, axis=0)]
    unnamed x84 -> x106, local copies, waits for them, and re-layouts: 5.39 us -> 7.15 us
  transfers between devices with their start and end apart: 61 -> 61, of which waited for: 21 -> 24; matrix products, arithmetic and copies ran while one was open for 7% -> 8% of each run, Pallas kernels for 19% -> 21%
where the time goes in v2:
time: 219 us; the launch traced here: 218 us
  waiting for transfers between devices  87.5 us (40%)
  starting transfers between devices  52.2 us (24%)
  Pallas kernels  50.6 us (23%)
  local copies, waits for them, and re-layouts  15.5 us (7%)
  other arithmetic  11.3 us (5%)
    ppermute x61, waiting for transfers between devices, route(): return lax.ppermute(value, ('dp', 'adapter'), pairs)  87.5 us
    ppermute x61, starting transfers between devices, route(): return lax.ppermute(value, ('dp', 'adapter'), pairs)  52.2 us
    pallas_call x1, Pallas kernels, queries_of(): pl.pallas_call(functools.partial(query_kernel, count, inner), out_shape=[...  13.5 us
    pallas_call x4, Pallas kernels, attend(): pl.pallas_call(attend_kernel, grid=(1,), out_shape=jax.ShapeDtypeStruct((...  12.6 us
    pallas_call x2, Pallas kernels, keys_values(): pl.pallas_call(functools.partial(kv_kernel, pieces, inner, head), out_sha...  12.2 us
    pallas_call x1, Pallas kernels, first_ranks(): pl.pallas_call(functools.partial(first_rank_kernel, pieces), out_shape=[j...  7.42 us
    unnamed x106, local copies, waits for them, and re-layouts  7.15 us
  transfers between devices with their start and end apart: 61, of which 24 were waited for; matrix products, arithmetic and copies ran while one was open for 8% of the time, Pallas kernels for 21%

profile of v2, /device:TPU:6, one launch (start us, length us, event | category | flops | bytes accessed | tf_op | source)
XLA Modules:
  0.0 218.1 jit_solution(7271993314002355957)
XLA Ops:
  4.2 5.2 %collective-permute-start.2 = (bf16[320,512]{1,0:T(8,128)(2,1)S(1)}, bf16[320,512]{1,0:T(8,128)(2,1)S(1)}, u32[]{:S(2)}, u32[]{:S(2)}) collective-permute-start(bf16[320,512]{1,0:T(8,128)(2,1)S(1)} %constant_dynamic-slice_fusion), channel_id=1, source_target_pairs={{16,1},{17,0},{18,3},{19,2},{20,5},{21,4},{22,7},{23,6},{24,9},{25... | collective-permute-start | bytes 983048 | tf_op jit(solution)/shard_map/ppermute | solution.py:184
  15.8 3.1 %collective-permute-done.3 = bf16[16,2048]{1,0:T(8,128)(2,1)S(1)} collective-permute-done((bf16[16,2048]{1,0:T(8,128)(2,1)S(1)}, bf16[16,2048]{1,0:T(8,128)(2,1)S(1)}, u32[]{:S(2)}, u32[]{:S(2)}) %collective-permute-start.3) | collective-permute-done | bytes 65568 | tf_op jit(solution)/shard_map/ppermute | solution.py:184
  22.1 3.2 %fusion.14 = (bf16[128,2560]{1,0:T(8,128)(2,1)}, bf16[128,2560]{1,0:T(8,128)(2,1)}, bf16[128,2560]{1,0:T(8,128)(2,1)}, bf16[128,2560]{1,0:T(8,128)(2,1)}) fusion(bf16[512,2560]{1,0:T(8,128)(2,1)} %param.11), kind=kLoop, calls=%fused_computation.63 | loop fusion | bytes 5242880 | tf_op jit(solution)/shard_map/split | solution.py:614
  30.6 3.6 %collective-permute-done.12.refs_14_ = bf16[384,512]{1,0:T(8,128)(2,1)S(1)} collective-permute-done((bf16[384,512]{1,0:T(8,128)(2,1)S(1)}, bf16[384,512]{1,0:T(8,128)(2,1)S(1)}, u32[]{:S(2)}, u32[]{:S(2)}) %collective-permute-start.12) | collective-permute-done | bytes 393248 | tf_op jit(solution)/shard_map/ppermute | solution.py:184
  36.1 3.0 %collective-permute-done.13.refs_11_ = bf16[384,512]{1,0:T(8,128)(2,1)S(1)} collective-permute-done((bf16[384,512]{1,0:T(8,128)(2,1)S(1)}, bf16[384,512]{1,0:T(8,128)(2,1)S(1)}, u32[]{:S(2)}, u32[]{:S(2)}) %collective-permute-start.13) | collective-permute-done | bytes 393248 | tf_op jit(solution)/shard_map/ppermute | solution.py:184
  46.0 2.3 %fusion = f32[512]{0:T(512)S(1)} fusion(bf16[512,2560]{1,0:T(8,128)(2,1)} %param.11), kind=kLoop, calls=%fused_computation.4 | loop fusion | flops 3931648 | bytes 2623488 | tf_op jit(solution)/shard_map/reduce_sum | solution.py:193
  48.3 4.4 %collective-permute-done.20.refs_18_ = bf16[384,512]{1,0:T(8,128)(2,1)S(1)} collective-permute-done((bf16[384,512]{1,0:T(8,128)(2,1)S(1)}, bf16[384,512]{1,0:T(8,128)(2,1)S(1)}, u32[]{:S(2)}, u32[]{:S(2)}) %collective-permute-start.20) | collective-permute-done | bytes 393248 | tf_op jit(solution)/shard_map/ppermute | solution.py:184
  63.6 3.0 %collective-permute-done.26.refs_22_ = bf16[384,512]{1,0:T(8,128)(2,1)} collective-permute-done((bf16[384,512]{1,0:T(8,128)(2,1)S(1)}, bf16[384,512]{1,0:T(8,128)(2,1)}, u32[]{:S(2)}, u32[]{:S(2)}) %collective-permute-start.26) | collective-permute-done | bytes 393248 | tf_op jit(solution)/shard_map/ppermute | solution.py:184
  69.2 2.2 %collective-permute-done.17.refs_12_ = bf16[48,2560]{1,0:T(8,128)(2,1)} collective-permute-done((bf16[48,2560]{1,0:T(8,128)(2,1)S(1)}, bf16[48,2560]{1,0:T(8,128)(2,1)}, u32[]{:S(2)}, u32[]{:S(2)}) %collective-permute-start.17) | collective-permute-done | bytes 245792 | tf_op jit(solution)/shard_map/ppermute | solution.py:184
  75.8 7.0 %collective-permute-done.16.refs_14_ = bf16[192,1024]{1,0:T(8,128)(2,1)} collective-permute-done((bf16[192,1024]{1,0:T(8,128)(2,1)}, bf16[192,1024]{1,0:T(8,128)(2,1)}, u32[]{:S(2)}, u32[]{:S(2)}) %collective-permute-start.16) | collective-permute-done | bytes 393248 | tf_op jit(solution)/shard_map/ppermute | solution.py:184
  84.2 6.4 %collective-permute-done.24.refs_13_ = bf16[48,2560]{1,0:T(8,128)(2,1)} collective-permute-done((bf16[48,2560]{1,0:T(8,128)(2,1)}, bf16[48,2560]{1,0:T(8,128)(2,1)}, u32[]{:S(2)}, u32[]{:S(2)}) %collective-permute-start.24) | collective-permute-done | bytes 245792 | tf_op jit(solution)/shard_map/ppermute | solution.py:184
  94.9 2.6 %fusion.5 = (bf16[512,2560]{1,0:T(8,128)(2,1)S(1)}, bf16[512,2560]{1,0:T(8,128)(2,1)S(1)}) fusion(f32[512]{0:T(512)S(1)} %add_rsqrt_fusion, f32[2560]{0:T(1024)S(1)} %copy-done.48, bf16[128,2560]{1,0:T(8,128)(2,1)} %collective-permute-done.29, bf16[128,2560]{1,0:T(8,128)(2,1)} %copy-done.39, bf16[128,2560]{1,0:T(8,128)(2,1)} %collective-permute-done.15, ...), kind=kLoop, calls=%fused_computation.9 | loop fusion | flops 19660800 | bytes 10500096 | tf_op jit(solution)/shard_map/convert_element_type | solution.py:194
  97.6 7.4 %shard_map.109 = (bf16[48,512]{1,0:T(8,128)(2,1)S(1)}, bf16[768,2560]{1,0:T(8,128)(2,1)S(1)}) custom-call(s32[6,16]{1,0:T(8,128)S(1)} %stack.75.scalars.refs_0_, s32[1,512]{1,0:T(1,128)S(1)} %bitcast.41, bf16[512,2560]{1,0:T(8,128)(2,1)S(1)} %get-tuple-element.143.normed.refs_8_.refs_4_, bf16[48,2560]{1,0:T(8,128)(2,1)S(1)} %dynamic-slice_bitcast_fusion.refs_0_, ...), custom_call_target="tpu_custom_call" | custom-call | flops 1 | bytes 1 | tf_op jit(solution)/shard_map/pallas_call | solution.py:240
  105.1 2.3 %collective-permute-done.30.refs_18_ = bf16[192,1024]{1,0:T(8,128)(2,1)S(1)} collective-permute-done((bf16[192,1024]{1,0:T(8,128)(2,1)}, bf16[192,1024]{1,0:T(8,128)(2,1)S(1)}, u32[]{:S(2)}, u32[]{:S(2)}) %collective-permute-start.30) | collective-permute-done | bytes 393248 | tf_op jit(solution)/shard_map/ppermute | solution.py:184
  110.7 2.8 %shard_map.110.refs_6_.refs_8_ = bf16[48,512]{1,0:T(8,128)(2,1)S(1)} custom-call(s32[6,16]{1,0:T(8,128)S(1)} %stack.75.scalars.refs_0_, s32[1,512]{1,0:T(1,128)S(1)} %get-tuple-element.149.ids.refs_2_, bf16[512,2560]{1,0:T(8,128)(2,1)S(1)} %get-tuple-element.142.normed.refs_9_.refs_5_, bf16[768,2560]{1,0:T(8,128)(2,1)S(1)} %get-tuple-element.92.down), custom_call_target="tpu_custom_call" | custom-call | flops 1 | bytes 1 | tf_op jit(solution)/shard_map/pallas_call | solution.py:256
  113.9 3.8 %collective-permute-done.35.refs_5_.refs_7_ = bf16[48,512]{1,0:T(8,128)(2,1)S(1)} collective-permute-done((bf16[48,512]{1,0:T(8,128)(2,1)S(1)}, bf16[48,512]{1,0:T(8,128)(2,1)S(1)}, u32[]{:S(2)}, u32[]{:S(2)}) %collective-permute-start.35) | collective-permute-done | bytes 49184 | tf_op jit(solution)/shard_map/ppermute | solution.py:184
  118.0 3.8 %collective-permute-done.36.refs_7_.refs_9_ = bf16[48,512]{1,0:T(8,128)(2,1)S(1)} collective-permute-done((bf16[48,512]{1,0:T(8,128)(2,1)S(1)}, bf16[48,512]{1,0:T(8,128)(2,1)S(1)}, u32[]{:S(2)}, u32[]{:S(2)}) %collective-permute-start.36) | collective-permute-done | bytes 49184 | tf_op jit(solution)/shard_map/ppermute | solution.py:184
  121.8 2.6 %collective-permute-start.43 = (s32[1024]{0:T(1024)S(1)}, s32[1024]{0:T(1024)S(1)}, u32[]{:S(2)}, u32[]{:S(2)}) collective-permute-start(s32[1024]{0:T(1024)S(1)} %add_select_fusion), channel_id=1, source_target_pairs={{0,2},{1,3},{2,4},{3,5},{4,6},{5,7},{6,8},{7,9},{8,10},{9,11},{10,... | collective-permute-start | bytes 12296 | tf_op jit(solution)/shard_map/ppermute | solution.py:184
  124.4 6.1 %shard_map.111.refs_1_ = bf16[2,512,512]{2,1,0:T(8,128)(2,1)S(1)} custom-call(s32[6,16]{1,0:T(8,128)S(1)} %stack.75.scalars.refs_0_, s32[1,512]{1,0:T(1,128)S(1)} %bitcast.42, s32[1,512]{1,0:T(1,128)S(1)} %get-tuple-element.149.ids.refs_2_, f32[2,256]{1,0:T(2,128)S(1)} %copy-done.37, bf16[48,512]{1,0:T(8,128)(2,1)S(1)} %get-tuple-element.91.refs_4_.refs_6_, ...), custom_call_target="tpu_custom_call" | custom-call | flops 1 | bytes 1 | tf_op jit(solution)/shard_map/pallas_call | solution.py:344
  130.6 4.6 %collective-permute-done.47.refs_19_ = bf16[192,1024]{1,0:T(8,128)(2,1)S(1)} collective-permute-done((bf16[192,1024]{1,0:T(8,128)(2,1)S(1)}, bf16[192,1024]{1,0:T(8,128)(2,1)S(1)}, u32[]{:S(2)}, u32[]{:S(2)}) %collective-permute-start.47) | collective-permute-done | bytes 393248 | tf_op jit(solution)/shard_map/ppermute | solution.py:184
  135.2 2.2 %collective-permute-start.55 = (bf16[2,512,512]{2,1,0:T(8,128)(2,1)S(1)}, bf16[2,512,512]{2,1,0:T(8,128)(2,1)S(1)}, u32[]{:S(2)}, u32[]{:S(2)}) collective-permute-start(bf16[2,512,512]{2,1,0:T(8,128)(2,1)S(1)} %shard_map.111.refs_1_), channel_id=1, source_target_pairs={{0,2},{1,3},{2,4},{3,5},{4,6},{5,7},{6,8},{7,9},{8,10},{9,11},{10,... | collective-permute-start | bytes 3145736 | tf_op jit(solution)/shard_map/ppermute | solution.py:184
  140.5 6.1 %shard_map.112.refs_1_ = bf16[2,512,512]{2,1,0:T(8,128)(2,1)S(1)} custom-call(s32[6,16]{1,0:T(8,128)S(1)} %stack.75.scalars.refs_0_, s32[1,512]{1,0:T(1,128)S(1)} %bitcast.43, s32[1,512]{1,0:T(1,128)S(1)} %get-tuple-element.149.ids.refs_2_, f32[2,256]{1,0:T(2,128)S(1)} %copy-done.37, bf16[48,512]{1,0:T(8,128)(2,1)S(1)} %get-tuple-element.91.refs_4_.refs_6_, ...), custom_call_target="tpu_custom_call" | custom-call | flops 1 | bytes 1 | tf_op jit(solution)/shard_map/pallas_call | solution.py:344
  146.6 2.6 %collective-permute-start.58 = (bf16[2,512,512]{2,1,0:T(8,128)(2,1)S(1)}, bf16[2,512,512]{2,1,0:T(8,128)(2,1)}, u32[]{:S(2)}, u32[]{:S(2)}) collective-permute-start(bf16[2,512,512]{2,1,0:T(8,128)(2,1)S(1)} %shard_map.112.refs_1_), channel_id=1, source_target_pairs={{0,2},{1,3},{2,4},{3,5},{4,6},{5,7},{6,8},{7,9},{8,10},{9,11},{10,... | collective-permute-start | bytes 3145736 | tf_op jit(solution)/shard_map/ppermute | solution.py:184
  149.8 3.0 %collective-permute-done.54.refs_23_ = bf16[192,1024]{1,0:T(8,128)(2,1)S(1)} collective-permute-done((bf16[192,1024]{1,0:T(8,128)(2,1)S(1)}, bf16[192,1024]{1,0:T(8,128)(2,1)S(1)}, u32[]{:S(2)}, u32[]{:S(2)}) %collective-permute-start.54) | collective-permute-done | bytes 393248 | tf_op jit(solution)/shard_map/ppermute | solution.py:184
  152.8 12.5 %collective-permute-done.55.refs_0_ = bf16[2,512,512]{2,1,0:T(8,128)(2,1)S(1)} collective-permute-done((bf16[2,512,512]{2,1,0:T(8,128)(2,1)S(1)}, bf16[2,512,512]{2,1,0:T(8,128)(2,1)S(1)}, u32[]{:S(2)}, u32[]{:S(2)}) %collective-permute-start.55) | collective-permute-done | bytes 1048608 | tf_op jit(solution)/shard_map/ppermute | solution.py:184
  170.7 13.5 %shard_map.113 = (bf16[512,1024]{1,0:T(8,128)(2,1)}, bf16[512,1024]{1,0:T(8,128)(2,1)}) custom-call(s32[6,16]{1,0:T(8,128)} %copy-done.34, s32[1,512]{1,0:T(1,128)} %bitcast.40, s32[1,512]{1,0:T(1,128)} %copy-done.36, f32[2,256]{1,0:T(2,128)} %refs_3_.5, bf16[512,2560]{1,0:T(8,128)(2,1)} %copy-done.2, bf16[512,2560]{1,0:T(8,128)(2,1)} %copy-done.1, ...), custom_call_target="tpu_custom_call" | custom-call | flops 1 | bytes 1 | tf_op jit(solution)/shard_map/pallas_call | solution.py:398
  185.4 2.7 %shard_map.114.refs_0_ = bf16[512,512]{1,0:T(8,128)(2,1)S(1)} custom-call(s32[4]{0:T(128)S(1)} %broadcast_subtract_fusion.1.places, bf16[512,1024]{1,0:T(8,128)(2,1)S(1)} %copy-done.5, s32[512,1]{1,0:T(8,128)S(1)} %copy.12.seg_rows, s32[1,1536]{1,0:T(1,128)S(1)} %broadcast_in_dim.32.seg_keys, bf16[2,512,512]{2,1,0:T(8,128)(2,1)S(1)} %copy-done.4, ...), custom_call_target="tpu_custom_call" | custom-call | flops 1 | bytes 1 | tf_op jit(solution)/shard_map/pallas_call | solution.py:477
  188.1 2.7 %shard_map.116 = bf16[512,512]{1,0:T(8,128)(2,1)S(1)} custom-call(s32[4]{0:T(128)S(1)} %get-tuple-element.123.places, bf16[512,1024]{1,0:T(8,128)(2,1)S(1)} %copy-done.7, s32[512,1]{1,0:T(8,128)S(1)} %copy-done.8, s32[1,1536]{1,0:T(1,128)S(1)} %broadcast_in_dim.34.seg_keys, bf16[2,512,512]{2,1,0:T(8,128)(2,1)S(1)} %copy-done.4, ...), custom_call_target="tpu_custom_call" | custom-call | flops 1 | bytes 1 | tf_op jit(solution)/shard_map/pallas_call | solution.py:477
  191.1 3.7 %shard_map.117 = bf16[512,512]{1,0:T(8,128)(2,1)S(1)} custom-call(s32[4]{0:T(128)S(1)} %get-tuple-element.123.places, bf16[512,1024]{1,0:T(8,128)(2,1)S(1)} %copy-done.7, s32[512,1]{1,0:T(8,128)S(1)} %copy-done.8, s32[1,1536]{1,0:T(1,128)S(1)} %broadcast_in_dim.34.seg_keys, bf16[2,512,512]{2,1,0:T(8,128)(2,1)} %collective-permute-done.58.refs_0_, ...), custom_call_target="tpu_custom_call" | custom-call | flops 1 | bytes 1 | tf_op jit(solution)/shard_map/pallas_call | solution.py:477
  196.6 3.6 %shard_map.115.refs_1_ = bf16[512,512]{1,0:T(8,128)(2,1)S(1)} custom-call(s32[4]{0:T(128)S(1)} %broadcast_subtract_fusion.1.places, bf16[512,1024]{1,0:T(8,128)(2,1)S(1)} %copy-done.6, s32[512,1]{1,0:T(8,128)S(1)} %copy.12.seg_rows, s32[1,1536]{1,0:T(1,128)S(1)} %broadcast_in_dim.32.seg_keys, bf16[2,512,512]{2,1,0:T(8,128)(2,1)} %collective-permute-done.58.refs_0_, ...), custom_call_target="tpu_custom_call" | custom-call | flops 1 | bytes 1 | tf_op jit(solution)/shard_map/pallas_call | solution.py:477
  200.2 5.5 %collective-permute-done.59.refs_2_ = bf16[512,512]{1,0:T(8,128)(2,1)S(1)} collective-permute-done((bf16[512,512]{1,0:T(8,128)(2,1)S(1)}, bf16[512,512]{1,0:T(8,128)(2,1)S(1)}, u32[]{:S(2)}, u32[]{:S(2)}) %collective-permute-start.59) | collective-permute-done | bytes 524320 | tf_op jit(solution)/shard_map/ppermute | solution.py:184
  205.6 10.4 %collective-permute-done.60.refs_3_ = bf16[512,512]{1,0:T(8,128)(2,1)S(1)} collective-permute-done((bf16[512,512]{1,0:T(8,128)(2,1)S(1)}, bf16[512,512]{1,0:T(8,128)(2,1)S(1)}, u32[]{:S(2)}, u32[]{:S(2)}) %collective-permute-start.60) | collective-permute-done | bytes 524320 | tf_op jit(solution)/shard_map/ppermute | solution.py:184
  (242 shorter events, 69.1 us)
Async XLA Ops:
  1.2 19.6 %collective-permute-start = (bf16[160,1024]{1,0:T(8,128)(2,1)S(1)}, bf16[160,1024]{1,0:T(8,128)(2,1)S(1)}, u32[]{:S(2)}, u32[]{:S(2)}) collective-permute-start(bf16[160,1024]{1,0:T(8,128)(2,1)S(1)} %get-tuple-element.133), channel_id=1, source_target_pairs={{1,8},{3,10},{5,12},{7,14},{8,1},{10,3},{12,5},{14,7}} | collective-permute-start | bytes 983048 | tf_op jit(solution)/shard_map/ppermute | solution.py:184
  1.9 18.9 %collective-permute-start.1 = (bf16[160,1024]{1,0:T(8,128)(2,1)S(1)}, bf16[160,1024]{1,0:T(8,128)(2,1)}, u32[]{:S(2)}, u32[]{:S(2)}) collective-permute-start(bf16[160,1024]{1,0:T(8,128)(2,1)S(1)} %get-tuple-element.132), channel_id=1, source_target_pairs={{0,16},{1,24},{2,18},{3,26},{4,20},{5,28},{6,22},{7,30},{8,17},{9,... | collective-permute-start | bytes 983048 | tf_op jit(solution)/shard_map/ppermute | solution.py:184
  4.2 16.6 %collective-permute-start.2 = (bf16[320,512]{1,0:T(8,128)(2,1)S(1)}, bf16[320,512]{1,0:T(8,128)(2,1)S(1)}, u32[]{:S(2)}, u32[]{:S(2)}) collective-permute-start(bf16[320,512]{1,0:T(8,128)(2,1)S(1)} %constant_dynamic-slice_fusion), channel_id=1, source_target_pairs={{16,1},{17,0},{18,3},{19,2},{20,5},{21,4},{22,7},{23,6},{24,9},{25... | collective-permute-start | bytes 983048 | tf_op jit(solution)/shard_map/ppermute | solution.py:184
  22.1 12.1 %collective-permute-start.12 = (bf16[384,512]{1,0:T(8,128)(2,1)S(1)}, bf16[384,512]{1,0:T(8,128)(2,1)S(1)}, u32[]{:S(2)}, u32[]{:S(2)}) collective-permute-start(bf16[384,512]{1,0:T(8,128)(2,1)S(1)} %fusion.6.refs_10_), channel_id=1, source_target_pairs={{0,2},{1,3},{2,4},{3,5},{4,6},{5,7},{6,0},{7,1},{8,10},{9,11},{10,... | collective-permute-start | bytes 1179656 | tf_op jit(solution)/shard_map/ppermute | solution.py:184
  25.3 19.3 %collective-permute-start.9 = (bf16[128,2560]{1,0:T(8,128)(2,1)}, bf16[128,2560]{1,0:T(8,128)(2,1)}, u32[]{:S(2)}, u32[]{:S(2)}) collective-permute-start(bf16[128,2560]{1,0:T(8,128)(2,1)} %get-tuple-element.130), channel_id=1, source_target_pairs={{0,1},{1,0},{2,3},{3,2},{4,5},{5,4},{6,7},{7,6},{8,9},{9,8},{10,11... | collective-permute-start | bytes 1966088 | tf_op jit(solution)/shard_map/ppermute | solution.py:184
  27.0 12.0 %collective-permute-start.13 = (bf16[384,512]{1,0:T(8,128)(2,1)S(1)}, bf16[384,512]{1,0:T(8,128)(2,1)S(1)}, u32[]{:S(2)}, u32[]{:S(2)}) collective-permute-start(bf16[384,512]{1,0:T(8,128)(2,1)S(1)} %fusion.6.refs_10_), channel_id=1, source_target_pairs={{0,16},{1,17},{2,18},{3,19},{4,20},{5,21},{6,22},{7,23},{8,24},{9,... | collective-permute-start | bytes 1179656 | tf_op jit(solution)/shard_map/ppermute | solution.py:184
  39.1 13.6 %collective-permute-start.20 = (bf16[384,512]{1,0:T(8,128)(2,1)S(1)}, bf16[384,512]{1,0:T(8,128)(2,1)S(1)}, u32[]{:S(2)}, u32[]{:S(2)}) collective-permute-start(bf16[384,512]{1,0:T(8,128)(2,1)S(1)} %collective-permute-done.12.refs_14_), channel_id=1, source_target_pairs={{0,2},{1,3},{2,4},{3,5},{4,6},{5,7},{6,0},{7,1},{8,10},{9,11},{10,... | collective-permute-start | bytes 1179656 | tf_op jit(solution)/shard_map/ppermute | solution.py:184
  40.6 12.1 %collective-permute-start.21 = (bf16[384,512]{1,0:T(8,128)(2,1)S(1)}, bf16[384,512]{1,0:T(8,128)(2,1)}, u32[]{:S(2)}, u32[]{:S(2)}) collective-permute-start(bf16[384,512]{1,0:T(8,128)(2,1)S(1)} %collective-permute-done.12.refs_14_), channel_id=1, source_target_pairs={{0,16},{1,17},{2,18},{3,19},{4,20},{5,21},{6,22},{7,23},{8,24},{9,... | collective-permute-start | bytes 1179656 | tf_op jit(solution)/shard_map/ppermute | solution.py:184
  43.8 17.5 %collective-permute-start.15 = (bf16[128,2560]{1,0:T(8,128)(2,1)}, bf16[128,2560]{1,0:T(8,128)(2,1)}, u32[]{:S(2)}, u32[]{:S(2)}) collective-permute-start(bf16[128,2560]{1,0:T(8,128)(2,1)} %get-tuple-element.74), channel_id=1, source_target_pairs={{0,1},{1,0},{2,3},{3,2},{4,5},{5,4},{6,7},{7,6},{8,9},{9,8},{10,11... | collective-permute-start | bytes 1966088 | tf_op jit(solution)/shard_map/ppermute | solution.py:184
  44.7 13.2 %collective-permute-start.10 = (bf16[48,2560]{1,0:T(8,128)(2,1)S(1)}, bf16[48,2560]{1,0:T(8,128)(2,1)S(1)}, u32[]{:S(2)}, u32[]{:S(2)}) collective-permute-start(bf16[48,2560]{1,0:T(8,128)(2,1)S(1)} %collective-permute-done.5.refs_4_), channel_id=1, source_target_pairs={{0,16},{1,17},{2,18},{3,19},{4,20},{5,21},{6,22},{7,23},{8,24},{9,... | collective-permute-start | bytes 737288 | tf_op jit(solution)/shard_map/ppermute | solution.py:184
  52.7 13.9 %collective-permute-start.26 = (bf16[384,512]{1,0:T(8,128)(2,1)S(1)}, bf16[384,512]{1,0:T(8,128)(2,1)}, u32[]{:S(2)}, u32[]{:S(2)}) collective-permute-start(bf16[384,512]{1,0:T(8,128)(2,1)S(1)} %collective-permute-done.20.refs_18_), channel_id=1, source_target_pairs={{0,2},{1,3},{2,4},{3,5},{4,6},{5,7},{6,0},{7,1},{8,10},{9,11},{10,... | collective-permute-start | bytes 1179656 | tf_op jit(solution)/shard_map/ppermute | solution.py:184
  54.3 14.1 %collective-permute-start.27 = (bf16[384,512]{1,0:T(8,128)(2,1)S(1)}, bf16[384,512]{1,0:T(8,128)(2,1)}, u32[]{:S(2)}, u32[]{:S(2)}) collective-permute-start(bf16[384,512]{1,0:T(8,128)(2,1)S(1)} %collective-permute-done.20.refs_18_), channel_id=1, source_target_pairs={{0,16},{1,17},{2,18},{3,19},{4,20},{5,21},{6,22},{7,23},{8,24},{9,... | collective-permute-start | bytes 1179656 | tf_op jit(solution)/shard_map/ppermute | solution.py:184
  59.2 23.6 %collective-permute-start.23 = (bf16[128,2560]{1,0:T(8,128)(2,1)S(1)}, bf16[128,2560]{1,0:T(8,128)(2,1)S(1)}, u32[]{:S(2)}, u32[]{:S(2)}) collective-permute-start(bf16[128,2560]{1,0:T(8,128)(2,1)S(1)} %copy-done.42), channel_id=1, source_target_pairs={{0,1},{1,0},{2,3},{3,2},{4,5},{5,4},{6,7},{7,6},{8,9},{9,8},{10,11... | collective-permute-start | bytes 1966088 | tf_op jit(solution)/shard_map/ppermute | solution.py:184
  69.1 13.6 %collective-permute-start.16 = (bf16[192,1024]{1,0:T(8,128)(2,1)}, bf16[192,1024]{1,0:T(8,128)(2,1)}, u32[]{:S(2)}, u32[]{:S(2)}) collective-permute-start(bf16[192,1024]{1,0:T(8,128)(2,1)} %pad_maximum_fusion.2.refs_10_), channel_id=1, source_target_pairs={{0,2},{1,3},{2,4},{3,5},{4,6},{5,7},{6,0},{7,1},{8,10},{9,11},{10,... | collective-permute-start | bytes 1179656 | tf_op jit(solution)/shard_map/ppermute | solution.py:184
  71.4 19.8 %collective-permute-start.29 = (bf16[128,2560]{1,0:T(8,128)(2,1)}, bf16[128,2560]{1,0:T(8,128)(2,1)}, u32[]{:S(2)}, u32[]{:S(2)}) collective-permute-start(bf16[128,2560]{1,0:T(8,128)(2,1)} %get-tuple-element.83), channel_id=1, source_target_pairs={{0,1},{1,0},{2,3},{3,2},{4,5},{5,4},{6,7},{7,6},{8,9},{9,8},{10,11... | collective-permute-start | bytes 1966088 | tf_op jit(solution)/shard_map/ppermute | solution.py:184
  83.8 24.8 %collective-permute-start.37 = (bf16[384,512]{1,0:T(8,128)(2,1)S(1)}, bf16[384,512]{1,0:T(8,128)(2,1)S(1)}, u32[]{:S(2)}, u32[]{:S(2)}) collective-permute-start(bf16[384,512]{1,0:T(8,128)(2,1)S(1)} %collective-permute-done.13.refs_11_), channel_id=1, source_target_pairs={{0,8},{1,9},{2,10},{3,11},{4,12},{5,13},{6,14},{7,15},{8,0},{9,1},... | collective-permute-start | bytes 1179656 | tf_op jit(solution)/shard_map/ppermute | solution.py:184
  93.4 16.1 %collective-permute-start.38 = (bf16[384,512]{1,0:T(8,128)(2,1)}, bf16[384,512]{1,0:T(8,128)(2,1)S(1)}, u32[]{:S(2)}, u32[]{:S(2)}) collective-permute-start(bf16[384,512]{1,0:T(8,128)(2,1)} %collective-permute-done.21.refs_15_), channel_id=1, source_target_pairs={{0,8},{1,9},{2,10},{3,11},{4,12},{5,13},{6,14},{7,15},{8,0},{9,1},... | collective-permute-start | bytes 1179656 | tf_op jit(solution)/shard_map/ppermute | solution.py:184
  93.9 15.6 %collective-permute-start.39 = (bf16[384,512]{1,0:T(8,128)(2,1)}, bf16[384,512]{1,0:T(8,128)(2,1)S(1)}, u32[]{:S(2)}, u32[]{:S(2)}) collective-permute-start(bf16[384,512]{1,0:T(8,128)(2,1)} %collective-permute-done.27.refs_19_), channel_id=1, source_target_pairs={{0,8},{1,9},{2,10},{3,11},{4,12},{5,13},{6,14},{7,15},{8,0},{9,1},... | collective-permute-start | bytes 1179656 | tf_op jit(solution)/shard_map/ppermute | solution.py:184
  94.0 13.5 %collective-permute-start.30 = (bf16[192,1024]{1,0:T(8,128)(2,1)}, bf16[192,1024]{1,0:T(8,128)(2,1)S(1)}, u32[]{:S(2)}, u32[]{:S(2)}) collective-permute-start(bf16[192,1024]{1,0:T(8,128)(2,1)} %collective-permute-done.16.refs_14_), channel_id=1, source_target_pairs={{0,2},{1,3},{2,4},{3,5},{4,6},{5,7},{6,0},{7,1},{8,10},{9,11},{10,... | collective-permute-start | bytes 1179656 | tf_op jit(solution)/shard_map/ppermute | solution.py:184
  94.7 18.8 %collective-permute-start.42 = (bf16[384,512]{1,0:T(8,128)(2,1)}, bf16[384,512]{1,0:T(8,128)(2,1)S(1)}, u32[]{:S(2)}, u32[]{:S(2)}) collective-permute-start(bf16[384,512]{1,0:T(8,128)(2,1)} %collective-permute-done.40.refs_23_), channel_id=1, source_target_pairs={{0,8},{1,9},{2,10},{3,11},{4,12},{5,13},{6,14},{7,15},{8,0},{9,1},... | collective-permute-start | bytes 1179656 | tf_op jit(solution)/shard_map/ppermute | solution.py:184
  107.4 23.1 %collective-permute-start.46 = (bf16[192,1024]{1,0:T(8,128)(2,1)}, bf16[192,1024]{1,0:T(8,128)(2,1)}, u32[]{:S(2)}, u32[]{:S(2)}) collective-permute-start(bf16[192,1024]{1,0:T(8,128)(2,1)} %collective-permute-done.16.refs_14_), channel_id=1, source_target_pairs={{0,16},{1,17},{2,18},{3,19},{4,20},{5,21},{6,22},{7,23},{8,24},{9,... | collective-permute-start | bytes 1179656 | tf_op jit(solution)/shard_map/ppermute | solution.py:184
  108.6 22.0 %collective-permute-start.45 = (bf16[192,1024]{1,0:T(8,128)(2,1)}, bf16[192,1024]{1,0:T(8,128)(2,1)}, u32[]{:S(2)}, u32[]{:S(2)}) collective-permute-start(bf16[192,1024]{1,0:T(8,128)(2,1)} %pad_maximum_fusion.2.refs_10_), channel_id=1, source_target_pairs={{0,16},{1,17},{2,18},{3,19},{4,20},{5,21},{6,22},{7,23},{8,24},{9,... | collective-permute-start | bytes 1179656 | tf_op jit(solution)/shard_map/ppermute | solution.py:184
  109.5 21.1 %collective-permute-start.44 = (bf16[192,1024]{1,0:T(8,128)(2,1)S(1)}, bf16[192,1024]{1,0:T(8,128)(2,1)S(1)}, u32[]{:S(2)}, u32[]{:S(2)}) collective-permute-start(bf16[192,1024]{1,0:T(8,128)(2,1)S(1)} %collective-permute-done.30.refs_18_), channel_id=1, source_target_pairs={{0,2},{1,3},{2,4},{3,5},{4,6},{5,7},{6,0},{7,1},{8,10},{9,11},{10,... | collective-permute-start | bytes 1179656 | tf_op jit(solution)/shard_map/ppermute | solution.py:184
  109.5 25.7 %collective-permute-start.47 = (bf16[192,1024]{1,0:T(8,128)(2,1)S(1)}, bf16[192,1024]{1,0:T(8,128)(2,1)S(1)}, u32[]{:S(2)}, u32[]{:S(2)}) collective-permute-start(bf16[192,1024]{1,0:T(8,128)(2,1)S(1)} %collective-permute-done.30.refs_18_), channel_id=1, source_target_pairs={{0,16},{1,17},{2,18},{3,19},{4,20},{5,21},{6,22},{7,23},{8,24},{9,... | collective-permute-start | bytes 1179656 | tf_op jit(solution)/shard_map/ppermute | solution.py:184
  135.2 30.1 %collective-permute-start.55 = (bf16[2,512,512]{2,1,0:T(8,128)(2,1)S(1)}, bf16[2,512,512]{2,1,0:T(8,128)(2,1)S(1)}, u32[]{:S(2)}, u32[]{:S(2)}) collective-permute-start(bf16[2,512,512]{2,1,0:T(8,128)(2,1)S(1)} %shard_map.111.refs_1_), channel_id=1, source_target_pairs={{0,2},{1,3},{2,4},{3,5},{4,6},{5,7},{6,8},{7,9},{8,10},{9,11},{10,... | collective-permute-start | bytes 3145736 | tf_op jit(solution)/shard_map/ppermute | solution.py:184
  137.5 15.3 %collective-permute-start.54 = (bf16[192,1024]{1,0:T(8,128)(2,1)S(1)}, bf16[192,1024]{1,0:T(8,128)(2,1)S(1)}, u32[]{:S(2)}, u32[]{:S(2)}) collective-permute-start(bf16[192,1024]{1,0:T(8,128)(2,1)S(1)} %collective-permute-done.44.refs_22_), channel_id=1, source_target_pairs={{0,16},{1,17},{2,18},{3,19},{4,20},{5,21},{6,22},{7,23},{8,24},{9,... | collective-permute-start | bytes 1179656 | tf_op jit(solution)/shard_map/ppermute | solution.py:184
  146.6 41.5 %collective-permute-start.58 = (bf16[2,512,512]{2,1,0:T(8,128)(2,1)S(1)}, bf16[2,512,512]{2,1,0:T(8,128)(2,1)}, u32[]{:S(2)}, u32[]{:S(2)}) collective-permute-start(bf16[2,512,512]{2,1,0:T(8,128)(2,1)S(1)} %shard_map.112.refs_1_), channel_id=1, source_target_pairs={{0,2},{1,3},{2,4},{3,5},{4,6},{5,7},{6,8},{7,9},{8,10},{9,11},{10,... | collective-permute-start | bytes 3145736 | tf_op jit(solution)/shard_map/ppermute | solution.py:184
  149.2 17.3 %collective-permute-start.48 = (bf16[192,1024]{1,0:T(8,128)(2,1)}, bf16[192,1024]{1,0:T(8,128)(2,1)}, u32[]{:S(2)}, u32[]{:S(2)}) collective-permute-start(bf16[192,1024]{1,0:T(8,128)(2,1)} %pad_maximum_fusion.2.refs_10_), channel_id=1, source_target_pairs={{0,8},{1,9},{2,10},{3,11},{4,12},{5,13},{6,14},{7,15},{8,0},{9,1},... | collective-permute-start | bytes 1179656 | tf_op jit(solution)/shard_map/ppermute | solution.py:184
  149.3 17.8 %collective-permute-start.49 = (bf16[192,1024]{1,0:T(8,128)(2,1)}, bf16[192,1024]{1,0:T(8,128)(2,1)}, u32[]{:S(2)}, u32[]{:S(2)}) collective-permute-start(bf16[192,1024]{1,0:T(8,128)(2,1)} %collective-permute-done.45.refs_11_), channel_id=1, source_target_pairs={{0,8},{1,9},{2,10},{3,11},{4,12},{5,13},{6,14},{7,15},{8,0},{9,1},... | collective-permute-start | bytes 1179656 | tf_op jit(solution)/shard_map/ppermute | solution.py:184
  152.8 14.3 %collective-permute-start.50 = (bf16[192,1024]{1,0:T(8,128)(2,1)}, bf16[192,1024]{1,0:T(8,128)(2,1)}, u32[]{:S(2)}, u32[]{:S(2)}) collective-permute-start(bf16[192,1024]{1,0:T(8,128)(2,1)} %collective-permute-done.16.refs_14_), channel_id=1, source_target_pairs={{0,8},{1,9},{2,10},{3,11},{4,12},{5,13},{6,14},{7,15},{8,0},{9,1},... | collective-permute-start | bytes 1179656 | tf_op jit(solution)/shard_map/ppermute | solution.py:184
  190.8 14.8 %collective-permute-start.59 = (bf16[512,512]{1,0:T(8,128)(2,1)S(1)}, bf16[512,512]{1,0:T(8,128)(2,1)S(1)}, u32[]{:S(2)}, u32[]{:S(2)}) collective-permute-start(bf16[512,512]{1,0:T(8,128)(2,1)S(1)} %shard_map.116), channel_id=1, source_target_pairs={{0,1},{1,0},{2,3},{3,2},{4,5},{5,4},{6,7},{7,6},{8,9},{9,8},{10,11... | collective-permute-start | bytes 1572872 | tf_op jit(solution)/shard_map/ppermute | solution.py:184
  194.8 21.3 %collective-permute-start.60 = (bf16[512,512]{1,0:T(8,128)(2,1)S(1)}, bf16[512,512]{1,0:T(8,128)(2,1)S(1)}, u32[]{:S(2)}, u32[]{:S(2)}) collective-permute-start(bf16[512,512]{1,0:T(8,128)(2,1)S(1)} %shard_map.117), channel_id=1, source_target_pairs={{0,1},{1,0},{2,3},{3,2},{4,5},{5,4},{6,7},{7,6},{8,9},{9,8},{10,11... | collective-permute-start | bytes 1572872 | tf_op jit(solution)/shard_map/ppermute | solution.py:184
  (82 other events, 1254.5 us)

commit v3 on v2

--- a/solution.py
+++ b/solution.py
@@ -213,8 +213,9 @@
     out[...] = total.astype(BF16)
 
 
-def rank_kernel(count, scalars, ids, normed, down, out):
-    masked_ranks(scalars, ids, down, normed, out, count)
+def rank_kernel(count, scalars, ids, normed, down, first, out):
+    out[0] = first[...]
+    masked_ranks(scalars, ids, down, normed, out.at[1], count)
 
 
 def first_rank_kernel(pieces, scalars, ids, normed, *refs):
@@ -251,16 +252,16 @@
     )(scalars, ids, normed, *pieces.arrays)
 
 
-def more_ranks(scalars, ids, normed, down, count):
+def more_ranks(scalars, ids, normed, down, first, count):
     rows, width = normed.shape
     return pl.pallas_call(
         functools.partial(rank_kernel, count),
-        out_shape=jax.ShapeDtypeStruct((down.shape[0] // count, rows), BF16),
-        in_specs=[SMEM, VMEM, VMEM, VMEM],
+        out_shape=jax.ShapeDtypeStruct((2, down.shape[0] // count, rows), BF16),
+        in_specs=[SMEM, VMEM, VMEM, VMEM, VMEM],
         out_specs=VMEM,
         compiler_params=params(24),
         cost_estimate=SMALL,
-    )(scalars, ids, normed, down)
+    )(scalars, ids, normed, down, first)
 
 
 def spread(ranks, ids, scalars, count, into):
@@ -297,10 +298,10 @@
 
 def kv_kernel(pieces, inner, head, *refs):
     scalars, ids_own, ids_nb, gains = refs[:4]
-    ranks = refs[4:8]
-    normed = refs[8:10]
-    held = refs[10 : 10 + len(pieces.arrays)]
-    out, weight, up, into, sems = refs[10 + len(pieces.arrays) :]
+    ranks, ranks_there = refs[4:6]
+    normed = refs[6:8]
+    held = refs[8 : 8 + len(pieces.arrays)]
+    out, weight, up, into, sems = refs[8 + len(pieces.arrays) :]
     deep, count = pieces.deep - 4 * inner, len(pieces.names)
     columns = pl.ds(head * HEAD_DIM, HEAD_DIM)
     copies = []
@@ -325,7 +326,7 @@
     for copy in copies:
         copy.start()
     for side, ids in ((0, ids_own), (1, ids_nb)):
-        both = ranks[2 * side][...] + ranks[2 * side + 1][...]
+        both = ranks[side] + ranks_there[1 - side]
         for kind in range(2):
             part = both[(1 + kind) * inner : (2 + kind) * inner]
             spread(part, ids, scalars, count, into.at[2 * side + kind])
@@ -340,11 +341,11 @@
 
 def keys_values(head, scalars, ids_own, ids_nb, gains, ranks, normed_own, normed_nb, pieces):
     rows, width = normed_own.shape
-    count, inner = len(pieces.names), ranks[0].shape[0] // 3
+    count, inner = len(pieces.names), ranks[0].shape[1] // 3
     return pl.pallas_call(
         functools.partial(kv_kernel, pieces, inner, head),
         out_shape=jax.ShapeDtypeStruct((2, rows, 2 * HEAD_DIM), BF16),
-        in_specs=[SMEM] + [VMEM] * 9 + [ANY] * len(pieces.arrays),
+        in_specs=[SMEM] + [VMEM] * 7 + [ANY] * len(pieces.arrays),
         out_specs=VMEM,
         scratch_shapes=[
             pltpu.VMEM((2, width, HEAD_DIM), BF16),
@@ -357,59 +358,70 @@
     )(scalars, ids_own, ids_nb, gains, *ranks, normed_own, normed_nb, *pieces.arrays)
 
 
-def query_kernel(count, inner, *refs):
-    scalars, ids_own, ids_nb, gains, normed_own, normed_nb = refs[:6]
-    ranks = refs[6:10]
-    pieces = refs[10 : 10 + count]
-    out_own, out_nb, weight, up, into_own, into_nb, sems = refs[10 + count :]
+def query_kernel(count, inner, head, *refs):
+    scalars, ids_own, ids_nb, gains = refs[:4]
+    ranks, ranks_there = refs[4:6]
+    pieces = refs[8 : 8 + count]
+    out, weight, up, into, normed, sems = refs[8 + count :]
     deep = pieces[0].shape[0] - 2 * inner
+    columns = pl.ds(head * weight.shape[1], weight.shape[1])
+    whole = [
+        pltpu.make_async_copy(refs[6 + side], normed.at[side], sems.at[2 * count + side])
+        for side in range(2)
+    ]
+    whole[0].start()
     copies = []
     for i in range(count):
         row = pl.multiple_of(scalars[Q_ROW, i], deep)
         copies.append(
             pltpu.make_async_copy(
-                pieces[i].at[pl.ds(0, deep)], weight.at[pl.ds(row, deep)], sems.at[2 * i]
+                pieces[i].at[pl.ds(0, deep), columns],
+                weight.at[pl.ds(row, deep)],
+                sems.at[2 * i],
             )
         )
         copies.append(
             pltpu.make_async_copy(
-                pieces[i].at[pl.ds(deep, 2 * inner)],
+                pieces[i].at[pl.ds(deep, 2 * inner), columns],
                 up.at[pl.ds(2 * inner * i, 2 * inner)],
                 sems.at[2 * i + 1],
             )
         )
     for copy in copies:
         copy.start()
-    spread(ranks[0][0:inner] + ranks[1][0:inner], ids_own, scalars, count, into_own)
-    spread(ranks[2][0:inner] + ranks[3][0:inner], ids_nb, scalars, count, into_nb)
+    whole[1].start()
+    for side, ids in ((0, ids_own), (1, ids_nb)):
+        both = ranks[side, 0:inner] + ranks_there[1 - side, 0:inner]
+        spread(both, ids, scalars, count, into.at[side])
     for copy in copies:
         copy.wait()
-    for head in range(weight.shape[1] // HEAD_DIM):
-        cut = slice(head * HEAD_DIM, (head + 1) * HEAD_DIM)
-        for normed, into, out in ((normed_nb, into_nb, out_nb), (normed_own, into_own, out_own)):
-            block = project(normed[...], weight[:, cut], into[...], up[:, cut])
-            out[:, cut] = unit(block, gains[0:1, :])
-
-
-def queries_of(scalars, ids_own, ids_nb, gains, normed_own, normed_nb, ranks, pieces):
+    for side in range(2):
+        whole[side].wait()
+        for at in range(weight.shape[1] // HEAD_DIM):
+            cut = slice(at * HEAD_DIM, (at + 1) * HEAD_DIM)
+            block = project(normed[side], weight[:, cut], into[side], up[:, cut])
+            out[side, :, cut] = unit(block, gains[0:1, :])
+
+
+def queries_of(head, scalars, ids_own, ids_nb, gains, ranks, normed_own, normed_nb, pieces):
     rows, width = normed_own.shape
-    count, inner = len(pieces), ranks[0].shape[0] // 3
-    columns = pieces[0].shape[1]
+    count, inner = len(pieces), ranks[0].shape[1] // 3
+    columns = pieces[0].shape[1] // 2
     return pl.pallas_call(
-        functools.partial(query_kernel, count, inner),
-        out_shape=[jax.ShapeDtypeStruct((rows, columns), BF16)] * 2,
-        in_specs=[SMEM] + [VMEM] * 9 + [ANY] * count,
-        out_specs=[VMEM, VMEM],
+        functools.partial(query_kernel, count, inner, head),
+        out_shape=jax.ShapeDtypeStruct((2, rows, columns), BF16),
+        in_specs=[SMEM] + [VMEM] * 5 + [ANY] * (2 + count),
+        out_specs=VMEM,
         scratch_shapes=[
             pltpu.VMEM((width, columns), BF16),
             pltpu.VMEM((2 * inner * count, columns), BF16),
-            pltpu.VMEM((2 * inner * count, rows), BF16),
-            pltpu.VMEM((2 * inner * count, rows), BF16),
-            pltpu.SemaphoreType.DMA((2 * count,)),
+            pltpu.VMEM((2, 2 * inner * count, rows), BF16),
+            pltpu.VMEM((2, rows, width), BF16),
+            pltpu.SemaphoreType.DMA((2 * count + 2,)),
         ],
         compiler_params=params(56),
         cost_estimate=SMALL,
-    )(scalars, ids_own, ids_nb, gains, normed_own, normed_nb, *ranks, *pieces)
+    )(scalars, ids_own, ids_nb, gains, *ranks, normed_own, normed_nb, *pieces)
 
 
 def attend_kernel(places, queries, seg_rows, seg_keys, *refs):
@@ -470,9 +482,8 @@
             ].astype(BF16)
 
 
-def attend(head, places, queries, seg_rows, seg_keys, blocks):
-    rows = queries.shape[0]
-    width = queries.shape[1] // 2
+def attend(side, places, queries, seg_rows, seg_keys, blocks):
+    rows, width = queries.shape[1:]
     slots = seg_keys.shape[1] // rows
     return pl.pallas_call(
         attend_kernel,
@@ -480,7 +491,7 @@
         out_shape=jax.ShapeDtypeStruct((rows, width), BF16),
         in_specs=[
             SMEM,
-            pl.BlockSpec((rows, width), lambda i: (0, head)),
+            pl.BlockSpec((None, rows, width), lambda i: (side, 0, 0)),
             pl.BlockSpec((rows, 1), lambda i: (0, 0)),
             pl.BlockSpec((1, slots * rows), lambda i: (0, 0)),
         ]
@@ -667,12 +678,9 @@
     part_own, down_all = first_ranks(scalars, ids_own, normed_own, down_parts)
     q[2], part_own = tied((q[2], part_own))
     q.append(ring(q[2]))
-    part_nb = more_ranks(scalars, ids_nb, normed_nb, down_all, 16)
-    back_nb = swap_y(part_own)
-    back_own = swap_y(part_nb)
-    back_own, back_nb = tied((back_own, back_nb))
+    ranks_here = more_ranks(scalars, ids_nb, normed_nb, down_all, part_own, 16)
+    ranks = (ranks_here, swap_y(ranks_here))
     gains = query_key_gains
-    ranks = (part_own, back_own, part_nb, back_nb)
     kv_all = Pieces(kv_pieces, [(i, 0) for i in range(16)], kv_pieces[0].shape[0])
     kv_heads = [
         keys_values(head, scalars, ids_own, ids_nb, gains, ranks, normed_own, normed_nb, kv_all)
@@ -680,16 +688,17 @@
     ]
     seg_before = halo(seg_pair)
     q_x = [swap_x(part) for part in q[:3]]
-    kv_heads[0], seg_before, q, q_x = tied((kv_heads[0], seg_before, q, q_x))
+    kv_heads[0], seg_before, q, q_x[:2] = tied((kv_heads[0], seg_before, q, q_x[:2]))
     arriving = [halo(kv_heads[0]), halo(kv_heads[1])]
     q_x.append(swap_x(q[3]))
     q, q_x[:3] = tied((q, q_x[:3]), kv_heads[1])
     q_c = [swap_core(part) for part in q]
-    q_x[3], arriving[0] = tied((q_x[3], arriving[0]))
-    q_xc = [swap_core(part) for part in q_x]
+    q_xc = [swap_core(part) for part in q_x[:3]]
+    q_x[3], arriving[0], q_c, q_xc = tied((q_x[3], arriving[0], q_c, q_xc))
+    q_xc.append(swap_core(q_x[3]))
     q_pieces = flat(q, q_x, q_c, q_xc)
-    queries_own, queries_nb = queries_of(
-        scalars, ids_own, ids_nb, gains, normed_own, normed_nb, ranks, q_pieces
+    project_queries = lambda head, ranks: queries_of(
+        head, scalars, ids_own, ids_nb, gains, ranks, normed_own, normed_nb, q_pieces
     )
     seg_before = jnp.where((place == 0) & (z == 0), -1, seg_before)
     seg_span = jnp.concatenate([seg_before, seg_pair])
@@ -701,13 +710,17 @@
         places = jnp.stack([y, 1 - y, 2 + y, 3 - y]) - parity
         spans[name] = (places.astype(jnp.int32), seg_rows, seg_keys)
     where = jnp.stack([y, place, x, core]).astype(jnp.int32)
-    kept, got = [], []
+    kept, got, queries, last = [], [], [], ranks
     for head, both in enumerate(kv_heads):
-        blocks = (tied(arriving[head], kept[-1]) if kept else arriving[head], both)
+        queries.append(project_queries(head, last))
         places, seg_rows, seg_keys = spans["nb"]
-        got.append(swap_y(attend(head, places, queries_nb, seg_rows, seg_keys, blocks)))
+        sent = attend(1, places, queries[head], seg_rows, seg_keys, (arriving[head], both))
+        got.append(swap_y(sent))
+        last = tied(ranks, sent)
+    for head, both in enumerate(kv_heads):
         places, seg_rows, seg_keys = spans["own"]
-        kept.append(attend(head, places, queries_own, seg_rows, seg_keys, blocks))
+        mine = tied(queries[head], last)
+        kept.append(attend(0, places, mine, seg_rows, seg_keys, (arriving[head], both)))
     return side_by_side(where, kept, got)
 
 

time: 219 us -> 210 us (0.959)
  waiting for transfers between devices: 87.5 us -> 68.1 us
  Pallas kernels: 50.6 us -> 58.5 us
    ppermute x61 -> x60, waiting for transfers between devices: 87.5 us -> 68.1 us  [route(): return lax.ppermute(value, ('dp', 'adapter'), pairs)]
    pallas_call x1 -> x2, Pallas kernels: 13.5 us -> 17.3 us  [queries_of(): pl.pallas_call(functools.partial(query_kernel, count, inner, head), out_s...]
    pallas_call x4, Pallas kernels: 12.6 us -> 16.1 us  [attend(): pl.pallas_call(attend_kernel, grid=(1,), out_shape=jax.ShapeDtypeStruct((...]
    unnamed x106 -> x112, local copies, waits for them, and re-layouts: 7.15 us -> 9.95 us
    ppermute x61 -> x60, starting transfers between devices: 52.2 us -> 51.7 us  [route(): return lax.ppermute(value, ('dp', 'adapter'), pairs)]
  transfers between devices with their start and end apart: 61 -> 60, of which waited for: 24 -> 22; matrix products, arithmetic and copies ran while one was open for 8% -> 8% of each run, Pallas kernels for 21% -> 27%
where the time goes in v3:
time: 210 us; the launch traced here: 207 us
  waiting for transfers between devices  68.1 us (32%)
  Pallas kernels  58.5 us (28%)
  starting transfers between devices  51.7 us (25%)
  local copies, waits for them, and re-layouts  17.6 us (8%)
  other arithmetic  10.5 us (5%)
    ppermute x60, waiting for transfers between devices, route(): return lax.ppermute(value, ('dp', 'adapter'), pairs)  68.1 us
    ppermute x60, starting transfers between devices, route(): return lax.ppermute(value, ('dp', 'adapter'), pairs)  51.7 us
    pallas_call x2, Pallas kernels, queries_of(): pl.pallas_call(functools.partial(query_kernel, count, inner, head), out_s...  17.3 us
    pallas_call x4, Pallas kernels, attend(): pl.pallas_call(attend_kernel, grid=(1,), out_shape=jax.ShapeDtypeStruct((...  16.1 us
    pallas_call x2, Pallas kernels, keys_values(): pl.pallas_call(functools.partial(kv_kernel, pieces, inner, head), out_sha...  12.1 us
    unnamed x112, local copies, waits for them, and re-layouts  9.95 us
    pallas_call x1, Pallas kernels, first_ranks(): pl.pallas_call(functools.partial(first_rank_kernel, pieces), out_shape=[j...  7.43 us
    reduce_sum x2, other arithmetic, row_norm(): scale = lax.rsqrt(jnp.mean(values * values, axis=-1, keepdims=True) + 1e-06)  4.33 us
  transfers between devices with their start and end apart: 60, of which 22 were waited for; matrix products, arithmetic and copies ran while one was open for 8% of the time, Pallas kernels for 27%

profile of v3, /device:TPU:6, one launch (start us, length us, event | category | flops | bytes accessed | tf_op | source)
XLA Modules:
  0.0 207.4 jit_solution(744801701327133488)
XLA Ops:
  4.2 5.2 %collective-permute-start.2 = (bf16[320,512]{1,0:T(8,128)(2,1)S(1)}, bf16[320,512]{1,0:T(8,128)(2,1)S(1)}, u32[]{:S(2)}, u32[]{:S(2)}) collective-permute-start(bf16[320,512]{1,0:T(8,128)(2,1)S(1)} %constant_dynamic-slice_fusion), channel_id=1, source_target_pairs={{16,1},{17,0},{18,3},{19,2},{20,5},{21,4},{22,7},{23,6},{24,9},{25... | collective-permute-start | bytes 983048 | tf_op jit(solution)/shard_map/ppermute | solution.py:184
  15.8 3.1 %collective-permute-done.3 = bf16[16,2048]{1,0:T(8,128)(2,1)S(1)} collective-permute-done((bf16[16,2048]{1,0:T(8,128)(2,1)S(1)}, bf16[16,2048]{1,0:T(8,128)(2,1)S(1)}, u32[]{:S(2)}, u32[]{:S(2)}) %collective-permute-start.3) | collective-permute-done | bytes 65568 | tf_op jit(solution)/shard_map/ppermute | solution.py:184
  22.1 3.2 %fusion.14 = (bf16[128,2560]{1,0:T(8,128)(2,1)}, bf16[128,2560]{1,0:T(8,128)(2,1)}, bf16[128,2560]{1,0:T(8,128)(2,1)}, bf16[128,2560]{1,0:T(8,128)(2,1)}) fusion(bf16[512,2560]{1,0:T(8,128)(2,1)} %param.11), kind=kLoop, calls=%fused_computation.63 | loop fusion | bytes 5242880 | tf_op jit(solution)/shard_map/split | solution.py:625
  30.6 3.6 %collective-permute-done.12.refs_12_ = bf16[384,512]{1,0:T(8,128)(2,1)S(1)} collective-permute-done((bf16[384,512]{1,0:T(8,128)(2,1)S(1)}, bf16[384,512]{1,0:T(8,128)(2,1)S(1)}, u32[]{:S(2)}, u32[]{:S(2)}) %collective-permute-start.12) | collective-permute-done | bytes 393248 | tf_op jit(solution)/shard_map/ppermute | solution.py:184
  36.1 3.0 %collective-permute-done.13.refs_9_ = bf16[384,512]{1,0:T(8,128)(2,1)S(1)} collective-permute-done((bf16[384,512]{1,0:T(8,128)(2,1)S(1)}, bf16[384,512]{1,0:T(8,128)(2,1)S(1)}, u32[]{:S(2)}, u32[]{:S(2)}) %collective-permute-start.13) | collective-permute-done | bytes 393248 | tf_op jit(solution)/shard_map/ppermute | solution.py:184
  40.7 2.1 collective-permute-start.21
  46.0 2.3 %fusion.3 = f32[512]{0:T(512)S(1)} fusion(bf16[512,2560]{1,0:T(8,128)(2,1)} %param.11), kind=kLoop, calls=%fused_computation.7 | loop fusion | flops 3931648 | bytes 2623488 | tf_op jit(solution)/shard_map/reduce_sum | solution.py:193
  48.3 4.4 %collective-permute-done.20.refs_16_ = bf16[384,512]{1,0:T(8,128)(2,1)S(1)} collective-permute-done((bf16[384,512]{1,0:T(8,128)(2,1)S(1)}, bf16[384,512]{1,0:T(8,128)(2,1)S(1)}, u32[]{:S(2)}, u32[]{:S(2)}) %collective-permute-start.20) | collective-permute-done | bytes 393248 | tf_op jit(solution)/shard_map/ppermute | solution.py:184
  54.3 2.1 collective-permute-start.27
  62.9 3.7 %collective-permute-done.26.refs_20_ = bf16[384,512]{1,0:T(8,128)(2,1)} collective-permute-done((bf16[384,512]{1,0:T(8,128)(2,1)S(1)}, bf16[384,512]{1,0:T(8,128)(2,1)}, u32[]{:S(2)}, u32[]{:S(2)}) %collective-permute-start.26) | collective-permute-done | bytes 393248 | tf_op jit(solution)/shard_map/ppermute | solution.py:184
  69.1 2.3 %collective-permute-done.17.refs_12_ = bf16[48,2560]{1,0:T(8,128)(2,1)} collective-permute-done((bf16[48,2560]{1,0:T(8,128)(2,1)S(1)}, bf16[48,2560]{1,0:T(8,128)(2,1)}, u32[]{:S(2)}, u32[]{:S(2)}) %collective-permute-start.17) | collective-permute-done | bytes 245792 | tf_op jit(solution)/shard_map/ppermute | solution.py:184
  71.8 2.0 collective-permute-done.18.refs_9_
  75.8 6.6 %collective-permute-done.16.refs_12_ = bf16[192,1024]{1,0:T(8,128)(2,1)S(1)} collective-permute-done((bf16[192,1024]{1,0:T(8,128)(2,1)S(1)}, bf16[192,1024]{1,0:T(8,128)(2,1)S(1)}, u32[]{:S(2)}, u32[]{:S(2)}) %collective-permute-start.16) | collective-permute-done | bytes 393248 | tf_op jit(solution)/shard_map/ppermute | solution.py:184
  84.1 6.3 %collective-permute-done.24.refs_13_ = bf16[48,2560]{1,0:T(8,128)(2,1)} collective-permute-done((bf16[48,2560]{1,0:T(8,128)(2,1)}, bf16[48,2560]{1,0:T(8,128)(2,1)}, u32[]{:S(2)}, u32[]{:S(2)}) %collective-permute-start.24) | collective-permute-done | bytes 245792 | tf_op jit(solution)/shard_map/ppermute | solution.py:184
  91.0 2.0 fusion
  94.9 2.6 %fusion.5 = (bf16[512,2560]{1,0:T(8,128)(2,1)S(1)}, bf16[512,2560]{1,0:T(8,128)(2,1)S(1)}) fusion(bf16[512,2560]{1,0:T(8,128)(2,1)S(1)} %copy-done.34, f32[512]{0:T(512)S(1)} %add_rsqrt_fusion, f32[2560]{0:T(1024)S(1)} %copy-done.51, f32[512]{0:T(512)S(1)} %add_rsqrt_fusion.1, bf16[128,2560]{1,0:T(8,128)(2,1)} %collective-permute-done.29, ...), kind=kLoop, calls=%fused_computation.9 | loop fusion | flops 19660800 | bytes 10500096 | tf_op jit(solution)/shard_map/convert_element_type | solution.py:194
  97.7 7.4 %shard_map.109 = (bf16[48,512]{1,0:T(8,128)(2,1)S(1)}, bf16[768,2560]{1,0:T(8,128)(2,1)S(1)}) custom-call(s32[6,16]{1,0:T(8,128)S(1)} %stack.75.scalars.refs_0_, s32[1,512]{1,0:T(1,128)S(1)} %bitcast.42, bf16[512,2560]{1,0:T(8,128)(2,1)S(1)} %get-tuple-element.156.normed.refs_6_, bf16[48,2560]{1,0:T(8,128)(2,1)S(1)} %dynamic-slice_bitcast_fusion.refs_0_, ...), custom_call_target="tpu_custom_call" | custom-call | flops 1 | bytes 1 | tf_op jit(solution)/shard_map/pallas_call | solution.py:241
  110.7 2.8 %shard_map.110.refs_4_ = bf16[2,48,512]{2,1,0:T(8,128)(2,1)S(1)} custom-call(s32[6,16]{1,0:T(8,128)S(1)} %stack.75.scalars.refs_0_, s32[1,512]{1,0:T(1,128)S(1)} %get-tuple-element.163.ids.refs_2_, bf16[512,2560]{1,0:T(8,128)(2,1)S(1)} %get-tuple-element.157.normed.refs_7_, bf16[768,2560]{1,0:T(8,128)(2,1)S(1)} %get-tuple-element.96.down, ...), custom_call_target="tpu_custom_call" | custom-call | flops 1 | bytes 1 | tf_op jit(solution)/shard_map/pallas_call | solution.py:257
  113.9 4.3 %collective-permute-done.35.refs_5_ = bf16[2,48,512]{2,1,0:T(8,128)(2,1)S(1)} collective-permute-done((bf16[2,48,512]{2,1,0:T(8,128)(2,1)S(1)}, bf16[2,48,512]{2,1,0:T(8,128)(2,1)S(1)}, u32[]{:S(2)}, u32[]{:S(2)}) %collective-permute-start.35) | collective-permute-done | bytes 98336 | tf_op jit(solution)/shard_map/ppermute | solution.py:184
  118.2 2.6 %collective-permute-start.42 = (s32[1024]{0:T(1024)S(1)}, s32[1024]{0:T(1024)S(1)}, u32[]{:S(2)}, u32[]{:S(2)}) collective-permute-start(s32[1024]{0:T(1024)S(1)} %add_select_fusion), channel_id=1, source_target_pairs={{0,2},{1,3},{2,4},{3,5},{4,6},{5,7},{6,8},{7,9},{8,10},{9,11},{10,... | collective-permute-start | bytes 12296 | tf_op jit(solution)/shard_map/ppermute | solution.py:184
  120.9 6.1 %shard_map.111.refs_1_ = bf16[2,512,512]{2,1,0:T(8,128)(2,1)S(1)} custom-call(s32[6,16]{1,0:T(8,128)S(1)} %stack.75.scalars.refs_0_, s32[1,512]{1,0:T(1,128)S(1)} %bitcast.43, s32[1,512]{1,0:T(1,128)S(1)} %get-tuple-element.163.ids.refs_2_, f32[2,256]{1,0:T(2,128)S(1)} %copy-done.33, bf16[2,48,512]{2,1,0:T(8,128)(2,1)S(1)} %shard_map.110.refs_4_, ...), custom_call_target="tpu_custom_call" | custom-call | flops 1 | bytes 1 | tf_op jit(solution)/shard_map/pallas_call | solution.py:345
  133.1 6.0 %shard_map.112.refs_1_ = bf16[2,512,512]{2,1,0:T(8,128)(2,1)S(1)} custom-call(s32[6,16]{1,0:T(8,128)S(1)} %stack.75.scalars.refs_0_, s32[1,512]{1,0:T(1,128)S(1)} %bitcast.44, s32[1,512]{1,0:T(1,128)S(1)} %get-tuple-element.163.ids.refs_2_, f32[2,256]{1,0:T(2,128)S(1)} %copy-done.33, bf16[2,48,512]{2,1,0:T(8,128)(2,1)S(1)} %shard_map.110.refs_4_, ...), custom_call_target="tpu_custom_call" | custom-call | flops 1 | bytes 1 | tf_op jit(solution)/shard_map/pallas_call | solution.py:345
  139.8 9.6 %collective-permute-done.47.refs_21_ = bf16[192,1024]{1,0:T(8,128)(2,1)S(1)} collective-permute-done((bf16[192,1024]{1,0:T(8,128)(2,1)S(1)}, bf16[192,1024]{1,0:T(8,128)(2,1)S(1)}, u32[]{:S(2)}, u32[]{:S(2)}) %collective-permute-start.47) | collective-permute-done | bytes 393248 | tf_op jit(solution)/shard_map/ppermute | solution.py:184
  155.6 3.8 %collective-permute-done.48.refs_0_ = bf16[2,512,512]{2,1,0:T(8,128)(2,1)} collective-permute-done((bf16[2,512,512]{2,1,0:T(8,128)(2,1)S(1)}, bf16[2,512,512]{2,1,0:T(8,128)(2,1)}, u32[]{:S(2)}, u32[]{:S(2)}) %collective-permute-start.48) | collective-permute-done | bytes 1048608 | tf_op jit(solution)/shard_map/ppermute | solution.py:184
  161.4 8.7 %shard_map.113.queries = bf16[2,512,512]{2,1,0:T(8,128)(2,1)} custom-call(s32[6,16]{1,0:T(8,128)} %copy-done.30, s32[1,512]{1,0:T(1,128)} %bitcast.40, s32[1,512]{1,0:T(1,128)} %copy-done.32, f32[2,256]{1,0:T(2,128)} %refs_3_.7, bf16[2,48,512]{2,1,0:T(8,128)(2,1)} %copy-done.7, bf16[2,48,512]{2,1,0:T(8,128)(2,1)} %copy-done.8, bf16[512,2560]{1,0:T(8,128)(2,1)} %copy-done.1, ...), custom_call_target="tpu_custom_call" | custom-call | flops 1 | bytes 1 | tf_op jit(solution)/shard_map/pallas_call | solution.py:410
  171.3 4.5 %shard_map.114 = bf16[512,512]{1,0:T(8,128)(2,1)} custom-call(s32[4]{0:T(128)S(1)} %get-tuple-element.137.places, bf16[2,512,512]{2,1,0:T(8,128)(2,1)S(1)} %copy-done.3, s32[512,1]{1,0:T(8,128)S(1)} %copy.12.seg_rows, s32[1,1536]{1,0:T(1,128)S(1)} %broadcast_in_dim.32.seg_keys, bf16[2,512,512]{2,1,0:T(8,128)(2,1)} %collective-permute-done.48.refs_0_, ...), custom_call_target="tpu_custom_call" | custom-call | flops 1 | bytes 1 | tf_op jit(solution)/shard_map/pallas_call | solution.py:488
  176.1 8.7 %shard_map.115.queries = bf16[2,512,512]{2,1,0:T(8,128)(2,1)} custom-call(s32[6,16]{1,0:T(8,128)} %copy-done.30, s32[1,512]{1,0:T(1,128)} %bitcast.41, s32[1,512]{1,0:T(1,128)} %copy-done.32, f32[2,256]{1,0:T(2,128)} %refs_3_.7, bf16[2,48,512]{2,1,0:T(8,128)(2,1)} %copy-done.7, bf16[2,48,512]{2,1,0:T(8,128)(2,1)} %copy-done.8, bf16[512,2560]{1,0:T(8,128)(2,1)} %copy-done.1, ...), custom_call_target="tpu_custom_call" | custom-call | flops 1 | bytes 1 | tf_op jit(solution)/shard_map/pallas_call | solution.py:410
  186.0 4.5 %shard_map.116 = bf16[512,512]{1,0:T(8,128)(2,1)} custom-call(s32[4]{0:T(128)S(1)} %get-tuple-element.137.places, bf16[2,512,512]{2,1,0:T(8,128)(2,1)S(1)} %copy-done.5, s32[512,1]{1,0:T(8,128)S(1)} %copy.12.seg_rows, s32[1,1536]{1,0:T(1,128)S(1)} %broadcast_in_dim.32.seg_keys, bf16[2,512,512]{2,1,0:T(8,128)(2,1)} %collective-permute-done.57.refs_0_, ...), custom_call_target="tpu_custom_call" | custom-call | flops 1 | bytes 1 | tf_op jit(solution)/shard_map/pallas_call | solution.py:488
  193.8 3.6 %shard_map.117.refs_0_ = bf16[512,512]{1,0:T(8,128)(2,1)S(1)} custom-call(s32[4]{0:T(128)S(1)} %broadcast_subtract_fusion.1.places, bf16[2,512,512]{2,1,0:T(8,128)(2,1)S(1)} %copy-done.4, s32[512,1]{1,0:T(8,128)S(1)} %copy.14.seg_rows, s32[1,1536]{1,0:T(1,128)S(1)} %broadcast_in_dim.34.seg_keys, bf16[2,512,512]{2,1,0:T(8,128)(2,1)} %collective-permute-done.48.refs_0_, ...), custom_call_target="tpu_custom_call" | custom-call | flops 1 | bytes 1 | tf_op jit(solution)/shard_map/pallas_call | solution.py:488
  197.3 3.6 %shard_map.118.refs_1_ = bf16[512,512]{1,0:T(8,128)(2,1)S(1)} custom-call(s32[4]{0:T(128)S(1)} %broadcast_subtract_fusion.1.places, bf16[2,512,512]{2,1,0:T(8,128)(2,1)S(1)} %copy-done.6, s32[512,1]{1,0:T(8,128)S(1)} %copy.14.seg_rows, s32[1,1536]{1,0:T(1,128)S(1)} %broadcast_in_dim.34.seg_keys, bf16[2,512,512]{2,1,0:T(8,128)(2,1)} %collective-permute-done.57.refs_0_, ...), custom_call_target="tpu_custom_call" | custom-call | flops 1 | bytes 1 | tf_op jit(solution)/shard_map/pallas_call | solution.py:488
  200.9 3.8 %collective-permute-done.59.refs_3_ = bf16[512,512]{1,0:T(8,128)(2,1)} collective-permute-done((bf16[512,512]{1,0:T(8,128)(2,1)}, bf16[512,512]{1,0:T(8,128)(2,1)}, u32[]{:S(2)}, u32[]{:S(2)}) %collective-permute-start.59) | collective-permute-done | bytes 524320 | tf_op jit(solution)/shard_map/ppermute | solution.py:184
  204.7 2.7 %shard_map.119 = bf16[512,2048]{1,0:T(8,128)(2,1)} custom-call(s32[4]{0:T(128)S(1)} %pad_add_fusion.1.where, bf16[512,512]{1,0:T(8,128)(2,1)S(1)} %shard_map.117.refs_0_, bf16[512,512]{1,0:T(8,128)(2,1)S(1)} %shard_map.118.refs_1_, bf16[512,512]{1,0:T(8,128)(2,1)} %collective-permute-done.58.refs_2_, bf16[512,512]{1,0:T(8,128)(2,1)} %collective-permute-done.59.refs_3_), custom_call_target="tpu_custom_call" | custom-call | flops 1 | bytes 1 | tf_op jit(solution)/shard_map/pallas_call | solution.py:521
  (247 shorter events, 69.2 us)
Async XLA Ops:
  1.2 19.6 %collective-permute-start = (bf16[160,1024]{1,0:T(8,128)(2,1)S(1)}, bf16[160,1024]{1,0:T(8,128)(2,1)S(1)}, u32[]{:S(2)}, u32[]{:S(2)}) collective-permute-start(bf16[160,1024]{1,0:T(8,128)(2,1)S(1)} %get-tuple-element.147), channel_id=1, source_target_pairs={{1,8},{3,10},{5,12},{7,14},{8,1},{10,3},{12,5},{14,7}} | collective-permute-start | bytes 983048 | tf_op jit(solution)/shard_map/ppermute | solution.py:184
  1.9 18.9 %collective-permute-start.1 = (bf16[160,1024]{1,0:T(8,128)(2,1)S(1)}, bf16[160,1024]{1,0:T(8,128)(2,1)}, u32[]{:S(2)}, u32[]{:S(2)}) collective-permute-start(bf16[160,1024]{1,0:T(8,128)(2,1)S(1)} %get-tuple-element.146), channel_id=1, source_target_pairs={{0,16},{1,24},{2,18},{3,26},{4,20},{5,28},{6,22},{7,30},{8,17},{9,... | collective-permute-start | bytes 983048 | tf_op jit(solution)/shard_map/ppermute | solution.py:184
  4.2 16.6 %collective-permute-start.2 = (bf16[320,512]{1,0:T(8,128)(2,1)S(1)}, bf16[320,512]{1,0:T(8,128)(2,1)S(1)}, u32[]{:S(2)}, u32[]{:S(2)}) collective-permute-start(bf16[320,512]{1,0:T(8,128)(2,1)S(1)} %constant_dynamic-slice_fusion), channel_id=1, source_target_pairs={{16,1},{17,0},{18,3},{19,2},{20,5},{21,4},{22,7},{23,6},{24,9},{25... | collective-permute-start | bytes 983048 | tf_op jit(solution)/shard_map/ppermute | solution.py:184
  22.1 12.1 %collective-permute-start.12 = (bf16[384,512]{1,0:T(8,128)(2,1)S(1)}, bf16[384,512]{1,0:T(8,128)(2,1)S(1)}, u32[]{:S(2)}, u32[]{:S(2)}) collective-permute-start(bf16[384,512]{1,0:T(8,128)(2,1)S(1)} %fusion.6.refs_8_), channel_id=1, source_target_pairs={{0,2},{1,3},{2,4},{3,5},{4,6},{5,7},{6,0},{7,1},{8,10},{9,11},{10,... | collective-permute-start | bytes 1179656 | tf_op jit(solution)/shard_map/ppermute | solution.py:184
  25.4 19.3 %collective-permute-start.9 = (bf16[128,2560]{1,0:T(8,128)(2,1)}, bf16[128,2560]{1,0:T(8,128)(2,1)}, u32[]{:S(2)}, u32[]{:S(2)}) collective-permute-start(bf16[128,2560]{1,0:T(8,128)(2,1)} %get-tuple-element.145), channel_id=1, source_target_pairs={{0,1},{1,0},{2,3},{3,2},{4,5},{5,4},{6,7},{7,6},{8,9},{9,8},{10,11... | collective-permute-start | bytes 1966088 | tf_op jit(solution)/shard_map/ppermute | solution.py:184
  27.1 12.0 %collective-permute-start.13 = (bf16[384,512]{1,0:T(8,128)(2,1)S(1)}, bf16[384,512]{1,0:T(8,128)(2,1)S(1)}, u32[]{:S(2)}, u32[]{:S(2)}) collective-permute-start(bf16[384,512]{1,0:T(8,128)(2,1)S(1)} %fusion.6.refs_8_), channel_id=1, source_target_pairs={{0,16},{1,17},{2,18},{3,19},{4,20},{5,21},{6,22},{7,23},{8,24},{9,... | collective-permute-start | bytes 1179656 | tf_op jit(solution)/shard_map/ppermute | solution.py:184
  29.0 11.6 %collective-permute-start.6 = (bf16[48,2560]{1,0:T(8,128)(2,1)S(1)}, bf16[48,2560]{1,0:T(8,128)(2,1)S(1)}, u32[]{:S(2)}, u32[]{:S(2)}) collective-permute-start(bf16[48,2560]{1,0:T(8,128)(2,1)S(1)} %collective-permute-done.5.refs_4_), channel_id=1, source_target_pairs={{0,2},{1,3},{2,4},{3,5},{4,6},{5,7},{6,0},{7,1},{8,10},{9,11},{10,... | collective-permute-start | bytes 737288 | tf_op jit(solution)/shard_map/ppermute | solution.py:184
  39.1 13.6 %collective-permute-start.20 = (bf16[384,512]{1,0:T(8,128)(2,1)S(1)}, bf16[384,512]{1,0:T(8,128)(2,1)S(1)}, u32[]{:S(2)}, u32[]{:S(2)}) collective-permute-start(bf16[384,512]{1,0:T(8,128)(2,1)S(1)} %collective-permute-done.12.refs_12_), channel_id=1, source_target_pairs={{0,2},{1,3},{2,4},{3,5},{4,6},{5,7},{6,0},{7,1},{8,10},{9,11},{10,... | collective-permute-start | bytes 1179656 | tf_op jit(solution)/shard_map/ppermute | solution.py:184
  40.7 12.1 %collective-permute-start.21 = (bf16[384,512]{1,0:T(8,128)(2,1)S(1)}, bf16[384,512]{1,0:T(8,128)(2,1)}, u32[]{:S(2)}, u32[]{:S(2)}) collective-permute-start(bf16[384,512]{1,0:T(8,128)(2,1)S(1)} %collective-permute-done.12.refs_12_), channel_id=1, source_target_pairs={{0,16},{1,17},{2,18},{3,19},{4,20},{5,21},{6,22},{7,23},{8,24},{9,... | collective-permute-start | bytes 1179656 | tf_op jit(solution)/shard_map/ppermute | solution.py:184
  43.8 17.5 %collective-permute-start.15 = (bf16[128,2560]{1,0:T(8,128)(2,1)}, bf16[128,2560]{1,0:T(8,128)(2,1)}, u32[]{:S(2)}, u32[]{:S(2)}) collective-permute-start(bf16[128,2560]{1,0:T(8,128)(2,1)} %get-tuple-element.81), channel_id=1, source_target_pairs={{0,1},{1,0},{2,3},{3,2},{4,5},{5,4},{6,7},{7,6},{8,9},{9,8},{10,11... | collective-permute-start | bytes 1966088 | tf_op jit(solution)/shard_map/ppermute | solution.py:184
  44.7 13.2 %collective-permute-start.10 = (bf16[48,2560]{1,0:T(8,128)(2,1)S(1)}, bf16[48,2560]{1,0:T(8,128)(2,1)S(1)}, u32[]{:S(2)}, u32[]{:S(2)}) collective-permute-start(bf16[48,2560]{1,0:T(8,128)(2,1)S(1)} %collective-permute-done.5.refs_4_), channel_id=1, source_target_pairs={{0,16},{1,17},{2,18},{3,19},{4,20},{5,21},{6,22},{7,23},{8,24},{9,... | collective-permute-start | bytes 737288 | tf_op jit(solution)/shard_map/ppermute | solution.py:184
  52.8 13.9 %collective-permute-start.26 = (bf16[384,512]{1,0:T(8,128)(2,1)S(1)}, bf16[384,512]{1,0:T(8,128)(2,1)}, u32[]{:S(2)}, u32[]{:S(2)}) collective-permute-start(bf16[384,512]{1,0:T(8,128)(2,1)S(1)} %collective-permute-done.20.refs_16_), channel_id=1, source_target_pairs={{0,2},{1,3},{2,4},{3,5},{4,6},{5,7},{6,0},{7,1},{8,10},{9,11},{10,... | collective-permute-start | bytes 1179656 | tf_op jit(solution)/shard_map/ppermute | solution.py:184
  54.3 14.1 %collective-permute-start.27 = (bf16[384,512]{1,0:T(8,128)(2,1)S(1)}, bf16[384,512]{1,0:T(8,128)(2,1)}, u32[]{:S(2)}, u32[]{:S(2)}) collective-permute-start(bf16[384,512]{1,0:T(8,128)(2,1)S(1)} %collective-permute-done.20.refs_16_), channel_id=1, source_target_pairs={{0,16},{1,17},{2,18},{3,19},{4,20},{5,21},{6,22},{7,23},{8,24},{9,... | collective-permute-start | bytes 1179656 | tf_op jit(solution)/shard_map/ppermute | solution.py:184
  59.2 23.2 %collective-permute-start.23 = (bf16[128,2560]{1,0:T(8,128)(2,1)S(1)}, bf16[128,2560]{1,0:T(8,128)(2,1)S(1)}, u32[]{:S(2)}, u32[]{:S(2)}) collective-permute-start(bf16[128,2560]{1,0:T(8,128)(2,1)S(1)} %copy-done.49), channel_id=1, source_target_pairs={{0,1},{1,0},{2,3},{3,2},{4,5},{5,4},{6,7},{7,6},{8,9},{9,8},{10,11... | collective-permute-start | bytes 1966088 | tf_op jit(solution)/shard_map/ppermute | solution.py:184
  69.1 13.3 %collective-permute-start.16 = (bf16[192,1024]{1,0:T(8,128)(2,1)S(1)}, bf16[192,1024]{1,0:T(8,128)(2,1)S(1)}, u32[]{:S(2)}, u32[]{:S(2)}) collective-permute-start(bf16[192,1024]{1,0:T(8,128)(2,1)S(1)} %pad_maximum_fusion.2.refs_8_), channel_id=1, source_target_pairs={{0,2},{1,3},{2,4},{3,5},{4,6},{5,7},{6,0},{7,1},{8,10},{9,11},{10,... | collective-permute-start | bytes 1179656 | tf_op jit(solution)/shard_map/ppermute | solution.py:184
  71.4 19.5 %collective-permute-start.29 = (bf16[128,2560]{1,0:T(8,128)(2,1)}, bf16[128,2560]{1,0:T(8,128)(2,1)}, u32[]{:S(2)}, u32[]{:S(2)}) collective-permute-start(bf16[128,2560]{1,0:T(8,128)(2,1)} %get-tuple-element.90), channel_id=1, source_target_pairs={{0,1},{1,0},{2,3},{3,2},{4,5},{5,4},{6,7},{7,6},{8,9},{9,8},{10,11... | collective-permute-start | bytes 1966088 | tf_op jit(solution)/shard_map/ppermute | solution.py:184
  83.6 25.0 %collective-permute-start.36 = (bf16[384,512]{1,0:T(8,128)(2,1)S(1)}, bf16[384,512]{1,0:T(8,128)(2,1)S(1)}, u32[]{:S(2)}, u32[]{:S(2)}) collective-permute-start(bf16[384,512]{1,0:T(8,128)(2,1)S(1)} %collective-permute-done.13.refs_9_), channel_id=1, source_target_pairs={{0,8},{1,9},{2,10},{3,11},{4,12},{5,13},{6,14},{7,15},{8,0},{9,1},... | collective-permute-start | bytes 1179656 | tf_op jit(solution)/shard_map/ppermute | solution.py:184
  93.1 16.1 %collective-permute-start.37 = (bf16[384,512]{1,0:T(8,128)(2,1)}, bf16[384,512]{1,0:T(8,128)(2,1)S(1)}, u32[]{:S(2)}, u32[]{:S(2)}) collective-permute-start(bf16[384,512]{1,0:T(8,128)(2,1)} %collective-permute-done.21.refs_13_), channel_id=1, source_target_pairs={{0,8},{1,9},{2,10},{3,11},{4,12},{5,13},{6,14},{7,15},{8,0},{9,1},... | collective-permute-start | bytes 1179656 | tf_op jit(solution)/shard_map/ppermute | solution.py:184
  93.6 15.6 %collective-permute-start.38 = (bf16[384,512]{1,0:T(8,128)(2,1)}, bf16[384,512]{1,0:T(8,128)(2,1)S(1)}, u32[]{:S(2)}, u32[]{:S(2)}) collective-permute-start(bf16[384,512]{1,0:T(8,128)(2,1)} %collective-permute-done.27.refs_17_), channel_id=1, source_target_pairs={{0,8},{1,9},{2,10},{3,11},{4,12},{5,13},{6,14},{7,15},{8,0},{9,1},... | collective-permute-start | bytes 1179656 | tf_op jit(solution)/shard_map/ppermute | solution.py:184
  93.7 13.5 %collective-permute-start.34 = (bf16[192,1024]{1,0:T(8,128)(2,1)}, bf16[192,1024]{1,0:T(8,128)(2,1)S(1)}, u32[]{:S(2)}, u32[]{:S(2)}) collective-permute-start(bf16[192,1024]{1,0:T(8,128)(2,1)} %copy-done.38), channel_id=1, source_target_pairs={{0,2},{1,3},{2,4},{3,5},{4,6},{5,7},{6,0},{7,1},{8,10},{9,11},{10,... | collective-permute-start | bytes 1179656 | tf_op jit(solution)/shard_map/ppermute | solution.py:184
  94.7 18.8 %collective-permute-start.41 = (bf16[384,512]{1,0:T(8,128)(2,1)}, bf16[384,512]{1,0:T(8,128)(2,1)S(1)}, u32[]{:S(2)}, u32[]{:S(2)}) collective-permute-start(bf16[384,512]{1,0:T(8,128)(2,1)} %collective-permute-done.39.refs_21_), channel_id=1, source_target_pairs={{0,8},{1,9},{2,10},{3,11},{4,12},{5,13},{6,14},{7,15},{8,0},{9,1},... | collective-permute-start | bytes 1179656 | tf_op jit(solution)/shard_map/ppermute | solution.py:184
  107.1 19.8 %collective-permute-start.45 = (bf16[192,1024]{1,0:T(8,128)(2,1)S(1)}, bf16[192,1024]{1,0:T(8,128)(2,1)}, u32[]{:S(2)}, u32[]{:S(2)}) collective-permute-start(bf16[192,1024]{1,0:T(8,128)(2,1)S(1)} %copy-done.39), channel_id=1, source_target_pairs={{0,16},{1,17},{2,18},{3,19},{4,20},{5,21},{6,22},{7,23},{8,24},{9,... | collective-permute-start | bytes 1179656 | tf_op jit(solution)/shard_map/ppermute | solution.py:184
  108.6 19.2 %collective-permute-start.44 = (bf16[192,1024]{1,0:T(8,128)(2,1)S(1)}, bf16[192,1024]{1,0:T(8,128)(2,1)}, u32[]{:S(2)}, u32[]{:S(2)}) collective-permute-start(bf16[192,1024]{1,0:T(8,128)(2,1)S(1)} %copy-done.36), channel_id=1, source_target_pairs={{0,16},{1,17},{2,18},{3,19},{4,20},{5,21},{6,22},{7,23},{8,24},{9,... | collective-permute-start | bytes 1179656 | tf_op jit(solution)/shard_map/ppermute | solution.py:184
  109.2 18.6 %collective-permute-start.43 = (bf16[192,1024]{1,0:T(8,128)(2,1)S(1)}, bf16[192,1024]{1,0:T(8,128)(2,1)S(1)}, u32[]{:S(2)}, u32[]{:S(2)}) collective-permute-start(bf16[192,1024]{1,0:T(8,128)(2,1)S(1)} %collective-permute-done.34.refs_16_), channel_id=1, source_target_pairs={{0,2},{1,3},{2,4},{3,5},{4,6},{5,7},{6,0},{7,1},{8,10},{9,11},{10,... | collective-permute-start | bytes 1179656 | tf_op jit(solution)/shard_map/ppermute | solution.py:184
  109.2 30.0 %collective-permute-start.46 = (bf16[192,1024]{1,0:T(8,128)(2,1)S(1)}, bf16[192,1024]{1,0:T(8,128)(2,1)}, u32[]{:S(2)}, u32[]{:S(2)}) collective-permute-start(bf16[192,1024]{1,0:T(8,128)(2,1)S(1)} %collective-permute-done.34.refs_16_), channel_id=1, source_target_pairs={{0,16},{1,17},{2,18},{3,19},{4,20},{5,21},{6,22},{7,23},{8,24},{9,... | collective-permute-start | bytes 1179656 | tf_op jit(solution)/shard_map/ppermute | solution.py:184
  127.8 21.7 %collective-permute-start.47 = (bf16[192,1024]{1,0:T(8,128)(2,1)S(1)}, bf16[192,1024]{1,0:T(8,128)(2,1)S(1)}, u32[]{:S(2)}, u32[]{:S(2)}) collective-permute-start(bf16[192,1024]{1,0:T(8,128)(2,1)S(1)} %collective-permute-done.43.refs_20_), channel_id=1, source_target_pairs={{0,16},{1,17},{2,18},{3,19},{4,20},{5,21},{6,22},{7,23},{8,24},{9,... | collective-permute-start | bytes 1179656 | tf_op jit(solution)/shard_map/ppermute | solution.py:184
  129.2 30.2 %collective-permute-start.48 = (bf16[2,512,512]{2,1,0:T(8,128)(2,1)S(1)}, bf16[2,512,512]{2,1,0:T(8,128)(2,1)}, u32[]{:S(2)}, u32[]{:S(2)}) collective-permute-start(bf16[2,512,512]{2,1,0:T(8,128)(2,1)S(1)} %shard_map.111.refs_1_), channel_id=1, source_target_pairs={{0,2},{1,3},{2,4},{3,5},{4,6},{5,7},{6,8},{7,9},{8,10},{9,11},{10,... | collective-permute-start | bytes 3145736 | tf_op jit(solution)/shard_map/ppermute | solution.py:184
  139.3 12.2 %collective-permute-start.50 = (bf16[192,1024]{1,0:T(8,128)(2,1)S(1)}, bf16[192,1024]{1,0:T(8,128)(2,1)S(1)}, u32[]{:S(2)}, u32[]{:S(2)}) collective-permute-start(bf16[192,1024]{1,0:T(8,128)(2,1)S(1)} %copy-done.39), channel_id=1, source_target_pairs={{0,8},{1,9},{2,10},{3,11},{4,12},{5,13},{6,14},{7,15},{8,0},{9,1},... | collective-permute-start | bytes 1179656 | tf_op jit(solution)/shard_map/ppermute | solution.py:184
  139.8 12.2 %collective-permute-start.51 = (bf16[192,1024]{1,0:T(8,128)(2,1)S(1)}, bf16[192,1024]{1,0:T(8,128)(2,1)S(1)}, u32[]{:S(2)}, u32[]{:S(2)}) collective-permute-start(bf16[192,1024]{1,0:T(8,128)(2,1)S(1)} %collective-permute-done.34.refs_16_), channel_id=1, source_target_pairs={{0,8},{1,9},{2,10},{3,11},{4,12},{5,13},{6,14},{7,15},{8,0},{9,1},... | collective-permute-start | bytes 1179656 | tf_op jit(solution)/shard_map/ppermute | solution.py:184
  149.5 35.2 %collective-permute-start.57 = (bf16[2,512,512]{2,1,0:T(8,128)(2,1)S(1)}, bf16[2,512,512]{2,1,0:T(8,128)(2,1)}, u32[]{:S(2)}, u32[]{:S(2)}) collective-permute-start(bf16[2,512,512]{2,1,0:T(8,128)(2,1)S(1)} %shard_map.112.refs_1_), channel_id=1, source_target_pairs={{0,2},{1,3},{2,4},{3,5},{4,6},{5,7},{6,8},{7,9},{8,10},{9,11},{10,... | collective-permute-start | bytes 3145736 | tf_op jit(solution)/shard_map/ppermute | solution.py:184
  175.9 25.0 %collective-permute-start.58 = (bf16[512,512]{1,0:T(8,128)(2,1)}, bf16[512,512]{1,0:T(8,128)(2,1)}, u32[]{:S(2)}, u32[]{:S(2)}) collective-permute-start(bf16[512,512]{1,0:T(8,128)(2,1)} %shard_map.114), channel_id=1, source_target_pairs={{0,1},{1,0},{2,3},{3,2},{4,5},{5,4},{6,7},{7,6},{8,9},{9,8},{10,11... | collective-permute-start | bytes 1572872 | tf_op jit(solution)/shard_map/ppermute | solution.py:184
  190.5 14.3 %collective-permute-start.59 = (bf16[512,512]{1,0:T(8,128)(2,1)}, bf16[512,512]{1,0:T(8,128)(2,1)}, u32[]{:S(2)}, u32[]{:S(2)}) collective-permute-start(bf16[512,512]{1,0:T(8,128)(2,1)} %shard_map.116), channel_id=1, source_target_pairs={{0,1},{1,0},{2,3},{3,2},{4,5},{5,4},{6,7},{7,6},{8,9},{9,8},{10,11... | collective-permute-start | bytes 1572872 | tf_op jit(solution)/shard_map/ppermute | solution.py:184
  (84 other events, 1155.7 us)

commit v4 on v3

--- a/solution.py
+++ b/solution.py
@@ -201,15 +201,21 @@
         copy.wait()
 
 
-def masked_ranks(scalars, ids, down, normed, out, count):
-    deep = out.shape[0]
-    every = lax.dot_general(
-        down[...], normed[...], (((1,), (1,)), ((), ())), preferred_element_type=F32
-    )
+def masked_ranks(scalars, ids, down, normed, out, count, waits=((),)):
+    deep, share = out.shape[0], count // len(waits)
     total = jnp.zeros(out.shape, F32)
-    for i in range(count):
-        mine = ids[...] == scalars[DOWN_ID, i]
-        total = total + jnp.where(mine, every[i * deep : (i + 1) * deep], 0.0)
+    for part, copies in enumerate(waits):
+        for copy in copies:
+            copy.wait()
+        every = lax.dot_general(
+            down[part * share * deep : (part + 1) * share * deep],
+            normed[...],
+            (((1,), (1,)), ((), ())),
+            preferred_element_type=F32,
+        )
+        for i in range(share):
+            mine = ids[...] == scalars[DOWN_ID, part * share + i]
+            total = total + jnp.where(mine, every[i * deep : (i + 1) * deep], 0.0)
     out[...] = total.astype(BF16)
 
 
@@ -230,9 +236,7 @@
     ]
     for copy in copies:
         copy.start()
-    for copy in copies:
-        copy.wait()
-    masked_ranks(scalars, ids, down, normed, out, count)
+    masked_ranks(scalars, ids, down, normed, out, count, (copies[: count // 2], copies[count // 2 :]))
 
 
 def first_ranks(scalars, ids, normed, pieces):

time: 210 us -> 210 us (level)
  no operation moved by 1% of the time
where the time goes in v4:
time: 210 us; the launch traced here: 207 us
  waiting for transfers between devices  68.8 us (33%)
  Pallas kernels  57.8 us (28%)
  starting transfers between devices  51.7 us (25%)
  local copies, waits for them, and re-layouts  17.6 us (8%)
  other arithmetic  10.5 us (5%)
    ppermute x60, waiting for transfers between devices, route(): return lax.ppermute(value, ('dp', 'adapter'), pairs)  68.8 us
    ppermute x60, starting transfers between devices, route(): return lax.ppermute(value, ('dp', 'adapter'), pairs)  51.7 us
    pallas_call x2, Pallas kernels, queries_of(): pl.pallas_call(functools.partial(query_kernel, count, inner, head), out_s...  17.3 us
    pallas_call x4, Pallas kernels, attend(): pl.pallas_call(attend_kernel, grid=(1,), out_shape=jax.ShapeDtypeStruct((...  16.1 us
    pallas_call x2, Pallas kernels, keys_values(): pl.pallas_call(functools.partial(kv_kernel, pieces, inner, head), out_sha...  12.1 us
    unnamed x112, local copies, waits for them, and re-layouts  9.95 us
    pallas_call x1, Pallas kernels, first_ranks(): pl.pallas_call(functools.partial(first_rank_kernel, pieces), out_shape=[j...  6.75 us
    reduce_sum x2, other arithmetic, row_norm(): scale = lax.rsqrt(jnp.mean(values * values, axis=-1, keepdims=True) + 1e-06)  4.33 us
  transfers between devices with their start and end apart: 60, of which 22 were waited for; matrix products, arithmetic and copies ran while one was open for 8% of the time, Pallas kernels for 27%

profile of v4, /device:TPU:6, one launch (start us, length us, event | category | flops | bytes accessed | tf_op | source)
XLA Modules:
  0.0 207.4 jit_solution(3538931097001154335)
XLA Ops:
  4.2 5.2 %collective-permute-start.2 = (bf16[320,512]{1,0:T(8,128)(2,1)S(1)}, bf16[320,512]{1,0:T(8,128)(2,1)S(1)}, u32[]{:S(2)}, u32[]{:S(2)}) collective-permute-start(bf16[320,512]{1,0:T(8,128)(2,1)S(1)} %constant_dynamic-slice_fusion), channel_id=1, source_target_pairs={{16,1},{17,0},{18,3},{19,2},{20,5},{21,4},{22,7},{23,6},{24,9},{25... | collective-permute-start | bytes 983048 | tf_op jit(solution)/shard_map/ppermute | solution.py:184
  15.8 3.1 %collective-permute-done.3 = bf16[16,2048]{1,0:T(8,128)(2,1)S(1)} collective-permute-done((bf16[16,2048]{1,0:T(8,128)(2,1)S(1)}, bf16[16,2048]{1,0:T(8,128)(2,1)S(1)}, u32[]{:S(2)}, u32[]{:S(2)}) %collective-permute-start.3) | collective-permute-done | bytes 65568 | tf_op jit(solution)/shard_map/ppermute | solution.py:184
  22.1 3.2 %fusion.14 = (bf16[128,2560]{1,0:T(8,128)(2,1)}, bf16[128,2560]{1,0:T(8,128)(2,1)}, bf16[128,2560]{1,0:T(8,128)(2,1)}, bf16[128,2560]{1,0:T(8,128)(2,1)}) fusion(bf16[512,2560]{1,0:T(8,128)(2,1)} %param.11), kind=kLoop, calls=%fused_computation.63 | loop fusion | bytes 5242880 | tf_op jit(solution)/shard_map/split | solution.py:629
  30.6 3.6 %collective-permute-done.12.refs_12_ = bf16[384,512]{1,0:T(8,128)(2,1)S(1)} collective-permute-done((bf16[384,512]{1,0:T(8,128)(2,1)S(1)}, bf16[384,512]{1,0:T(8,128)(2,1)S(1)}, u32[]{:S(2)}, u32[]{:S(2)}) %collective-permute-start.12) | collective-permute-done | bytes 393248 | tf_op jit(solution)/shard_map/ppermute | solution.py:184
  36.1 3.0 %collective-permute-done.13.refs_9_ = bf16[384,512]{1,0:T(8,128)(2,1)S(1)} collective-permute-done((bf16[384,512]{1,0:T(8,128)(2,1)S(1)}, bf16[384,512]{1,0:T(8,128)(2,1)S(1)}, u32[]{:S(2)}, u32[]{:S(2)}) %collective-permute-start.13) | collective-permute-done | bytes 393248 | tf_op jit(solution)/shard_map/ppermute | solution.py:184
  40.7 2.1 collective-permute-start.21
  46.0 2.3 %fusion.3 = f32[512]{0:T(512)S(1)} fusion(bf16[512,2560]{1,0:T(8,128)(2,1)} %param.11), kind=kLoop, calls=%fused_computation.7 | loop fusion | flops 3931648 | bytes 2623488 | tf_op jit(solution)/shard_map/reduce_sum | solution.py:193
  48.3 4.4 %collective-permute-done.20.refs_16_ = bf16[384,512]{1,0:T(8,128)(2,1)S(1)} collective-permute-done((bf16[384,512]{1,0:T(8,128)(2,1)S(1)}, bf16[384,512]{1,0:T(8,128)(2,1)S(1)}, u32[]{:S(2)}, u32[]{:S(2)}) %collective-permute-start.20) | collective-permute-done | bytes 393248 | tf_op jit(solution)/shard_map/ppermute | solution.py:184
  54.3 2.1 collective-permute-start.27
  62.9 3.7 %collective-permute-done.26.refs_20_ = bf16[384,512]{1,0:T(8,128)(2,1)} collective-permute-done((bf16[384,512]{1,0:T(8,128)(2,1)S(1)}, bf16[384,512]{1,0:T(8,128)(2,1)}, u32[]{:S(2)}, u32[]{:S(2)}) %collective-permute-start.26) | collective-permute-done | bytes 393248 | tf_op jit(solution)/shard_map/ppermute | solution.py:184
  69.1 2.3 %collective-permute-done.17.refs_12_ = bf16[48,2560]{1,0:T(8,128)(2,1)} collective-permute-done((bf16[48,2560]{1,0:T(8,128)(2,1)S(1)}, bf16[48,2560]{1,0:T(8,128)(2,1)}, u32[]{:S(2)}, u32[]{:S(2)}) %collective-permute-start.17) | collective-permute-done | bytes 245792 | tf_op jit(solution)/shard_map/ppermute | solution.py:184
  71.8 2.0 collective-permute-done.18.refs_9_
  75.8 6.6 %collective-permute-done.16.refs_12_ = bf16[192,1024]{1,0:T(8,128)(2,1)S(1)} collective-permute-done((bf16[192,1024]{1,0:T(8,128)(2,1)S(1)}, bf16[192,1024]{1,0:T(8,128)(2,1)S(1)}, u32[]{:S(2)}, u32[]{:S(2)}) %collective-permute-start.16) | collective-permute-done | bytes 393248 | tf_op jit(solution)/shard_map/ppermute | solution.py:184
  84.1 6.3 %collective-permute-done.24.refs_13_ = bf16[48,2560]{1,0:T(8,128)(2,1)} collective-permute-done((bf16[48,2560]{1,0:T(8,128)(2,1)}, bf16[48,2560]{1,0:T(8,128)(2,1)}, u32[]{:S(2)}, u32[]{:S(2)}) %collective-permute-start.24) | collective-permute-done | bytes 245792 | tf_op jit(solution)/shard_map/ppermute | solution.py:184
  94.9 2.6 %fusion.5 = (bf16[512,2560]{1,0:T(8,128)(2,1)S(1)}, bf16[512,2560]{1,0:T(8,128)(2,1)S(1)}) fusion(bf16[512,2560]{1,0:T(8,128)(2,1)S(1)} %copy-done.34, f32[512]{0:T(512)S(1)} %add_rsqrt_fusion, f32[2560]{0:T(1024)S(1)} %copy-done.51, f32[512]{0:T(512)S(1)} %add_rsqrt_fusion.1, bf16[128,2560]{1,0:T(8,128)(2,1)} %collective-permute-done.29, ...), kind=kLoop, calls=%fused_computation.9 | loop fusion | flops 19660800 | bytes 10500096 | tf_op jit(solution)/shard_map/convert_element_type | solution.py:194
  97.7 6.8 %shard_map.109 = (bf16[48,512]{1,0:T(8,128)(2,1)S(1)}, bf16[768,2560]{1,0:T(8,128)(2,1)S(1)}) custom-call(s32[6,16]{1,0:T(8,128)S(1)} %stack.75.scalars.refs_0_, s32[1,512]{1,0:T(1,128)S(1)} %bitcast.42, bf16[512,2560]{1,0:T(8,128)(2,1)S(1)} %get-tuple-element.156.normed.refs_6_, bf16[48,2560]{1,0:T(8,128)(2,1)S(1)} %dynamic-slice_bitcast_fusion.refs_0_, ...), custom_call_target="tpu_custom_call" | custom-call | flops 1 | bytes 1 | tf_op jit(solution)/shard_map/pallas_call | solution.py:245
  104.5 2.7 %collective-permute-done.34.refs_16_ = bf16[192,1024]{1,0:T(8,128)(2,1)S(1)} collective-permute-done((bf16[192,1024]{1,0:T(8,128)(2,1)}, bf16[192,1024]{1,0:T(8,128)(2,1)S(1)}, u32[]{:S(2)}, u32[]{:S(2)}) %collective-permute-start.34) | collective-permute-done | bytes 393248 | tf_op jit(solution)/shard_map/ppermute | solution.py:184
  110.7 2.8 %shard_map.110.refs_4_ = bf16[2,48,512]{2,1,0:T(8,128)(2,1)S(1)} custom-call(s32[6,16]{1,0:T(8,128)S(1)} %stack.75.scalars.refs_0_, s32[1,512]{1,0:T(1,128)S(1)} %get-tuple-element.163.ids.refs_2_, bf16[512,2560]{1,0:T(8,128)(2,1)S(1)} %get-tuple-element.157.normed.refs_7_, bf16[768,2560]{1,0:T(8,128)(2,1)S(1)} %get-tuple-element.96.down, ...), custom_call_target="tpu_custom_call" | custom-call | flops 1 | bytes 1 | tf_op jit(solution)/shard_map/pallas_call | solution.py:261
  113.9 4.3 %collective-permute-done.35.refs_5_ = bf16[2,48,512]{2,1,0:T(8,128)(2,1)S(1)} collective-permute-done((bf16[2,48,512]{2,1,0:T(8,128)(2,1)S(1)}, bf16[2,48,512]{2,1,0:T(8,128)(2,1)S(1)}, u32[]{:S(2)}, u32[]{:S(2)}) %collective-permute-start.35) | collective-permute-done | bytes 98336 | tf_op jit(solution)/shard_map/ppermute | solution.py:184
  118.2 2.6 %collective-permute-start.42 = (s32[1024]{0:T(1024)S(1)}, s32[1024]{0:T(1024)S(1)}, u32[]{:S(2)}, u32[]{:S(2)}) collective-permute-start(s32[1024]{0:T(1024)S(1)} %add_select_fusion), channel_id=1, source_target_pairs={{0,2},{1,3},{2,4},{3,5},{4,6},{5,7},{6,8},{7,9},{8,10},{9,11},{10,... | collective-permute-start | bytes 12296 | tf_op jit(solution)/shard_map/ppermute | solution.py:184
  120.9 6.1 %shard_map.111.refs_1_ = bf16[2,512,512]{2,1,0:T(8,128)(2,1)S(1)} custom-call(s32[6,16]{1,0:T(8,128)S(1)} %stack.75.scalars.refs_0_, s32[1,512]{1,0:T(1,128)S(1)} %bitcast.43, s32[1,512]{1,0:T(1,128)S(1)} %get-tuple-element.163.ids.refs_2_, f32[2,256]{1,0:T(2,128)S(1)} %copy-done.33, bf16[2,48,512]{2,1,0:T(8,128)(2,1)S(1)} %shard_map.110.refs_4_, ...), custom_call_target="tpu_custom_call" | custom-call | flops 1 | bytes 1 | tf_op jit(solution)/shard_map/pallas_call | solution.py:349
  133.1 6.0 %shard_map.112.refs_1_ = bf16[2,512,512]{2,1,0:T(8,128)(2,1)S(1)} custom-call(s32[6,16]{1,0:T(8,128)S(1)} %stack.75.scalars.refs_0_, s32[1,512]{1,0:T(1,128)S(1)} %bitcast.44, s32[1,512]{1,0:T(1,128)S(1)} %get-tuple-element.163.ids.refs_2_, f32[2,256]{1,0:T(2,128)S(1)} %copy-done.33, bf16[2,48,512]{2,1,0:T(8,128)(2,1)S(1)} %shard_map.110.refs_4_, ...), custom_call_target="tpu_custom_call" | custom-call | flops 1 | bytes 1 | tf_op jit(solution)/shard_map/pallas_call | solution.py:349
  139.8 9.6 %collective-permute-done.47.refs_21_ = bf16[192,1024]{1,0:T(8,128)(2,1)S(1)} collective-permute-done((bf16[192,1024]{1,0:T(8,128)(2,1)S(1)}, bf16[192,1024]{1,0:T(8,128)(2,1)S(1)}, u32[]{:S(2)}, u32[]{:S(2)}) %collective-permute-start.47) | collective-permute-done | bytes 393248 | tf_op jit(solution)/shard_map/ppermute | solution.py:184
  155.6 3.8 %collective-permute-done.48.refs_0_ = bf16[2,512,512]{2,1,0:T(8,128)(2,1)} collective-permute-done((bf16[2,512,512]{2,1,0:T(8,128)(2,1)S(1)}, bf16[2,512,512]{2,1,0:T(8,128)(2,1)}, u32[]{:S(2)}, u32[]{:S(2)}) %collective-permute-start.48) | collective-permute-done | bytes 1048608 | tf_op jit(solution)/shard_map/ppermute | solution.py:184
  161.4 8.7 %shard_map.113.queries = bf16[2,512,512]{2,1,0:T(8,128)(2,1)} custom-call(s32[6,16]{1,0:T(8,128)} %copy-done.30, s32[1,512]{1,0:T(1,128)} %bitcast.40, s32[1,512]{1,0:T(1,128)} %copy-done.32, f32[2,256]{1,0:T(2,128)} %refs_3_.7, bf16[2,48,512]{2,1,0:T(8,128)(2,1)} %copy-done.7, bf16[2,48,512]{2,1,0:T(8,128)(2,1)} %copy-done.8, bf16[512,2560]{1,0:T(8,128)(2,1)} %copy-done.1, ...), custom_call_target="tpu_custom_call" | custom-call | flops 1 | bytes 1 | tf_op jit(solution)/shard_map/pallas_call | solution.py:414
  171.3 4.5 %shard_map.114 = bf16[512,512]{1,0:T(8,128)(2,1)} custom-call(s32[4]{0:T(128)S(1)} %get-tuple-element.137.places, bf16[2,512,512]{2,1,0:T(8,128)(2,1)S(1)} %copy-done.3, s32[512,1]{1,0:T(8,128)S(1)} %copy.12.seg_rows, s32[1,1536]{1,0:T(1,128)S(1)} %broadcast_in_dim.32.seg_keys, bf16[2,512,512]{2,1,0:T(8,128)(2,1)} %collective-permute-done.48.refs_0_, ...), custom_call_target="tpu_custom_call" | custom-call | flops 1 | bytes 1 | tf_op jit(solution)/shard_map/pallas_call | solution.py:492
  176.1 8.7 %shard_map.115.queries = bf16[2,512,512]{2,1,0:T(8,128)(2,1)} custom-call(s32[6,16]{1,0:T(8,128)} %copy-done.30, s32[1,512]{1,0:T(1,128)} %bitcast.41, s32[1,512]{1,0:T(1,128)} %copy-done.32, f32[2,256]{1,0:T(2,128)} %refs_3_.7, bf16[2,48,512]{2,1,0:T(8,128)(2,1)} %copy-done.7, bf16[2,48,512]{2,1,0:T(8,128)(2,1)} %copy-done.8, bf16[512,2560]{1,0:T(8,128)(2,1)} %copy-done.1, ...), custom_call_target="tpu_custom_call" | custom-call | flops 1 | bytes 1 | tf_op jit(solution)/shard_map/pallas_call | solution.py:414
  186.0 4.5 %shard_map.116 = bf16[512,512]{1,0:T(8,128)(2,1)} custom-call(s32[4]{0:T(128)S(1)} %get-tuple-element.137.places, bf16[2,512,512]{2,1,0:T(8,128)(2,1)S(1)} %copy-done.5, s32[512,1]{1,0:T(8,128)S(1)} %copy.12.seg_rows, s32[1,1536]{1,0:T(1,128)S(1)} %broadcast_in_dim.32.seg_keys, bf16[2,512,512]{2,1,0:T(8,128)(2,1)} %collective-permute-done.57.refs_0_, ...), custom_call_target="tpu_custom_call" | custom-call | flops 1 | bytes 1 | tf_op jit(solution)/shard_map/pallas_call | solution.py:492
  193.8 3.6 %shard_map.117.refs_0_ = bf16[512,512]{1,0:T(8,128)(2,1)S(1)} custom-call(s32[4]{0:T(128)S(1)} %broadcast_subtract_fusion.1.places, bf16[2,512,512]{2,1,0:T(8,128)(2,1)S(1)} %copy-done.4, s32[512,1]{1,0:T(8,128)S(1)} %copy.14.seg_rows, s32[1,1536]{1,0:T(1,128)S(1)} %broadcast_in_dim.34.seg_keys, bf16[2,512,512]{2,1,0:T(8,128)(2,1)} %collective-permute-done.48.refs_0_, ...), custom_call_target="tpu_custom_call" | custom-call | flops 1 | bytes 1 | tf_op jit(solution)/shard_map/pallas_call | solution.py:492
  197.3 3.6 %shard_map.118.refs_1_ = bf16[512,512]{1,0:T(8,128)(2,1)S(1)} custom-call(s32[4]{0:T(128)S(1)} %broadcast_subtract_fusion.1.places, bf16[2,512,512]{2,1,0:T(8,128)(2,1)S(1)} %copy-done.6, s32[512,1]{1,0:T(8,128)S(1)} %copy.14.seg_rows, s32[1,1536]{1,0:T(1,128)S(1)} %broadcast_in_dim.34.seg_keys, bf16[2,512,512]{2,1,0:T(8,128)(2,1)} %collective-permute-done.57.refs_0_, ...), custom_call_target="tpu_custom_call" | custom-call | flops 1 | bytes 1 | tf_op jit(solution)/shard_map/pallas_call | solution.py:492
  200.9 3.8 %collective-permute-done.59.refs_3_ = bf16[512,512]{1,0:T(8,128)(2,1)} collective-permute-done((bf16[512,512]{1,0:T(8,128)(2,1)}, bf16[512,512]{1,0:T(8,128)(2,1)}, u32[]{:S(2)}, u32[]{:S(2)}) %collective-permute-start.59) | collective-permute-done | bytes 524320 | tf_op jit(solution)/shard_map/ppermute | solution.py:184
  204.7 2.7 %shard_map.119 = bf16[512,2048]{1,0:T(8,128)(2,1)} custom-call(s32[4]{0:T(128)S(1)} %pad_add_fusion.1.where, bf16[512,512]{1,0:T(8,128)(2,1)S(1)} %shard_map.117.refs_0_, bf16[512,512]{1,0:T(8,128)(2,1)S(1)} %shard_map.118.refs_1_, bf16[512,512]{1,0:T(8,128)(2,1)} %collective-permute-done.58.refs_2_, bf16[512,512]{1,0:T(8,128)(2,1)} %collective-permute-done.59.refs_3_), custom_call_target="tpu_custom_call" | custom-call | flops 1 | bytes 1 | tf_op jit(solution)/shard_map/pallas_call | solution.py:525
  (247 shorter events, 69.2 us)
Async XLA Ops:
  1.2 19.6 %collective-permute-start = (bf16[160,1024]{1,0:T(8,128)(2,1)S(1)}, bf16[160,1024]{1,0:T(8,128)(2,1)S(1)}, u32[]{:S(2)}, u32[]{:S(2)}) collective-permute-start(bf16[160,1024]{1,0:T(8,128)(2,1)S(1)} %get-tuple-element.147), channel_id=1, source_target_pairs={{1,8},{3,10},{5,12},{7,14},{8,1},{10,3},{12,5},{14,7}} | collective-permute-start | bytes 983048 | tf_op jit(solution)/shard_map/ppermute | solution.py:184
  1.9 18.9 %collective-permute-start.1 = (bf16[160,1024]{1,0:T(8,128)(2,1)S(1)}, bf16[160,1024]{1,0:T(8,128)(2,1)}, u32[]{:S(2)}, u32[]{:S(2)}) collective-permute-start(bf16[160,1024]{1,0:T(8,128)(2,1)S(1)} %get-tuple-element.146), channel_id=1, source_target_pairs={{0,16},{1,24},{2,18},{3,26},{4,20},{5,28},{6,22},{7,30},{8,17},{9,... | collective-permute-start | bytes 983048 | tf_op jit(solution)/shard_map/ppermute | solution.py:184
  4.2 16.6 %collective-permute-start.2 = (bf16[320,512]{1,0:T(8,128)(2,1)S(1)}, bf16[320,512]{1,0:T(8,128)(2,1)S(1)}, u32[]{:S(2)}, u32[]{:S(2)}) collective-permute-start(bf16[320,512]{1,0:T(8,128)(2,1)S(1)} %constant_dynamic-slice_fusion), channel_id=1, source_target_pairs={{16,1},{17,0},{18,3},{19,2},{20,5},{21,4},{22,7},{23,6},{24,9},{25... | collective-permute-start | bytes 983048 | tf_op jit(solution)/shard_map/ppermute | solution.py:184
  22.1 12.1 %collective-permute-start.12 = (bf16[384,512]{1,0:T(8,128)(2,1)S(1)}, bf16[384,512]{1,0:T(8,128)(2,1)S(1)}, u32[]{:S(2)}, u32[]{:S(2)}) collective-permute-start(bf16[384,512]{1,0:T(8,128)(2,1)S(1)} %fusion.6.refs_8_), channel_id=1, source_target_pairs={{0,2},{1,3},{2,4},{3,5},{4,6},{5,7},{6,0},{7,1},{8,10},{9,11},{10,... | collective-permute-start | bytes 1179656 | tf_op jit(solution)/shard_map/ppermute | solution.py:184
  25.4 19.3 %collective-permute-start.9 = (bf16[128,2560]{1,0:T(8,128)(2,1)}, bf16[128,2560]{1,0:T(8,128)(2,1)}, u32[]{:S(2)}, u32[]{:S(2)}) collective-permute-start(bf16[128,2560]{1,0:T(8,128)(2,1)} %get-tuple-element.145), channel_id=1, source_target_pairs={{0,1},{1,0},{2,3},{3,2},{4,5},{5,4},{6,7},{7,6},{8,9},{9,8},{10,11... | collective-permute-start | bytes 1966088 | tf_op jit(solution)/shard_map/ppermute | solution.py:184
  27.1 12.0 %collective-permute-start.13 = (bf16[384,512]{1,0:T(8,128)(2,1)S(1)}, bf16[384,512]{1,0:T(8,128)(2,1)S(1)}, u32[]{:S(2)}, u32[]{:S(2)}) collective-permute-start(bf16[384,512]{1,0:T(8,128)(2,1)S(1)} %fusion.6.refs_8_), channel_id=1, source_target_pairs={{0,16},{1,17},{2,18},{3,19},{4,20},{5,21},{6,22},{7,23},{8,24},{9,... | collective-permute-start | bytes 1179656 | tf_op jit(solution)/shard_map/ppermute | solution.py:184
  29.0 11.6 %collective-permute-start.6 = (bf16[48,2560]{1,0:T(8,128)(2,1)S(1)}, bf16[48,2560]{1,0:T(8,128)(2,1)S(1)}, u32[]{:S(2)}, u32[]{:S(2)}) collective-permute-start(bf16[48,2560]{1,0:T(8,128)(2,1)S(1)} %collective-permute-done.5.refs_4_), channel_id=1, source_target_pairs={{0,2},{1,3},{2,4},{3,5},{4,6},{5,7},{6,0},{7,1},{8,10},{9,11},{10,... | collective-permute-start | bytes 737288 | tf_op jit(solution)/shard_map/ppermute | solution.py:184
  39.1 13.6 %collective-permute-start.20 = (bf16[384,512]{1,0:T(8,128)(2,1)S(1)}, bf16[384,512]{1,0:T(8,128)(2,1)S(1)}, u32[]{:S(2)}, u32[]{:S(2)}) collective-permute-start(bf16[384,512]{1,0:T(8,128)(2,1)S(1)} %collective-permute-done.12.refs_12_), channel_id=1, source_target_pairs={{0,2},{1,3},{2,4},{3,5},{4,6},{5,7},{6,0},{7,1},{8,10},{9,11},{10,... | collective-permute-start | bytes 1179656 | tf_op jit(solution)/shard_map/ppermute | solution.py:184
  40.7 12.1 %collective-permute-start.21 = (bf16[384,512]{1,0:T(8,128)(2,1)S(1)}, bf16[384,512]{1,0:T(8,128)(2,1)}, u32[]{:S(2)}, u32[]{:S(2)}) collective-permute-start(bf16[384,512]{1,0:T(8,128)(2,1)S(1)} %collective-permute-done.12.refs_12_), channel_id=1, source_target_pairs={{0,16},{1,17},{2,18},{3,19},{4,20},{5,21},{6,22},{7,23},{8,24},{9,... | collective-permute-start | bytes 1179656 | tf_op jit(solution)/shard_map/ppermute | solution.py:184
  43.8 17.5 %collective-permute-start.15 = (bf16[128,2560]{1,0:T(8,128)(2,1)}, bf16[128,2560]{1,0:T(8,128)(2,1)}, u32[]{:S(2)}, u32[]{:S(2)}) collective-permute-start(bf16[128,2560]{1,0:T(8,128)(2,1)} %get-tuple-element.81), channel_id=1, source_target_pairs={{0,1},{1,0},{2,3},{3,2},{4,5},{5,4},{6,7},{7,6},{8,9},{9,8},{10,11... | collective-permute-start | bytes 1966088 | tf_op jit(solution)/shard_map/ppermute | solution.py:184
  44.7 13.2 %collective-permute-start.10 = (bf16[48,2560]{1,0:T(8,128)(2,1)S(1)}, bf16[48,2560]{1,0:T(8,128)(2,1)S(1)}, u32[]{:S(2)}, u32[]{:S(2)}) collective-permute-start(bf16[48,2560]{1,0:T(8,128)(2,1)S(1)} %collective-permute-done.5.refs_4_), channel_id=1, source_target_pairs={{0,16},{1,17},{2,18},{3,19},{4,20},{5,21},{6,22},{7,23},{8,24},{9,... | collective-permute-start | bytes 737288 | tf_op jit(solution)/shard_map/ppermute | solution.py:184
  52.8 13.9 %collective-permute-start.26 = (bf16[384,512]{1,0:T(8,128)(2,1)S(1)}, bf16[384,512]{1,0:T(8,128)(2,1)}, u32[]{:S(2)}, u32[]{:S(2)}) collective-permute-start(bf16[384,512]{1,0:T(8,128)(2,1)S(1)} %collective-permute-done.20.refs_16_), channel_id=1, source_target_pairs={{0,2},{1,3},{2,4},{3,5},{4,6},{5,7},{6,0},{7,1},{8,10},{9,11},{10,... | collective-permute-start | bytes 1179656 | tf_op jit(solution)/shard_map/ppermute | solution.py:184
  54.3 14.1 %collective-permute-start.27 = (bf16[384,512]{1,0:T(8,128)(2,1)S(1)}, bf16[384,512]{1,0:T(8,128)(2,1)}, u32[]{:S(2)}, u32[]{:S(2)}) collective-permute-start(bf16[384,512]{1,0:T(8,128)(2,1)S(1)} %collective-permute-done.20.refs_16_), channel_id=1, source_target_pairs={{0,16},{1,17},{2,18},{3,19},{4,20},{5,21},{6,22},{7,23},{8,24},{9,... | collective-permute-start | bytes 1179656 | tf_op jit(solution)/shard_map/ppermute | solution.py:184
  59.2 23.2 %collective-permute-start.23 = (bf16[128,2560]{1,0:T(8,128)(2,1)S(1)}, bf16[128,2560]{1,0:T(8,128)(2,1)S(1)}, u32[]{:S(2)}, u32[]{:S(2)}) collective-permute-start(bf16[128,2560]{1,0:T(8,128)(2,1)S(1)} %copy-done.49), channel_id=1, source_target_pairs={{0,1},{1,0},{2,3},{3,2},{4,5},{5,4},{6,7},{7,6},{8,9},{9,8},{10,11... | collective-permute-start | bytes 1966088 | tf_op jit(solution)/shard_map/ppermute | solution.py:184
  69.1 13.3 %collective-permute-start.16 = (bf16[192,1024]{1,0:T(8,128)(2,1)S(1)}, bf16[192,1024]{1,0:T(8,128)(2,1)S(1)}, u32[]{:S(2)}, u32[]{:S(2)}) collective-permute-start(bf16[192,1024]{1,0:T(8,128)(2,1)S(1)} %pad_maximum_fusion.2.refs_8_), channel_id=1, source_target_pairs={{0,2},{1,3},{2,4},{3,5},{4,6},{5,7},{6,0},{7,1},{8,10},{9,11},{10,... | collective-permute-start | bytes 1179656 | tf_op jit(solution)/shard_map/ppermute | solution.py:184
  71.4 19.5 %collective-permute-start.29 = (bf16[128,2560]{1,0:T(8,128)(2,1)}, bf16[128,2560]{1,0:T(8,128)(2,1)}, u32[]{:S(2)}, u32[]{:S(2)}) collective-permute-start(bf16[128,2560]{1,0:T(8,128)(2,1)} %get-tuple-element.90), channel_id=1, source_target_pairs={{0,1},{1,0},{2,3},{3,2},{4,5},{5,4},{6,7},{7,6},{8,9},{9,8},{10,11... | collective-permute-start | bytes 1966088 | tf_op jit(solution)/shard_map/ppermute | solution.py:184
  83.6 25.0 %collective-permute-start.36 = (bf16[384,512]{1,0:T(8,128)(2,1)S(1)}, bf16[384,512]{1,0:T(8,128)(2,1)S(1)}, u32[]{:S(2)}, u32[]{:S(2)}) collective-permute-start(bf16[384,512]{1,0:T(8,128)(2,1)S(1)} %collective-permute-done.13.refs_9_), channel_id=1, source_target_pairs={{0,8},{1,9},{2,10},{3,11},{4,12},{5,13},{6,14},{7,15},{8,0},{9,1},... | collective-permute-start | bytes 1179656 | tf_op jit(solution)/shard_map/ppermute | solution.py:184
  93.1 16.1 %collective-permute-start.37 = (bf16[384,512]{1,0:T(8,128)(2,1)}, bf16[384,512]{1,0:T(8,128)(2,1)S(1)}, u32[]{:S(2)}, u32[]{:S(2)}) collective-permute-start(bf16[384,512]{1,0:T(8,128)(2,1)} %collective-permute-done.21.refs_13_), channel_id=1, source_target_pairs={{0,8},{1,9},{2,10},{3,11},{4,12},{5,13},{6,14},{7,15},{8,0},{9,1},... | collective-permute-start | bytes 1179656 | tf_op jit(solution)/shard_map/ppermute | solution.py:184
  93.6 15.6 %collective-permute-start.38 = (bf16[384,512]{1,0:T(8,128)(2,1)}, bf16[384,512]{1,0:T(8,128)(2,1)S(1)}, u32[]{:S(2)}, u32[]{:S(2)}) collective-permute-start(bf16[384,512]{1,0:T(8,128)(2,1)} %collective-permute-done.27.refs_17_), channel_id=1, source_target_pairs={{0,8},{1,9},{2,10},{3,11},{4,12},{5,13},{6,14},{7,15},{8,0},{9,1},... | collective-permute-start | bytes 1179656 | tf_op jit(solution)/shard_map/ppermute | solution.py:184
  93.7 13.5 %collective-permute-start.34 = (bf16[192,1024]{1,0:T(8,128)(2,1)}, bf16[192,1024]{1,0:T(8,128)(2,1)S(1)}, u32[]{:S(2)}, u32[]{:S(2)}) collective-permute-start(bf16[192,1024]{1,0:T(8,128)(2,1)} %copy-done.38), channel_id=1, source_target_pairs={{0,2},{1,3},{2,4},{3,5},{4,6},{5,7},{6,0},{7,1},{8,10},{9,11},{10,... | collective-permute-start | bytes 1179656 | tf_op jit(solution)/shard_map/ppermute | solution.py:184
  94.7 18.8 %collective-permute-start.41 = (bf16[384,512]{1,0:T(8,128)(2,1)}, bf16[384,512]{1,0:T(8,128)(2,1)S(1)}, u32[]{:S(2)}, u32[]{:S(2)}) collective-permute-start(bf16[384,512]{1,0:T(8,128)(2,1)} %collective-permute-done.39.refs_21_), channel_id=1, source_target_pairs={{0,8},{1,9},{2,10},{3,11},{4,12},{5,13},{6,14},{7,15},{8,0},{9,1},... | collective-permute-start | bytes 1179656 | tf_op jit(solution)/shard_map/ppermute | solution.py:184
  107.1 19.8 %collective-permute-start.45 = (bf16[192,1024]{1,0:T(8,128)(2,1)S(1)}, bf16[192,1024]{1,0:T(8,128)(2,1)}, u32[]{:S(2)}, u32[]{:S(2)}) collective-permute-start(bf16[192,1024]{1,0:T(8,128)(2,1)S(1)} %copy-done.39), channel_id=1, source_target_pairs={{0,16},{1,17},{2,18},{3,19},{4,20},{5,21},{6,22},{7,23},{8,24},{9,... | collective-permute-start | bytes 1179656 | tf_op jit(solution)/shard_map/ppermute | solution.py:184
  108.6 19.2 %collective-permute-start.44 = (bf16[192,1024]{1,0:T(8,128)(2,1)S(1)}, bf16[192,1024]{1,0:T(8,128)(2,1)}, u32[]{:S(2)}, u32[]{:S(2)}) collective-permute-start(bf16[192,1024]{1,0:T(8,128)(2,1)S(1)} %copy-done.36), channel_id=1, source_target_pairs={{0,16},{1,17},{2,18},{3,19},{4,20},{5,21},{6,22},{7,23},{8,24},{9,... | collective-permute-start | bytes 1179656 | tf_op jit(solution)/shard_map/ppermute | solution.py:184
  109.2 18.6 %collective-permute-start.43 = (bf16[192,1024]{1,0:T(8,128)(2,1)S(1)}, bf16[192,1024]{1,0:T(8,128)(2,1)S(1)}, u32[]{:S(2)}, u32[]{:S(2)}) collective-permute-start(bf16[192,1024]{1,0:T(8,128)(2,1)S(1)} %collective-permute-done.34.refs_16_), channel_id=1, source_target_pairs={{0,2},{1,3},{2,4},{3,5},{4,6},{5,7},{6,0},{7,1},{8,10},{9,11},{10,... | collective-permute-start | bytes 1179656 | tf_op jit(solution)/shard_map/ppermute | solution.py:184
  109.2 30.0 %collective-permute-start.46 = (bf16[192,1024]{1,0:T(8,128)(2,1)S(1)}, bf16[192,1024]{1,0:T(8,128)(2,1)}, u32[]{:S(2)}, u32[]{:S(2)}) collective-permute-start(bf16[192,1024]{1,0:T(8,128)(2,1)S(1)} %collective-permute-done.34.refs_16_), channel_id=1, source_target_pairs={{0,16},{1,17},{2,18},{3,19},{4,20},{5,21},{6,22},{7,23},{8,24},{9,... | collective-permute-start | bytes 1179656 | tf_op jit(solution)/shard_map/ppermute | solution.py:184
  127.8 21.7 %collective-permute-start.47 = (bf16[192,1024]{1,0:T(8,128)(2,1)S(1)}, bf16[192,1024]{1,0:T(8,128)(2,1)S(1)}, u32[]{:S(2)}, u32[]{:S(2)}) collective-permute-start(bf16[192,1024]{1,0:T(8,128)(2,1)S(1)} %collective-permute-done.43.refs_20_), channel_id=1, source_target_pairs={{0,16},{1,17},{2,18},{3,19},{4,20},{5,21},{6,22},{7,23},{8,24},{9,... | collective-permute-start | bytes 1179656 | tf_op jit(solution)/shard_map/ppermute | solution.py:184
  129.2 30.2 %collective-permute-start.48 = (bf16[2,512,512]{2,1,0:T(8,128)(2,1)S(1)}, bf16[2,512,512]{2,1,0:T(8,128)(2,1)}, u32[]{:S(2)}, u32[]{:S(2)}) collective-permute-start(bf16[2,512,512]{2,1,0:T(8,128)(2,1)S(1)} %shard_map.111.refs_1_), channel_id=1, source_target_pairs={{0,2},{1,3},{2,4},{3,5},{4,6},{5,7},{6,8},{7,9},{8,10},{9,11},{10,... | collective-permute-start | bytes 3145736 | tf_op jit(solution)/shard_map/ppermute | solution.py:184
  139.3 12.2 %collective-permute-start.50 = (bf16[192,1024]{1,0:T(8,128)(2,1)S(1)}, bf16[192,1024]{1,0:T(8,128)(2,1)S(1)}, u32[]{:S(2)}, u32[]{:S(2)}) collective-permute-start(bf16[192,1024]{1,0:T(8,128)(2,1)S(1)} %copy-done.39), channel_id=1, source_target_pairs={{0,8},{1,9},{2,10},{3,11},{4,12},{5,13},{6,14},{7,15},{8,0},{9,1},... | collective-permute-start | bytes 1179656 | tf_op jit(solution)/shard_map/ppermute | solution.py:184
  139.8 12.2 %collective-permute-start.51 = (bf16[192,1024]{1,0:T(8,128)(2,1)S(1)}, bf16[192,1024]{1,0:T(8,128)(2,1)S(1)}, u32[]{:S(2)}, u32[]{:S(2)}) collective-permute-start(bf16[192,1024]{1,0:T(8,128)(2,1)S(1)} %collective-permute-done.34.refs_16_), channel_id=1, source_target_pairs={{0,8},{1,9},{2,10},{3,11},{4,12},{5,13},{6,14},{7,15},{8,0},{9,1},... | collective-permute-start | bytes 1179656 | tf_op jit(solution)/shard_map/ppermute | solution.py:184
  149.5 35.2 %collective-permute-start.57 = (bf16[2,512,512]{2,1,0:T(8,128)(2,1)S(1)}, bf16[2,512,512]{2,1,0:T(8,128)(2,1)}, u32[]{:S(2)}, u32[]{:S(2)}) collective-permute-start(bf16[2,512,512]{2,1,0:T(8,128)(2,1)S(1)} %shard_map.112.refs_1_), channel_id=1, source_target_pairs={{0,2},{1,3},{2,4},{3,5},{4,6},{5,7},{6,8},{7,9},{8,10},{9,11},{10,... | collective-permute-start | bytes 3145736 | tf_op jit(solution)/shard_map/ppermute | solution.py:184
  175.9 25.0 %collective-permute-start.58 = (bf16[512,512]{1,0:T(8,128)(2,1)}, bf16[512,512]{1,0:T(8,128)(2,1)}, u32[]{:S(2)}, u32[]{:S(2)}) collective-permute-start(bf16[512,512]{1,0:T(8,128)(2,1)} %shard_map.114), channel_id=1, source_target_pairs={{0,1},{1,0},{2,3},{3,2},{4,5},{5,4},{6,7},{7,6},{8,9},{9,8},{10,11... | collective-permute-start | bytes 1572872 | tf_op jit(solution)/shard_map/ppermute | solution.py:184
  190.5 14.3 %collective-permute-start.59 = (bf16[512,512]{1,0:T(8,128)(2,1)}, bf16[512,512]{1,0:T(8,128)(2,1)}, u32[]{:S(2)}, u32[]{:S(2)}) collective-permute-start(bf16[512,512]{1,0:T(8,128)(2,1)} %shard_map.116), channel_id=1, source_target_pairs={{0,1},{1,0},{2,3},{3,2},{4,5},{5,4},{6,7},{7,6},{8,9},{9,8},{10,11... | collective-permute-start | bytes 1572872 | tf_op jit(solution)/shard_map/ppermute | solution.py:184
  (84 other events, 1159.1 us)

commit v5 on v4

--- a/solution.py
+++ b/solution.py
@@ -362,16 +362,16 @@
     )(scalars, ids_own, ids_nb, gains, *ranks, normed_own, normed_nb, *pieces.arrays)
 
 
-def query_kernel(count, inner, head, *refs):
-    scalars, ids_own, ids_nb, gains = refs[:4]
-    ranks, ranks_there = refs[4:6]
-    pieces = refs[8 : 8 + count]
-    out, weight, up, into, normed, sems = refs[8 + count :]
+def query_kernel(count, inner, start, sides, *refs):
+    scalars, gains, ranks, ranks_there = refs[:4]
+    ids, rows_in = refs[4 : 4 + len(sides)], refs[4 + len(sides) : 4 + 2 * len(sides)]
+    pieces = refs[4 + 2 * len(sides) : 4 + 2 * len(sides) + count]
+    out, weight, up, into, normed, sems = refs[4 + 2 * len(sides) + count :]
     deep = pieces[0].shape[0] - 2 * inner
-    columns = pl.ds(head * weight.shape[1], weight.shape[1])
+    columns = pl.ds(start, weight.shape[1])
     whole = [
-        pltpu.make_async_copy(refs[6 + side], normed.at[side], sems.at[2 * count + side])
-        for side in range(2)
+        pltpu.make_async_copy(rows_in[i], normed.at[i], sems.at[2 * count + i])
+        for i in range(len(sides))
     ]
     whole[0].start()
     copies = []
@@ -391,41 +391,40 @@
                 sems.at[2 * i + 1],
             )
         )
-    for copy in copies:
+    for copy in copies + whole[1:]:
         copy.start()
-    whole[1].start()
-    for side, ids in ((0, ids_own), (1, ids_nb)):
+    for i, side in enumerate(sides):
         both = ranks[side, 0:inner] + ranks_there[1 - side, 0:inner]
-        spread(both, ids, scalars, count, into.at[side])
+        spread(both, ids[i], scalars, count, into.at[i])
     for copy in copies:
         copy.wait()
-    for side in range(2):
-        whole[side].wait()
+    for i in range(len(sides)):
+        whole[i].wait()
         for at in range(weight.shape[1] // HEAD_DIM):
             cut = slice(at * HEAD_DIM, (at + 1) * HEAD_DIM)
-            block = project(normed[side], weight[:, cut], into[side], up[:, cut])
-            out[side, :, cut] = unit(block, gains[0:1, :])
-
-
-def queries_of(head, scalars, ids_own, ids_nb, gains, ranks, normed_own, normed_nb, pieces):
-    rows, width = normed_own.shape
-    count, inner = len(pieces), ranks[0].shape[1] // 3
-    columns = pieces[0].shape[1] // 2
+            block = project(normed[i], weight[:, cut], into[i], up[:, cut])
+            out[i, :, cut] = unit(block, gains[0:1, :])
+
+
+def queries_of(start, columns, sides, scalars, ids, gains, ranks, normed, pieces):
+    rows, width = normed[0].shape
+    count, inner, several = len(pieces), ranks[0].shape[1] // 3, len(sides)
+    chosen = [ids[side] for side in sides] + [normed[side] for side in sides]
     return pl.pallas_call(
-        functools.partial(query_kernel, count, inner, head),
-        out_shape=jax.ShapeDtypeStruct((2, rows, columns), BF16),
-        in_specs=[SMEM] + [VMEM] * 5 + [ANY] * (2 + count),
+        functools.partial(query_kernel, count, inner, start, sides),
+        out_shape=jax.ShapeDtypeStruct((several, rows, columns), BF16),
+        in_specs=[SMEM] + [VMEM] * (3 + several) + [ANY] * (several + count),
         out_specs=VMEM,
         scratch_shapes=[
             pltpu.VMEM((width, columns), BF16),
             pltpu.VMEM((2 * inner * count, columns), BF16),
-            pltpu.VMEM((2, 2 * inner * count, rows), BF16),
-            pltpu.VMEM((2, rows, width), BF16),
-            pltpu.SemaphoreType.DMA((2 * count + 2,)),
+            pltpu.VMEM((several, 2 * inner * count, rows), BF16),
+            pltpu.VMEM((several, rows, width), BF16),
+            pltpu.SemaphoreType.DMA((2 * count + several,)),
         ],
         compiler_params=params(56),
         cost_estimate=SMALL,
-    )(scalars, ids_own, ids_nb, gains, *ranks, normed_own, normed_nb, *pieces)
+    )(scalars, gains, *ranks, *chosen, *pieces)
 
 
 def attend_kernel(places, queries, seg_rows, seg_keys, *refs):
@@ -486,7 +485,7 @@
             ].astype(BF16)
 
 
-def attend(side, places, queries, seg_rows, seg_keys, blocks):
+def attend(at, places, queries, seg_rows, seg_keys, blocks):
     rows, width = queries.shape[1:]
     slots = seg_keys.shape[1] // rows
     return pl.pallas_call(
@@ -495,7 +494,7 @@
         out_shape=jax.ShapeDtypeStruct((rows, width), BF16),
         in_specs=[
             SMEM,
-            pl.BlockSpec((None, rows, width), lambda i: (side, 0, 0)),
+            pl.BlockSpec((None, rows, width), lambda i: (at, 0, 0)),
             pl.BlockSpec((rows, 1), lambda i: (0, 0)),
             pl.BlockSpec((1, slots * rows), lambda i: (0, 0)),
         ]
@@ -701,9 +700,13 @@
     q_x[3], arriving[0], q_c, q_xc = tied((q_x[3], arriving[0], q_c, q_xc))
     q_xc.append(swap_core(q_x[3]))
     q_pieces = flat(q, q_x, q_c, q_xc)
-    project_queries = lambda head, ranks: queries_of(
-        head, scalars, ids_own, ids_nb, gains, ranks, normed_own, normed_nb, q_pieces
-    )
+    def project_queries(head, sides, ranks):
+        width = half_q // len(kv_heads)
+        both_ids, both_rows = (ids_own, ids_nb), (normed_own, normed_nb)
+        return queries_of(
+            head * width, width, sides, scalars, both_ids, gains, ranks, both_rows, q_pieces
+        )
+
     seg_before = jnp.where((place == 0) & (z == 0), -1, seg_before)
     seg_span = jnp.concatenate([seg_before, seg_pair])
 
@@ -714,17 +717,18 @@
         places = jnp.stack([y, 1 - y, 2 + y, 3 - y]) - parity
         spans[name] = (places.astype(jnp.int32), seg_rows, seg_keys)
     where = jnp.stack([y, place, x, core]).astype(jnp.int32)
-    kept, got, queries, last = [], [], [], ranks
+    queries, got, last = [], [], ranks
     for head, both in enumerate(kv_heads):
-        queries.append(project_queries(head, last))
-        places, seg_rows, seg_keys = spans["nb"]
-        sent = attend(1, places, queries[head], seg_rows, seg_keys, (arriving[head], both))
+        queries.append(project_queries(head, (0, 1) if head else (1,), last))
+        at = queries[head].shape[0] - 1
+        sent = attend(at, spans["nb"][0], queries[head], *spans["nb"][1:], (arriving[head], both))
         got.append(swap_y(sent))
         last = tied(ranks, sent)
-    for head, both in enumerate(kv_heads):
-        places, seg_rows, seg_keys = spans["own"]
-        mine = tied(queries[head], last)
-        kept.append(attend(0, places, mine, seg_rows, seg_keys, (arriving[head], both)))
+    queries[0] = project_queries(0, (0,), last)
+    kept = [
+        attend(0, spans["own"][0], queries[head], *spans["own"][1:], (arriving[head], both))
+        for head, both in enumerate(kv_heads)
+    ]
     return side_by_side(where, kept, got)
 
 

time: 210 us -> 210 us (level)
  starting transfers between devices: 51.7 us -> 44.5 us
  Pallas kernels: 57.8 us -> 62.4 us
  waiting for transfers between devices: 68.8 us -> 71.1 us
    ppermute x60, starting transfers between devices: 51.7 us -> 44.5 us  [route(): return lax.ppermute(value, ('dp', 'adapter'), pairs)]
    pallas_call x2 -> x3, Pallas kernels: 17.3 us -> 21.8 us  [queries_of(): pl.pallas_call(functools.partial(query_kernel, count, inner, start, sides...]
    ppermute x60, waiting for transfers between devices: 68.8 us -> 71.1 us  [route(): return lax.ppermute(value, ('dp', 'adapter'), pairs)]
    unnamed x112 -> x130, local copies, waits for them, and re-layouts: 9.95 us -> 10.7 us
  transfers between devices with their start and end apart: 60 -> 60, of which waited for: 22 -> 22; matrix products, arithmetic and copies ran while one was open for 8% -> 8% of each run, Pallas kernels for 27% -> 29%
where the time goes in v5:
time: 210 us; the launch traced here: 209 us
  waiting for transfers between devices  71.1 us (34%)
  Pallas kernels  62.4 us (30%)
  starting transfers between devices  44.5 us (21%)
  local copies, waits for them, and re-layouts  19.2 us (9%)
  other arithmetic  10.5 us (5%)
    ppermute x60, waiting for transfers between devices, route(): return lax.ppermute(value, ('dp', 'adapter'), pairs)  71.1 us
    ppermute x60, starting transfers between devices, route(): return lax.ppermute(value, ('dp', 'adapter'), pairs)  44.5 us
    pallas_call x3, Pallas kernels, queries_of(): pl.pallas_call(functools.partial(query_kernel, count, inner, start, sides...  21.8 us
    pallas_call x4, Pallas kernels, attend(): pl.pallas_call(attend_kernel, grid=(1,), out_shape=jax.ShapeDtypeStruct((...  16.2 us
    pallas_call x2, Pallas kernels, keys_values(): pl.pallas_call(functools.partial(kv_kernel, pieces, inner, head), out_sha...  12.1 us
    unnamed x130, local copies, waits for them, and re-layouts  10.7 us
    pallas_call x1, Pallas kernels, first_ranks(): pl.pallas_call(functools.partial(first_rank_kernel, pieces), out_shape=[j...  6.75 us
    reduce_sum x2, other arithmetic, row_norm(): scale = lax.rsqrt(jnp.mean(values * values, axis=-1, keepdims=True) + 1e-06)  4.37 us
  transfers between devices with their start and end apart: 60, of which 22 were waited for; matrix products, arithmetic and copies ran while one was open for 8% of the time, Pallas kernels for 29%

profile of v5, /device:TPU:6, one launch (start us, length us, event | category | flops | bytes accessed | tf_op | source)
XLA Modules:
  0.0 208.8 jit_solution(4154006765864269208)
XLA Ops:
  4.2 4.5 %collective-permute-start.2 = (bf16[320,512]{1,0:T(8,128)(2,1)S(1)}, bf16[320,512]{1,0:T(8,128)(2,1)S(1)}, u32[]{:S(2)}, u32[]{:S(2)}) collective-permute-start(bf16[320,512]{1,0:T(8,128)(2,1)S(1)} %constant_dynamic-slice_fusion), channel_id=1, source_target_pairs={{16,1},{17,0},{18,3},{19,2},{20,5},{21,4},{22,7},{23,6},{24,9},{25... | collective-permute-start | bytes 983048 | tf_op jit(solution)/shard_map/ppermute | solution.py:184
  15.8 3.1 %collective-permute-done.3 = bf16[16,2048]{1,0:T(8,128)(2,1)S(1)} collective-permute-done((bf16[16,2048]{1,0:T(8,128)(2,1)S(1)}, bf16[16,2048]{1,0:T(8,128)(2,1)S(1)}, u32[]{:S(2)}, u32[]{:S(2)}) %collective-permute-start.3) | collective-permute-done | bytes 65568 | tf_op jit(solution)/shard_map/ppermute | solution.py:184
  18.9 2.1 collective-permute-done.5.refs_4_
  23.0 3.3 %fusion.14 = (bf16[128,2560]{1,0:T(8,128)(2,1)}, bf16[128,2560]{1,0:T(8,128)(2,1)}, bf16[128,2560]{1,0:T(8,128)(2,1)}, bf16[128,2560]{1,0:T(8,128)(2,1)}) fusion(bf16[512,2560]{1,0:T(8,128)(2,1)} %param.11), kind=kLoop, calls=%fused_computation.63 | loop fusion | bytes 5242880 | tf_op jit(solution)/shard_map/split | solution.py:628
  30.6 5.2 %collective-permute-done.12.refs_12_ = bf16[384,512]{1,0:T(8,128)(2,1)S(1)} collective-permute-done((bf16[384,512]{1,0:T(8,128)(2,1)S(1)}, bf16[384,512]{1,0:T(8,128)(2,1)S(1)}, u32[]{:S(2)}, u32[]{:S(2)}) %collective-permute-start.12) | collective-permute-done | bytes 393248 | tf_op jit(solution)/shard_map/ppermute | solution.py:184
  36.2 3.9 %collective-permute-done.13.refs_9_ = bf16[384,512]{1,0:T(8,128)(2,1)S(1)} collective-permute-done((bf16[384,512]{1,0:T(8,128)(2,1)S(1)}, bf16[384,512]{1,0:T(8,128)(2,1)S(1)}, u32[]{:S(2)}, u32[]{:S(2)}) %collective-permute-start.13) | collective-permute-done | bytes 393248 | tf_op jit(solution)/shard_map/ppermute | solution.py:184
  46.0 2.4 %fusion.3 = f32[512]{0:T(512)S(1)} fusion(bf16[512,2560]{1,0:T(8,128)(2,1)} %param.11), kind=kLoop, calls=%fused_computation.7 | loop fusion | flops 3931648 | bytes 2623488 | tf_op jit(solution)/shard_map/reduce_sum | solution.py:193
  48.4 6.0 %collective-permute-done.20.refs_16_ = bf16[384,512]{1,0:T(8,128)(2,1)S(1)} collective-permute-done((bf16[384,512]{1,0:T(8,128)(2,1)S(1)}, bf16[384,512]{1,0:T(8,128)(2,1)S(1)}, u32[]{:S(2)}, u32[]{:S(2)}) %collective-permute-start.20) | collective-permute-done | bytes 393248 | tf_op jit(solution)/shard_map/ppermute | solution.py:184
  57.1 2.3 %collective-permute-done.10.refs_5_ = bf16[48,2560]{1,0:T(8,128)(2,1)S(1)} collective-permute-done((bf16[48,2560]{1,0:T(8,128)(2,1)}, bf16[48,2560]{1,0:T(8,128)(2,1)S(1)}, u32[]{:S(2)}, u32[]{:S(2)}) %collective-permute-start.10) | collective-permute-done | bytes 245792 | tf_op jit(solution)/shard_map/ppermute | solution.py:184
  63.3 4.9 %collective-permute-done.26.refs_20_ = bf16[384,512]{1,0:T(8,128)(2,1)} collective-permute-done((bf16[384,512]{1,0:T(8,128)(2,1)S(1)}, bf16[384,512]{1,0:T(8,128)(2,1)}, u32[]{:S(2)}, u32[]{:S(2)}) %collective-permute-start.26) | collective-permute-done | bytes 393248 | tf_op jit(solution)/shard_map/ppermute | solution.py:184
  70.6 2.6 %collective-permute-done.17.refs_12_ = bf16[48,2560]{1,0:T(8,128)(2,1)} collective-permute-done((bf16[48,2560]{1,0:T(8,128)(2,1)S(1)}, bf16[48,2560]{1,0:T(8,128)(2,1)}, u32[]{:S(2)}, u32[]{:S(2)}) %collective-permute-start.17) | collective-permute-done | bytes 245792 | tf_op jit(solution)/shard_map/ppermute | solution.py:184
  76.7 6.8 %collective-permute-done.16.refs_10_.refs_12_ = bf16[192,1024]{1,0:T(8,128)(2,1)S(1)} collective-permute-done((bf16[192,1024]{1,0:T(8,128)(2,1)S(1)}, bf16[192,1024]{1,0:T(8,128)(2,1)S(1)}, u32[]{:S(2)}, u32[]{:S(2)}) %collective-permute-start.16) | collective-permute-done | bytes 393248 | tf_op jit(solution)/shard_map/ppermute | solution.py:184
  85.7 5.8 %collective-permute-done.24.refs_13_ = bf16[48,2560]{1,0:T(8,128)(2,1)} collective-permute-done((bf16[48,2560]{1,0:T(8,128)(2,1)}, bf16[48,2560]{1,0:T(8,128)(2,1)}, u32[]{:S(2)}, u32[]{:S(2)}) %collective-permute-start.24) | collective-permute-done | bytes 245792 | tf_op jit(solution)/shard_map/ppermute | solution.py:184
  96.4 2.6 %fusion.5 = (bf16[512,2560]{1,0:T(8,128)(2,1)S(1)}, bf16[512,2560]{1,0:T(8,128)(2,1)S(1)}) fusion(bf16[512,2560]{1,0:T(8,128)(2,1)S(1)} %copy-done.44, f32[512]{0:T(512)S(1)} %add_rsqrt_fusion, f32[2560]{0:T(1024)S(1)} %copy-done.60, f32[512]{0:T(512)S(1)} %add_rsqrt_fusion.1, bf16[128,2560]{1,0:T(8,128)(2,1)} %collective-permute-done.29, ...), kind=kLoop, calls=%fused_computation.9 | loop fusion | flops 19660800 | bytes 10500096 | tf_op jit(solution)/shard_map/convert_element_type | solution.py:194
  99.2 6.8 %shard_map.109 = (bf16[48,512]{1,0:T(8,128)(2,1)S(1)}, bf16[768,2560]{1,0:T(8,128)(2,1)S(1)}) custom-call(s32[6,16]{1,0:T(8,128)S(1)} %stack.75.scalars.refs_0_, s32[1,512]{1,0:T(1,128)S(1)} %bitcast.42, bf16[512,2560]{1,0:T(8,128)(2,1)S(1)} %get-tuple-element.152.normed.refs_6_.refs_5_, bf16[48,2560]{1,0:T(8,128)(2,1)} %dynamic-slice_bitcast_fusion.refs_0_, ...), custom_call_target="tpu_custom_call" | custom-call | flops 1 | bytes 1 | tf_op jit(solution)/shard_map/pallas_call | solution.py:245
  106.1 2.2 %collective-permute-done.34.refs_14_.refs_16_ = bf16[192,1024]{1,0:T(8,128)(2,1)S(1)} collective-permute-done((bf16[192,1024]{1,0:T(8,128)(2,1)}, bf16[192,1024]{1,0:T(8,128)(2,1)S(1)}, u32[]{:S(2)}, u32[]{:S(2)}) %collective-permute-start.34) | collective-permute-done | bytes 393248 | tf_op jit(solution)/shard_map/ppermute | solution.py:184
  111.6 2.8 %shard_map.110.refs_4_.refs_2_ = bf16[2,48,512]{2,1,0:T(8,128)(2,1)S(1)} custom-call(s32[6,16]{1,0:T(8,128)S(1)} %stack.75.scalars.refs_0_, s32[1,512]{1,0:T(1,128)S(1)} %get-tuple-element.159.ids.refs_2_.refs_4_.refs_5_, bf16[512,2560]{1,0:T(8,128)(2,1)S(1)} %get-tuple-element.153.normed.refs_7_.refs_5_, bf16[768,2560]{1,0:T(8,128)(2,1)S(1)} %get-tuple-element.94.down, ...), custom_call_target="tpu_custom_call" | custom-call | flops 1 | bytes 1 | tf_op jit(solution)/shard_map/pallas_call | solution.py:261
  114.8 4.3 %collective-permute-done.35.refs_5_.refs_3_ = bf16[2,48,512]{2,1,0:T(8,128)(2,1)S(1)} collective-permute-done((bf16[2,48,512]{2,1,0:T(8,128)(2,1)S(1)}, bf16[2,48,512]{2,1,0:T(8,128)(2,1)S(1)}, u32[]{:S(2)}, u32[]{:S(2)}) %collective-permute-start.35) | collective-permute-done | bytes 98336 | tf_op jit(solution)/shard_map/ppermute | solution.py:184
  119.1 2.7 %collective-permute-start.42 = (s32[1024]{0:T(1024)S(1)}, s32[1024]{0:T(1024)S(1)}, u32[]{:S(2)}, u32[]{:S(2)}) collective-permute-start(s32[1024]{0:T(1024)S(1)} %add_select_fusion), channel_id=1, source_target_pairs={{0,2},{1,3},{2,4},{3,5},{4,6},{5,7},{6,8},{7,9},{8,10},{9,11},{10,... | collective-permute-start | bytes 12296 | tf_op jit(solution)/shard_map/ppermute | solution.py:184
  121.9 6.0 %shard_map.111.refs_1_ = bf16[2,512,512]{2,1,0:T(8,128)(2,1)S(1)} custom-call(s32[6,16]{1,0:T(8,128)S(1)} %stack.75.scalars.refs_0_, s32[1,512]{1,0:T(1,128)S(1)} %bitcast.43, s32[1,512]{1,0:T(1,128)S(1)} %get-tuple-element.159.ids.refs_2_.refs_4_.refs_5_, f32[2,256]{1,0:T(2,128)S(1)} %copy-done.43, bf16[2,48,512]{2,1,0:T(8,128)(2,1)S(1)} %shard_map.110.refs_4_.refs_2_, ...), custom_call_target="tpu_custom_call" | custom-call | flops 1 | bytes 1 | tf_op jit(solution)/shard_map/pallas_call | solution.py:349
  130.0 2.1 %collective-permute-start.48 = (bf16[2,512,512]{2,1,0:T(8,128)(2,1)S(1)}, bf16[2,512,512]{2,1,0:T(8,128)(2,1)}, u32[]{:S(2)}, u32[]{:S(2)}) collective-permute-start(bf16[2,512,512]{2,1,0:T(8,128)(2,1)S(1)} %shard_map.111.refs_1_), channel_id=1, source_target_pairs={{0,2},{1,3},{2,4},{3,5},{4,6},{5,7},{6,8},{7,9},{8,10},{9,11},{10,... | collective-permute-start | bytes 3145736 | tf_op jit(solution)/shard_map/ppermute | solution.py:184
  134.2 6.0 %shard_map.112.refs_1_ = bf16[2,512,512]{2,1,0:T(8,128)(2,1)S(1)} custom-call(s32[6,16]{1,0:T(8,128)S(1)} %stack.75.scalars.refs_0_, s32[1,512]{1,0:T(1,128)S(1)} %bitcast.44, s32[1,512]{1,0:T(1,128)S(1)} %get-tuple-element.159.ids.refs_2_.refs_4_.refs_5_, f32[2,256]{1,0:T(2,128)S(1)} %copy-done.43, bf16[2,48,512]{2,1,0:T(8,128)(2,1)S(1)} %shard_map.110.refs_4_.refs_2_, ...), custom_call_target="tpu_custom_call" | custom-call | flops 1 | bytes 1 | tf_op jit(solution)/shard_map/pallas_call | solution.py:349
  140.9 9.9 %collective-permute-done.47.refs_19_.refs_21_ = bf16[192,1024]{1,0:T(8,128)(2,1)S(1)} collective-permute-done((bf16[192,1024]{1,0:T(8,128)(2,1)S(1)}, bf16[192,1024]{1,0:T(8,128)(2,1)S(1)}, u32[]{:S(2)}, u32[]{:S(2)}) %collective-permute-start.47) | collective-permute-done | bytes 393248 | tf_op jit(solution)/shard_map/ppermute | solution.py:184
  157.0 3.3 %collective-permute-done.48.refs_0_ = bf16[2,512,512]{2,1,0:T(8,128)(2,1)} collective-permute-done((bf16[2,512,512]{2,1,0:T(8,128)(2,1)S(1)}, bf16[2,512,512]{2,1,0:T(8,128)(2,1)}, u32[]{:S(2)}, u32[]{:S(2)}) %collective-permute-start.48) | collective-permute-done | bytes 1048608 | tf_op jit(solution)/shard_map/ppermute | solution.py:184
  162.3 6.6 %shard_map.113.queries = bf16[1,512,512]{2,1,0:T(8,128)(2,1)} custom-call(s32[6,16]{1,0:T(8,128)} %copy-done.25, f32[2,256]{1,0:T(2,128)} %refs_1_.5, bf16[2,48,512]{2,1,0:T(8,128)(2,1)} %copy-done.5, bf16[2,48,512]{2,1,0:T(8,128)(2,1)} %copy-done.8, s32[1,512]{1,0:T(1,128)} %copy-done.42, bf16[512,2560]{1,0:T(8,128)(2,1)} %copy-done.2, ...), custom_call_target="tpu_custom_call" | custom-call | flops 1 | bytes 1 | tf_op jit(solution)/shard_map/pallas_call | solution.py:413
  169.9 4.5 %shard_map.114 = bf16[512,512]{1,0:T(8,128)(2,1)} custom-call(s32[4]{0:T(128)S(1)} %get-tuple-element.133.places, bf16[1,512,512]{2,1,0:T(8,128)(2,1)S(1)} %copy-done.10, s32[512,1]{1,0:T(8,128)S(1)} %copy.12.seg_rows, s32[1,1536]{1,0:T(1,128)S(1)} %broadcast_in_dim.32.seg_keys, bf16[2,512,512]{2,1,0:T(8,128)(2,1)} %collective-permute-done.48.refs_0_, ...), custom_call_target="tpu_custom_call" | custom-call | flops 1 | bytes 1 | tf_op jit(solution)/shard_map/pallas_call | solution.py:491
  174.5 8.7 %shard_map.115.queries = bf16[2,512,512]{2,1,0:T(8,128)(2,1)} custom-call(s32[6,16]{1,0:T(8,128)} %copy-done.25, f32[2,256]{1,0:T(2,128)} %refs_1_.5, bf16[2,48,512]{2,1,0:T(8,128)(2,1)} %copy-done.5, bf16[2,48,512]{2,1,0:T(8,128)(2,1)} %copy-done.8, s32[1,512]{1,0:T(1,128)} %bitcast.40, s32[1,512]{1,0:T(1,128)} %copy-done.42, bf16[512,2560]{1,0:T(8,128)(2,1)} %copy-done.1, ...), custom_call_target="tpu_custom_call" | custom-call | flops 1 | bytes 1 | tf_op jit(solution)/shard_map/pallas_call | solution.py:413
  184.4 4.5 %shard_map.116 = bf16[512,512]{1,0:T(8,128)(2,1)} custom-call(s32[4]{0:T(128)S(1)} %get-tuple-element.133.places, bf16[2,512,512]{2,1,0:T(8,128)(2,1)S(1)} %copy-done.3, s32[512,1]{1,0:T(8,128)S(1)} %copy.12.seg_rows, s32[1,1536]{1,0:T(1,128)S(1)} %broadcast_in_dim.32.seg_keys, bf16[2,512,512]{2,1,0:T(8,128)(2,1)} %collective-permute-done.57.refs_0_, ...), custom_call_target="tpu_custom_call" | custom-call | flops 1 | bytes 1 | tf_op jit(solution)/shard_map/pallas_call | solution.py:491
  191.0 6.6 %shard_map.117.queries = bf16[1,512,512]{2,1,0:T(8,128)(2,1)} custom-call(s32[6,16]{1,0:T(8,128)} %copy-done.25, f32[2,256]{1,0:T(2,128)} %refs_1_.5, bf16[2,48,512]{2,1,0:T(8,128)(2,1)} %copy-done.5, bf16[2,48,512]{2,1,0:T(8,128)(2,1)} %copy-done.8, s32[1,512]{1,0:T(1,128)} %bitcast.41, bf16[512,2560]{1,0:T(8,128)(2,1)} %copy-done.1, ...), custom_call_target="tpu_custom_call" | custom-call | flops 1 | bytes 1 | tf_op jit(solution)/shard_map/pallas_call | solution.py:413
  198.8 3.6 %shard_map.118.refs_0_ = bf16[512,512]{1,0:T(8,128)(2,1)S(1)} custom-call(s32[4]{0:T(128)S(1)} %broadcast_subtract_fusion.1.places, bf16[1,512,512]{2,1,0:T(8,128)(2,1)S(1)} %copy-done.9, s32[512,1]{1,0:T(8,128)S(1)} %copy.14.seg_rows, s32[1,1536]{1,0:T(1,128)S(1)} %broadcast_in_dim.34.seg_keys, bf16[2,512,512]{2,1,0:T(8,128)(2,1)} %collective-permute-done.48.refs_0_, ...), custom_call_target="tpu_custom_call" | custom-call | flops 1 | bytes 1 | tf_op jit(solution)/shard_map/pallas_call | solution.py:491
  202.4 3.6 %shard_map.119.refs_1_ = bf16[512,512]{1,0:T(8,128)(2,1)S(1)} custom-call(s32[4]{0:T(128)S(1)} %broadcast_subtract_fusion.1.places, bf16[2,512,512]{2,1,0:T(8,128)(2,1)S(1)} %copy-done.4, s32[512,1]{1,0:T(8,128)S(1)} %copy.14.seg_rows, s32[1,1536]{1,0:T(1,128)S(1)} %broadcast_in_dim.34.seg_keys, bf16[2,512,512]{2,1,0:T(8,128)(2,1)} %collective-permute-done.57.refs_0_, ...), custom_call_target="tpu_custom_call" | custom-call | flops 1 | bytes 1 | tf_op jit(solution)/shard_map/pallas_call | solution.py:491
  206.1 2.7 %shard_map.120 = bf16[512,2048]{1,0:T(8,128)(2,1)} custom-call(s32[4]{0:T(128)S(1)} %pad_add_fusion.1.where, bf16[512,512]{1,0:T(8,128)(2,1)S(1)} %shard_map.118.refs_0_, bf16[512,512]{1,0:T(8,128)(2,1)S(1)} %shard_map.119.refs_1_, bf16[512,512]{1,0:T(8,128)(2,1)} %collective-permute-done.58.refs_2_, bf16[512,512]{1,0:T(8,128)(2,1)} %collective-permute-done.59.refs_3_), custom_call_target="tpu_custom_call" | custom-call | flops 1 | bytes 1 | tf_op jit(solution)/shard_map/pallas_call | solution.py:524
  (266 shorter events, 65.3 us)
Async XLA Ops:
  1.2 19.8 %collective-permute-start = (bf16[160,1024]{1,0:T(8,128)(2,1)S(1)}, bf16[160,1024]{1,0:T(8,128)(2,1)S(1)}, u32[]{:S(2)}, u32[]{:S(2)}) collective-permute-start(bf16[160,1024]{1,0:T(8,128)(2,1)S(1)} %get-tuple-element.143), channel_id=1, source_target_pairs={{1,8},{3,10},{5,12},{7,14},{8,1},{10,3},{12,5},{14,7}} | collective-permute-start | bytes 983048 | tf_op jit(solution)/shard_map/ppermute | solution.py:184
  1.9 19.1 %collective-permute-start.1 = (bf16[160,1024]{1,0:T(8,128)(2,1)S(1)}, bf16[160,1024]{1,0:T(8,128)(2,1)S(1)}, u32[]{:S(2)}, u32[]{:S(2)}) collective-permute-start(bf16[160,1024]{1,0:T(8,128)(2,1)S(1)} %get-tuple-element.142), channel_id=1, source_target_pairs={{0,16},{1,24},{2,18},{3,26},{4,20},{5,28},{6,22},{7,30},{8,17},{9,... | collective-permute-start | bytes 983048 | tf_op jit(solution)/shard_map/ppermute | solution.py:184
  4.2 16.8 %collective-permute-start.2 = (bf16[320,512]{1,0:T(8,128)(2,1)S(1)}, bf16[320,512]{1,0:T(8,128)(2,1)S(1)}, u32[]{:S(2)}, u32[]{:S(2)}) collective-permute-start(bf16[320,512]{1,0:T(8,128)(2,1)S(1)} %constant_dynamic-slice_fusion), channel_id=1, source_target_pairs={{16,1},{17,0},{18,3},{19,2},{20,5},{21,4},{22,7},{23,6},{24,9},{25... | collective-permute-start | bytes 983048 | tf_op jit(solution)/shard_map/ppermute | solution.py:184
  23.0 12.9 %collective-permute-start.12 = (bf16[384,512]{1,0:T(8,128)(2,1)S(1)}, bf16[384,512]{1,0:T(8,128)(2,1)S(1)}, u32[]{:S(2)}, u32[]{:S(2)}) collective-permute-start(bf16[384,512]{1,0:T(8,128)(2,1)S(1)} %fusion.6.refs_8_), channel_id=1, source_target_pairs={{0,2},{1,3},{2,4},{3,5},{4,6},{5,7},{6,0},{7,1},{8,10},{9,11},{10,... | collective-permute-start | bytes 1179656 | tf_op jit(solution)/shard_map/ppermute | solution.py:184
  26.3 19.4 %collective-permute-start.9 = (bf16[128,2560]{1,0:T(8,128)(2,1)}, bf16[128,2560]{1,0:T(8,128)(2,1)}, u32[]{:S(2)}, u32[]{:S(2)}) collective-permute-start(bf16[128,2560]{1,0:T(8,128)(2,1)} %get-tuple-element.141), channel_id=1, source_target_pairs={{0,1},{1,0},{2,3},{3,2},{4,5},{5,4},{6,7},{7,6},{8,9},{9,8},{10,11... | collective-permute-start | bytes 1966088 | tf_op jit(solution)/shard_map/ppermute | solution.py:184
  28.1 12.0 %collective-permute-start.13 = (bf16[384,512]{1,0:T(8,128)(2,1)S(1)}, bf16[384,512]{1,0:T(8,128)(2,1)S(1)}, u32[]{:S(2)}, u32[]{:S(2)}) collective-permute-start(bf16[384,512]{1,0:T(8,128)(2,1)S(1)} %fusion.6.refs_8_), channel_id=1, source_target_pairs={{0,16},{1,17},{2,18},{3,19},{4,20},{5,21},{6,22},{7,23},{8,24},{9,... | collective-permute-start | bytes 1179656 | tf_op jit(solution)/shard_map/ppermute | solution.py:184
  29.1 13.0 %collective-permute-start.6 = (bf16[48,2560]{1,0:T(8,128)(2,1)S(1)}, bf16[48,2560]{1,0:T(8,128)(2,1)S(1)}, u32[]{:S(2)}, u32[]{:S(2)}) collective-permute-start(bf16[48,2560]{1,0:T(8,128)(2,1)S(1)} %collective-permute-done.5.refs_4_), channel_id=1, source_target_pairs={{0,2},{1,3},{2,4},{3,5},{4,6},{5,7},{6,0},{7,1},{8,10},{9,11},{10,... | collective-permute-start | bytes 737288 | tf_op jit(solution)/shard_map/ppermute | solution.py:184
  40.9 13.5 %collective-permute-start.20 = (bf16[384,512]{1,0:T(8,128)(2,1)S(1)}, bf16[384,512]{1,0:T(8,128)(2,1)S(1)}, u32[]{:S(2)}, u32[]{:S(2)}) collective-permute-start(bf16[384,512]{1,0:T(8,128)(2,1)S(1)} %collective-permute-done.12.refs_12_), channel_id=1, source_target_pairs={{0,2},{1,3},{2,4},{3,5},{4,6},{5,7},{6,0},{7,1},{8,10},{9,11},{10,... | collective-permute-start | bytes 1179656 | tf_op jit(solution)/shard_map/ppermute | solution.py:184
  42.1 12.3 %collective-permute-start.21 = (bf16[384,512]{1,0:T(8,128)(2,1)S(1)}, bf16[384,512]{1,0:T(8,128)(2,1)S(1)}, u32[]{:S(2)}, u32[]{:S(2)}) collective-permute-start(bf16[384,512]{1,0:T(8,128)(2,1)S(1)} %collective-permute-done.12.refs_12_), channel_id=1, source_target_pairs={{0,16},{1,17},{2,18},{3,19},{4,20},{5,21},{6,22},{7,23},{8,24},{9,... | collective-permute-start | bytes 1179656 | tf_op jit(solution)/shard_map/ppermute | solution.py:184
  44.7 17.5 %collective-permute-start.15 = (bf16[128,2560]{1,0:T(8,128)(2,1)}, bf16[128,2560]{1,0:T(8,128)(2,1)}, u32[]{:S(2)}, u32[]{:S(2)}) collective-permute-start(bf16[128,2560]{1,0:T(8,128)(2,1)} %get-tuple-element.79), channel_id=1, source_target_pairs={{0,1},{1,0},{2,3},{3,2},{4,5},{5,4},{6,7},{7,6},{8,9},{9,8},{10,11... | collective-permute-start | bytes 1966088 | tf_op jit(solution)/shard_map/ppermute | solution.py:184
  45.8 13.6 %collective-permute-start.10 = (bf16[48,2560]{1,0:T(8,128)(2,1)}, bf16[48,2560]{1,0:T(8,128)(2,1)S(1)}, u32[]{:S(2)}, u32[]{:S(2)}) collective-permute-start(bf16[48,2560]{1,0:T(8,128)(2,1)} %copy-done.26), channel_id=1, source_target_pairs={{0,16},{1,17},{2,18},{3,19},{4,20},{5,21},{6,22},{7,23},{8,24},{9,... | collective-permute-start | bytes 737288 | tf_op jit(solution)/shard_map/ppermute | solution.py:184
  54.4 13.9 %collective-permute-start.26 = (bf16[384,512]{1,0:T(8,128)(2,1)S(1)}, bf16[384,512]{1,0:T(8,128)(2,1)}, u32[]{:S(2)}, u32[]{:S(2)}) collective-permute-start(bf16[384,512]{1,0:T(8,128)(2,1)S(1)} %collective-permute-done.20.refs_16_), channel_id=1, source_target_pairs={{0,2},{1,3},{2,4},{3,5},{4,6},{5,7},{6,0},{7,1},{8,10},{9,11},{10,... | collective-permute-start | bytes 1179656 | tf_op jit(solution)/shard_map/ppermute | solution.py:184
  55.8 13.7 %collective-permute-start.27 = (bf16[384,512]{1,0:T(8,128)(2,1)S(1)}, bf16[384,512]{1,0:T(8,128)(2,1)}, u32[]{:S(2)}, u32[]{:S(2)}) collective-permute-start(bf16[384,512]{1,0:T(8,128)(2,1)S(1)} %collective-permute-done.20.refs_16_), channel_id=1, source_target_pairs={{0,16},{1,17},{2,18},{3,19},{4,20},{5,21},{6,22},{7,23},{8,24},{9,... | collective-permute-start | bytes 1179656 | tf_op jit(solution)/shard_map/ppermute | solution.py:184
  60.7 22.8 %collective-permute-start.23 = (bf16[128,2560]{1,0:T(8,128)(2,1)S(1)}, bf16[128,2560]{1,0:T(8,128)(2,1)S(1)}, u32[]{:S(2)}, u32[]{:S(2)}) collective-permute-start(bf16[128,2560]{1,0:T(8,128)(2,1)S(1)} %copy-done.57), channel_id=1, source_target_pairs={{0,1},{1,0},{2,3},{3,2},{4,5},{5,4},{6,7},{7,6},{8,9},{9,8},{10,11... | collective-permute-start | bytes 1966088 | tf_op jit(solution)/shard_map/ppermute | solution.py:184
  70.2 13.3 %collective-permute-start.16 = (bf16[192,1024]{1,0:T(8,128)(2,1)S(1)}, bf16[192,1024]{1,0:T(8,128)(2,1)S(1)}, u32[]{:S(2)}, u32[]{:S(2)}) collective-permute-start(bf16[192,1024]{1,0:T(8,128)(2,1)S(1)} %pad_maximum_fusion.2.refs_6_.refs_8_), channel_id=1, source_target_pairs={{0,2},{1,3},{2,4},{3,5},{4,6},{5,7},{6,0},{7,1},{8,10},{9,11},{10,... | collective-permute-start | bytes 1179656 | tf_op jit(solution)/shard_map/ppermute | solution.py:184
  73.2 18.8 %collective-permute-start.29 = (bf16[128,2560]{1,0:T(8,128)(2,1)}, bf16[128,2560]{1,0:T(8,128)(2,1)}, u32[]{:S(2)}, u32[]{:S(2)}) collective-permute-start(bf16[128,2560]{1,0:T(8,128)(2,1)} %get-tuple-element.88), channel_id=1, source_target_pairs={{0,1},{1,0},{2,3},{3,2},{4,5},{5,4},{6,7},{7,6},{8,9},{9,8},{10,11... | collective-permute-start | bytes 1966088 | tf_op jit(solution)/shard_map/ppermute | solution.py:184
  85.2 24.2 %collective-permute-start.36 = (bf16[384,512]{1,0:T(8,128)(2,1)S(1)}, bf16[384,512]{1,0:T(8,128)(2,1)S(1)}, u32[]{:S(2)}, u32[]{:S(2)}) collective-permute-start(bf16[384,512]{1,0:T(8,128)(2,1)S(1)} %collective-permute-done.13.refs_9_), channel_id=1, source_target_pairs={{0,8},{1,9},{2,10},{3,11},{4,12},{5,13},{6,14},{7,15},{8,0},{9,1},... | collective-permute-start | bytes 1179656 | tf_op jit(solution)/shard_map/ppermute | solution.py:184
  94.2 16.1 %collective-permute-start.37 = (bf16[384,512]{1,0:T(8,128)(2,1)S(1)}, bf16[384,512]{1,0:T(8,128)(2,1)S(1)}, u32[]{:S(2)}, u32[]{:S(2)}) collective-permute-start(bf16[384,512]{1,0:T(8,128)(2,1)S(1)} %collective-permute-done.21.refs_13_), channel_id=1, source_target_pairs={{0,8},{1,9},{2,10},{3,11},{4,12},{5,13},{6,14},{7,15},{8,0},{9,1},... | collective-permute-start | bytes 1179656 | tf_op jit(solution)/shard_map/ppermute | solution.py:184
  94.7 15.6 %collective-permute-start.38 = (bf16[384,512]{1,0:T(8,128)(2,1)}, bf16[384,512]{1,0:T(8,128)(2,1)S(1)}, u32[]{:S(2)}, u32[]{:S(2)}) collective-permute-start(bf16[384,512]{1,0:T(8,128)(2,1)} %collective-permute-done.27.refs_17_), channel_id=1, source_target_pairs={{0,8},{1,9},{2,10},{3,11},{4,12},{5,13},{6,14},{7,15},{8,0},{9,1},... | collective-permute-start | bytes 1179656 | tf_op jit(solution)/shard_map/ppermute | solution.py:184
  94.8 13.5 %collective-permute-start.34 = (bf16[192,1024]{1,0:T(8,128)(2,1)}, bf16[192,1024]{1,0:T(8,128)(2,1)S(1)}, u32[]{:S(2)}, u32[]{:S(2)}) collective-permute-start(bf16[192,1024]{1,0:T(8,128)(2,1)} %copy-done.47), channel_id=1, source_target_pairs={{0,2},{1,3},{2,4},{3,5},{4,6},{5,7},{6,0},{7,1},{8,10},{9,11},{10,... | collective-permute-start | bytes 1179656 | tf_op jit(solution)/shard_map/ppermute | solution.py:184
  96.3 18.1 %collective-permute-start.41 = (bf16[384,512]{1,0:T(8,128)(2,1)}, bf16[384,512]{1,0:T(8,128)(2,1)S(1)}, u32[]{:S(2)}, u32[]{:S(2)}) collective-permute-start(bf16[384,512]{1,0:T(8,128)(2,1)} %collective-permute-done.39.refs_21_), channel_id=1, source_target_pairs={{0,8},{1,9},{2,10},{3,11},{4,12},{5,13},{6,14},{7,15},{8,0},{9,1},... | collective-permute-start | bytes 1179656 | tf_op jit(solution)/shard_map/ppermute | solution.py:184
  108.2 19.7 %collective-permute-start.45 = (bf16[192,1024]{1,0:T(8,128)(2,1)S(1)}, bf16[192,1024]{1,0:T(8,128)(2,1)}, u32[]{:S(2)}, u32[]{:S(2)}) collective-permute-start(bf16[192,1024]{1,0:T(8,128)(2,1)S(1)} %copy-done.48), channel_id=1, source_target_pairs={{0,16},{1,17},{2,18},{3,19},{4,20},{5,21},{6,22},{7,23},{8,24},{9,... | collective-permute-start | bytes 1179656 | tf_op jit(solution)/shard_map/ppermute | solution.py:184
  109.4 19.4 %collective-permute-start.44 = (bf16[192,1024]{1,0:T(8,128)(2,1)S(1)}, bf16[192,1024]{1,0:T(8,128)(2,1)}, u32[]{:S(2)}, u32[]{:S(2)}) collective-permute-start(bf16[192,1024]{1,0:T(8,128)(2,1)S(1)} %copy-done.46), channel_id=1, source_target_pairs={{0,16},{1,17},{2,18},{3,19},{4,20},{5,21},{6,22},{7,23},{8,24},{9,... | collective-permute-start | bytes 1179656 | tf_op jit(solution)/shard_map/ppermute | solution.py:184
  110.3 18.6 %collective-permute-start.43 = (bf16[192,1024]{1,0:T(8,128)(2,1)S(1)}, bf16[192,1024]{1,0:T(8,128)(2,1)S(1)}, u32[]{:S(2)}, u32[]{:S(2)}) collective-permute-start(bf16[192,1024]{1,0:T(8,128)(2,1)S(1)} %collective-permute-done.34.refs_14_.refs_16_), channel_id=1, source_target_pairs={{0,2},{1,3},{2,4},{3,5},{4,6},{5,7},{6,0},{7,1},{8,10},{9,11},{10,... | collective-permute-start | bytes 1179656 | tf_op jit(solution)/shard_map/ppermute | solution.py:184
  110.3 29.9 %collective-permute-start.46 = (bf16[192,1024]{1,0:T(8,128)(2,1)S(1)}, bf16[192,1024]{1,0:T(8,128)(2,1)}, u32[]{:S(2)}, u32[]{:S(2)}) collective-permute-start(bf16[192,1024]{1,0:T(8,128)(2,1)S(1)} %collective-permute-done.34.refs_14_.refs_16_), channel_id=1, source_target_pairs={{0,16},{1,17},{2,18},{3,19},{4,20},{5,21},{6,22},{7,23},{8,24},{9,... | collective-permute-start | bytes 1179656 | tf_op jit(solution)/shard_map/ppermute | solution.py:184
  128.8 22.0 %collective-permute-start.47 = (bf16[192,1024]{1,0:T(8,128)(2,1)S(1)}, bf16[192,1024]{1,0:T(8,128)(2,1)S(1)}, u32[]{:S(2)}, u32[]{:S(2)}) collective-permute-start(bf16[192,1024]{1,0:T(8,128)(2,1)S(1)} %collective-permute-done.43.refs_18_.refs_20_), channel_id=1, source_target_pairs={{0,16},{1,17},{2,18},{3,19},{4,20},{5,21},{6,22},{7,23},{8,24},{9,... | collective-permute-start | bytes 1179656 | tf_op jit(solution)/shard_map/ppermute | solution.py:184
  130.0 30.2 %collective-permute-start.48 = (bf16[2,512,512]{2,1,0:T(8,128)(2,1)S(1)}, bf16[2,512,512]{2,1,0:T(8,128)(2,1)}, u32[]{:S(2)}, u32[]{:S(2)}) collective-permute-start(bf16[2,512,512]{2,1,0:T(8,128)(2,1)S(1)} %shard_map.111.refs_1_), channel_id=1, source_target_pairs={{0,2},{1,3},{2,4},{3,5},{4,6},{5,7},{6,8},{7,9},{8,10},{9,11},{10,... | collective-permute-start | bytes 3145736 | tf_op jit(solution)/shard_map/ppermute | solution.py:184
  140.3 12.5 %collective-permute-start.50 = (bf16[192,1024]{1,0:T(8,128)(2,1)S(1)}, bf16[192,1024]{1,0:T(8,128)(2,1)S(1)}, u32[]{:S(2)}, u32[]{:S(2)}) collective-permute-start(bf16[192,1024]{1,0:T(8,128)(2,1)S(1)} %copy-done.48), channel_id=1, source_target_pairs={{0,8},{1,9},{2,10},{3,11},{4,12},{5,13},{6,14},{7,15},{8,0},{9,1},... | collective-permute-start | bytes 1179656 | tf_op jit(solution)/shard_map/ppermute | solution.py:184
  140.8 12.5 %collective-permute-start.51 = (bf16[192,1024]{1,0:T(8,128)(2,1)S(1)}, bf16[192,1024]{1,0:T(8,128)(2,1)S(1)}, u32[]{:S(2)}, u32[]{:S(2)}) collective-permute-start(bf16[192,1024]{1,0:T(8,128)(2,1)S(1)} %collective-permute-done.34.refs_14_.refs_16_), channel_id=1, source_target_pairs={{0,8},{1,9},{2,10},{3,11},{4,12},{5,13},{6,14},{7,15},{8,0},{9,1},... | collective-permute-start | bytes 1179656 | tf_op jit(solution)/shard_map/ppermute | solution.py:184
  150.8 32.3 %collective-permute-start.57 = (bf16[2,512,512]{2,1,0:T(8,128)(2,1)S(1)}, bf16[2,512,512]{2,1,0:T(8,128)(2,1)}, u32[]{:S(2)}, u32[]{:S(2)}) collective-permute-start(bf16[2,512,512]{2,1,0:T(8,128)(2,1)S(1)} %shard_map.112.refs_1_), channel_id=1, source_target_pairs={{0,2},{1,3},{2,4},{3,5},{4,6},{5,7},{6,8},{7,9},{8,10},{9,11},{10,... | collective-permute-start | bytes 3145736 | tf_op jit(solution)/shard_map/ppermute | solution.py:184
  174.4 31.7 %collective-permute-start.58 = (bf16[512,512]{1,0:T(8,128)(2,1)}, bf16[512,512]{1,0:T(8,128)(2,1)}, u32[]{:S(2)}, u32[]{:S(2)}) collective-permute-start(bf16[512,512]{1,0:T(8,128)(2,1)} %shard_map.114), channel_id=1, source_target_pairs={{0,1},{1,0},{2,3},{3,2},{4,5},{5,4},{6,7},{7,6},{8,9},{9,8},{10,11... | collective-permute-start | bytes 1572872 | tf_op jit(solution)/shard_map/ppermute | solution.py:184
  188.9 17.1 %collective-permute-start.59 = (bf16[512,512]{1,0:T(8,128)(2,1)}, bf16[512,512]{1,0:T(8,128)(2,1)}, u32[]{:S(2)}, u32[]{:S(2)}) collective-permute-start(bf16[512,512]{1,0:T(8,128)(2,1)} %shard_map.116), channel_id=1, source_target_pairs={{0,1},{1,0},{2,3},{3,2},{4,5},{5,4},{6,7},{7,6},{8,9},{9,8},{10,11... | collective-permute-start | bytes 1572872 | tf_op jit(solution)/shard_map/ppermute | solution.py:184
  (93 other events, 1355.9 us)
